TPU v7x, 128 devices: a whole 4x4x4 slice. The times are simulated.
128 devices in a mesh: pipe: 8 (over y_lo, z), expert: 16 (over y_hi, x, core).
Axes of the slice: x: 4, y: 4 (y_hi: 2, y_lo: 2; y = y_hi * 2 + y_lo), z: 4, core: 2. Of those that a mesh axis runs over, the one named last changes fastest.
Arguments:
- saved_input: bfloat16 [8, 3072, 7168], P('pipe', 'expert'), may hold values from -6 to 6
- grad_output: bfloat16 [8, 3072, 7168], P('pipe', 'expert'), may hold values from -6 to 6
- routes: int32 [8, 3072, 8], P('pipe', 'expert'), may hold values from 0 to 255, as said below
- route_weight: float32 [8, 3072, 8], P('pipe', 'expert'), may hold values from 0.2 to 1
- gate_weight: bfloat16 [8, 7168, 4096], P('pipe', None, 'expert'), may hold values from -0.0625 to 0.0625
- up_weight: bfloat16 [8, 7168, 4096], P('pipe', None, 'expert'), may hold values from -0.0625 to 0.0625
- down_weight: bfloat16 [8, 4096, 7168], P('pipe', 'expert'), may hold values from -0.125 to 0.125
- mirror_grad: bfloat16 [8, 4096, 7168], P('pipe', 'expert'), may hold values from -6 to 6
Outputs:
- next_cotangent: bfloat16 [8, 3072, 7168], P('pipe', 'expert')
- down_grad: bfloat16 [8, 4096, 7168], P('pipe', 'expert')
Inputs may be any that keep to these rules, and one draw needn't show every extreme that they name: `routes`: each token names 8 different experts; the window holds experts 0 to 1. Of the 192 tokens of one device (one section, aligned blocks of 192 tokens), at most 24 name any one window expert; in each section some window expert is named by exactly 24 tokens of every block.
All inputs are finite; a program needn't handle non-finite values.
Results may differ from a plain program's by a relative error of at most 0.0057.
Values may be sent and summed in bfloat16 or wider, within the bound.
No kernel may reach another device: no remote copies, remote signals or barrier semaphores. Data moves between devices by JAX's collectives and lax.ppermute only.
A program may use at most 128 MiB of HBM per device.

v0:
```python
import jax
import jax.numpy as jnp
from jax import lax
from jax.sharding import PartitionSpec as P

D = 7168
FF = 2048
HID_DEV = 256
CAP = 24


def from_behind(x, axis, by):
    length = lax.axis_size(axis)
    return lax.ppermute(x, axis, [(i, (i + by) % length) for i in range(length)])


def from_partner(x, axis, apart):
    return lax.ppermute(x, axis, [(i, i ^ 1 << apart) for i in range(lax.axis_size(axis))])


def local(
    saved_input, grad_output, routes, route_weight, gate_weight, up_weight, down_weight, mirror_grad
):
    devices = lax.axis_size("expert")
    split_count = FF // HID_DEV
    windows = devices // split_count
    inputs = saved_input[0]
    cotangent = grad_output[0]
    chosen = routes[0]
    weights = route_weight[0]
    gate_local = gate_weight[0]
    up_local = up_weight[0]
    down_local = down_weight[0]
    matches = chosen[:, None, :] == jnp.arange(windows, dtype=jnp.int32)[None, :, None]
    member = jnp.any(matches, axis=-1)
    scale = jnp.sum(jnp.where(matches, weights[:, None, :], jnp.float32(0.0)), axis=-1)
    slot_index = jnp.cumsum(member.astype(jnp.int32), axis=0) - 1
    slot_range = jnp.arange(CAP, dtype=jnp.int32)
    placement_map = (
        (slot_index[:, :, None] == slot_range[None, None, :]) & member[:, :, None]
    ).astype(jnp.bfloat16)
    cotangent_f = cotangent.astype(jnp.float32)
    scaled = (scale[:, :, None] * cotangent_f[:, None, :]).astype(jnp.bfloat16)
    input_rows = jnp.einsum(
        "twc,td->wcd", placement_map, inputs, preferred_element_type=jnp.float32
    ).astype(jnp.bfloat16)
    scaled_rows = jnp.einsum(
        "twc,twd->wcd", placement_map, scaled, preferred_element_type=jnp.float32
    ).astype(jnp.bfloat16)
    send_inputs = jnp.broadcast_to(input_rows[:, None], (windows, split_count, CAP, D)).reshape(
        devices, CAP, D
    )
    send_scaled = jnp.broadcast_to(scaled_rows[:, None], (windows, split_count, CAP, D)).reshape(
        devices, CAP, D
    )
    arrivals = lax.all_to_all(send_inputs, "expert", split_axis=0, concat_axis=0, tiled=True)
    scaled_in = lax.all_to_all(send_scaled, "expert", split_axis=0, concat_axis=0, tiled=True)
    pre_gate = jnp.einsum("scd,dh->sch", arrivals, gate_local, preferred_element_type=jnp.float32)
    pre_up = jnp.einsum("scd,dh->sch", arrivals, up_local, preferred_element_type=jnp.float32)
    from_down = jnp.einsum("scd,hd->sch", scaled_in, down_local, preferred_element_type=jnp.float32)
    sigma = jax.nn.sigmoid(pre_gate)
    activated = pre_gate * sigma
    hidden = (activated * pre_up).astype(jnp.bfloat16)
    slope = sigma * (1.0 + pre_gate * (1.0 - sigma))
    grad_gate = (from_down * pre_up * slope).astype(jnp.bfloat16)
    grad_up = (from_down * activated).astype(jnp.bfloat16)
    partial_value = jnp.einsum(
        "sch,dh->scd", grad_gate, gate_local, preferred_element_type=jnp.float32
    )
    partial_value = partial_value + jnp.einsum(
        "sch,dh->scd", grad_up, up_local, preferred_element_type=jnp.float32
    )
    partial_value, hidden, arrived = (partial_value.astype(jnp.bfloat16), hidden, scaled_in)
    local_grad = jnp.einsum("sch,scd->hd", hidden, arrived, preferred_element_type=jnp.float32)
    returned = lax.all_to_all(partial_value, "expert", split_axis=0, concat_axis=0, tiled=True)
    returned = returned.reshape(windows, split_count, CAP, D)
    combined = jnp.einsum(
        "twc,wscd->td", placement_map, returned, preferred_element_type=jnp.float32
    )
    back = (cotangent_f + combined).astype(jnp.bfloat16)
    next_cotangent = from_behind(back[None], "pipe", -1)
    mirrored = mirror_grad
    for bit_number in range(lax.axis_size("pipe").bit_length() - 1):
        mirrored = from_partner(mirrored, "pipe", bit_number)
    down_grad = (local_grad + mirrored[0].astype(jnp.float32)).astype(jnp.bfloat16)[None]
    return (next_cotangent, down_grad)


def solution(mesh):
    in_specs = (
        P("pipe", "expert", None),
        P("pipe", "expert", None),
        P("pipe", "expert", None),
        P("pipe", "expert", None),
        P("pipe", None, "expert"),
        P("pipe", None, "expert"),
        P("pipe", "expert", None),
        P("pipe", "expert", None),
    )
    out_specs = (P("pipe", "expert", None), P("pipe", "expert", None))
    return jax.shard_map(local, mesh=mesh, in_specs=in_specs, out_specs=out_specs, check_vma=False)
```

profile of v0, /device:TPU:6, one launch (start us, length us, event | category | flops | bytes accessed | tf_op | source)
XLA Modules:
  0.0 414.7 jit_solution(8307101913127644534)
XLA Ops:
  3.3 3.0 broadcast_in_dim.42
  6.3 7.7 %all-to-all-start.1 = ((bf16[16,24,7168]{2,1,0:T(8,128)(2,1)}), bf16[16,24,7168]{2,1,0:T(8,128)(2,1)}, u32[]{:S(2)}, u32[]{:S(2)}) async-start(bf16[16,24,7168]{2,1,0:T(8,128)(2,1)} %bitcast.65), calls=%async_computation.1 | async-start | bytes 11010048 | tf_op jit(solution)/shard_map/all_to_all | solution.py:56
  14.7 0.9 convolution_convert_fusion.1
  15.5 69.8 %all-to-all-done.1 = bf16[16,24,7168]{2,1,0:T(8,128)(2,1)} async-done(((bf16[16,24,7168]{2,1,0:T(8,128)(2,1)}), bf16[16,24,7168]{2,1,0:T(8,128)(2,1)}, u32[]{:S(2)}, u32[]{:S(2)}) %all-to-all-start.1) | async-done | bytes 5505056 | tf_op jit(solution)/shard_map/all_to_all | solution.py:56
  85.4 3.0 broadcast_in_dim.41
  88.4 8.9 %all-to-all-start = ((bf16[16,24,7168]{2,1,0:T(8,128)(2,1)}), bf16[16,24,7168]{2,1,0:T(8,128)(2,1)}, u32[]{:S(2)}, u32[]{:S(2)}) async-start(bf16[16,24,7168]{2,1,0:T(8,128)(2,1)} %bitcast.64), calls=%async_computation | async-start | bytes 11010048 | tf_op jit(solution)/shard_map/all_to_all | solution.py:57
  97.3 2.0 collective-permute-start.1
  99.3 5.3 %fusion.9 = f32[16,24,256]{2,1,0:T(8,128)S(1)} fusion(bf16[16,24,7168]{2,1,0:T(8,128)(2,1)} %all-to-all-done.1, bf16[1,7168,256]{2,1,0:T(8,128)(2,1)} %param.12), kind=kOutput, calls=%fused_computation.17 | convolution fusion | flops 1409286144 | bytes 9568256 | tf_op jit(solution)/shard_map/scd,dh->sch/dot_general | solution.py:58
  104.5 4.3 %fusion.12 = f32[16,24,256]{2,1,0:T(8,128)S(1)} fusion(bf16[16,24,7168]{2,1,0:T(8,128)(2,1)} %all-to-all-done.1, bf16[1,7168,256]{2,1,0:T(8,128)(2,1)S(1)} %copy-done.4), kind=kOutput, calls=%fused_computation.20 | convolution fusion | flops 1409286144 | bytes 9568256 | tf_op jit(solution)/shard_map/scd,dh->sch/dot_general | solution.py:59
  108.9 59.8 %all-to-all-done = bf16[16,24,7168]{2,1,0:T(8,128)(2,1)} async-done(((bf16[16,24,7168]{2,1,0:T(8,128)(2,1)}), bf16[16,24,7168]{2,1,0:T(8,128)(2,1)}, u32[]{:S(2)}, u32[]{:S(2)}) %all-to-all-start) | async-done | bytes 5505056 | tf_op jit(solution)/shard_map/all_to_all | solution.py:57
  168.6 5.5 %fusion.14 = f32[16,24,256]{2,1,0:T(8,128)S(1)} fusion(bf16[16,24,7168]{2,1,0:T(8,128)(2,1)} %all-to-all-done, bf16[1,256,7168]{2,1,0:T(8,128)(2,1)} %param.14), kind=kOutput, calls=%fused_computation.22 | convolution fusion | flops 1409286144 | bytes 9568256 | tf_op jit(solution)/shard_map/scd,hd->sch/dot_general | solution.py:60
  174.1 1.8 fusion.7
  175.9 6.1 %add_convert_fusion = bf16[16,24,7168]{2,1,0:T(8,128)(2,1)} fusion(f32[16,24,7168]{2,1,0:T(8,128)S(1)} %fusion.7, bf16[1,7168,256]{2,1,0:T(8,128)(2,1)} %param.13, f32[16,24,256]{2,1,0:T(8,128)S(1)} %fusion.14, f32[16,24,256]{2,1,0:T(8,128)S(1)} %fusion.9), kind=kOutput, calls=%fused_computation.1 | convolution fusion | flops 1415380992 | bytes 20971520 | tf_op jit(solution)/shard_map/sch,dh->scd/dot_general | solution.py:70
  182.0 8.8 %all-to-all-start.2 = ((bf16[16,24,7168]{2,1,0:T(8,128)(2,1)}), bf16[16,24,7168]{2,1,0:T(8,128)(2,1)}, u32[]{:S(2)}, u32[]{:S(2)}) async-start(bf16[16,24,7168]{2,1,0:T(8,128)(2,1)} %add_convert_fusion), calls=%async_computation.2 | async-start | bytes 11010048 | tf_op jit(solution)/shard_map/all_to_all | solution.py:75
  190.8 4.1 collective-permute-start.2
  195.0 80.0 %collective-permute-done.2 = bf16[1,256,7168]{2,1,0:T(8,128)(2,1)} collective-permute-done((bf16[1,256,7168]{2,1,0:T(8,128)(2,1)}, bf16[1,256,7168]{2,1,0:T(8,128)(2,1)}, u32[]{:S(2)}, u32[]{:S(2)}) %collective-permute-start.2) | collective-permute-done | bytes 3670048 | tf_op jit(solution)/shard_map/ppermute | solution.py:18
  275.6 3.3 convert_reduce_fusion
  278.9 0.9 fusion.2
  279.8 4.3 %collective-permute-start = (bf16[1,192,7168]{2,1,0:T(8,128)(2,1)S(1)}, bf16[1,192,7168]{2,1,0:T(8,128)(2,1)S(1)}, u32[]{:S(2)}, u32[]{:S(2)}) collective-permute-start(bf16[1,192,7168]{2,1,0:T(8,128)(2,1)S(1)} %fusion.2), channel_id=1, source_target_pairs={{0,112},{16,0},{32,16},{48,32},{64,48},{80,64},{96,80},{112,96},{1... | collective-permute-start | bytes 8257544 | tf_op jit(solution)/shard_map/ppermute | solution.py:14
  284.2 4.7 %convolution_bitcast_fusion = f32[256,7168]{1,0:T(8,128)S(1)} fusion(bf16[16,24,7168]{2,1,0:T(8,128)(2,1)} %all-to-all-done, f32[16,24,256]{2,1,0:T(8,128)S(1)} %fusion.12, f32[16,24,256]{2,1,0:T(8,128)S(1)} %fusion.9), kind=kOutput, calls=%fused_computation.3 | convolution fusion | flops 1409875968 | bytes 13631488 | tf_op jit(solution)/shard_map/sch,scd->hd/dot_general | solution.py:74
  288.9 68.6 %collective-permute-done.3 = bf16[1,256,7168]{2,1,0:T(8,128)(2,1)} collective-permute-done((bf16[1,256,7168]{2,1,0:T(8,128)(2,1)}, bf16[1,256,7168]{2,1,0:T(8,128)(2,1)}, u32[]{:S(2)}, u32[]{:S(2)}) %collective-permute-start.3) | collective-permute-done | bytes 3670048 | tf_op jit(solution)/shard_map/ppermute | solution.py:18
  357.5 5.1 %fusion.6 = bf16[1,256,7168]{2,1,0:T(8,128)(2,1)} fusion(f32[256,7168]{1,0:T(8,128)S(1)} %convolution_bitcast_fusion, bf16[1,256,7168]{2,1,0:T(8,128)(2,1)} %collective-permute-done.3), kind=kLoop, calls=%fused_computation.14 | loop fusion | flops 5505024 | bytes 14680064 | tf_op jit(solution)/shard_map/broadcast_in_dim | solution.py:85
  362.6 50.6 %collective-permute-done = bf16[1,192,7168]{2,1,0:T(8,128)(2,1)S(1)} collective-permute-done((bf16[1,192,7168]{2,1,0:T(8,128)(2,1)S(1)}, bf16[1,192,7168]{2,1,0:T(8,128)(2,1)S(1)}, u32[]{:S(2)}, u32[]{:S(2)}) %collective-permute-start) | collective-permute-done | bytes 2752544 | tf_op jit(solution)/shard_map/ppermute | solution.py:14
  413.2 1.5 copy.18
  (29 shorter events, 3.9 us)
Async XLA Ops:
  0.6 2.0 copy-start
  6.3 7.7 %copy-start.5 = (s32[1,192,8]{1,2,0:T(8,128)S(1)}, s32[1,192,8]{1,2,0:T(8,128)}, u32[]{:S(2)}) copy-start(s32[1,192,8]{1,2,0:T(8,128)} %param.10) | copy-start | bytes 18436
  6.3 7.7 %copy-start.6 = (f32[1,192,8]{1,2,0:T(8,128)S(1)}, f32[1,192,8]{1,2,0:T(8,128)}, u32[]{:S(2)}) copy-start(f32[1,192,8]{1,2,0:T(8,128)} %param.11) | copy-start | bytes 18436
  6.3 7.7 %copy-start.2 = (bf16[1,192,7168]{2,1,0:T(8,128)(2,1)S(1)}, bf16[1,192,7168]{2,1,0:T(8,128)(2,1)}, u32[]{:S(2)}) copy-start(bf16[1,192,7168]{2,1,0:T(8,128)(2,1)} %param.9) | copy-start | bytes 8257540
  6.3 79.1 %all-to-all-start.1 = ((bf16[16,24,7168]{2,1,0:T(8,128)(2,1)}), bf16[16,24,7168]{2,1,0:T(8,128)(2,1)}, u32[]{:S(2)}, u32[]{:S(2)}) async-start(bf16[16,24,7168]{2,1,0:T(8,128)(2,1)} %bitcast.65), calls=%async_computation.1 | async-start | bytes 11010048 | tf_op jit(solution)/shard_map/all_to_all | solution.py:56
  88.4 80.3 %all-to-all-start = ((bf16[16,24,7168]{2,1,0:T(8,128)(2,1)}), bf16[16,24,7168]{2,1,0:T(8,128)(2,1)}, u32[]{:S(2)}, u32[]{:S(2)}) async-start(bf16[16,24,7168]{2,1,0:T(8,128)(2,1)} %bitcast.64), calls=%async_computation | async-start | bytes 11010048 | tf_op jit(solution)/shard_map/all_to_all | solution.py:57
  97.3 7.3 %copy-start.4 = (bf16[1,7168,256]{2,1,0:T(8,128)(2,1)S(1)}, bf16[1,7168,256]{2,1,0:T(8,128)(2,1)}, u32[]{:S(2)}) copy-start(bf16[1,7168,256]{2,1,0:T(8,128)(2,1)} %param.13) | copy-start | bytes 11010052
  97.3 93.5 %collective-permute-start.1 = (bf16[1,256,7168]{2,1,0:T(8,128)(2,1)}, bf16[1,256,7168]{2,1,0:T(8,128)(2,1)}, u32[]{:S(2)}, u32[]{:S(2)}) collective-permute-start(bf16[1,256,7168]{2,1,0:T(8,128)(2,1)} %param.15), channel_id=1, source_target_pairs={{0,16},{16,0},{32,48},{48,32},{64,80},{80,64},{96,112},{112,96},{1... | collective-permute-start | bytes 11010056 | tf_op jit(solution)/shard_map/ppermute | solution.py:18
  168.6 5.5 %copy-start.3 = (bf16[1,7168,256]{2,1,0:T(8,128)(2,1)S(1)}, bf16[1,7168,256]{2,1,0:T(8,128)(2,1)}, u32[]{:S(2)}) copy-start(bf16[1,7168,256]{2,1,0:T(8,128)(2,1)} %param.12) | copy-start | bytes 11010052
  182.0 93.6 %all-to-all-start.2 = ((bf16[16,24,7168]{2,1,0:T(8,128)(2,1)}), bf16[16,24,7168]{2,1,0:T(8,128)(2,1)}, u32[]{:S(2)}, u32[]{:S(2)}) async-start(bf16[16,24,7168]{2,1,0:T(8,128)(2,1)} %add_convert_fusion), calls=%async_computation.2 | async-start | bytes 11010048 | tf_op jit(solution)/shard_map/all_to_all | solution.py:75
  190.8 84.1 %collective-permute-start.2 = (bf16[1,256,7168]{2,1,0:T(8,128)(2,1)}, bf16[1,256,7168]{2,1,0:T(8,128)(2,1)}, u32[]{:S(2)}, u32[]{:S(2)}) collective-permute-start(bf16[1,256,7168]{2,1,0:T(8,128)(2,1)} %collective-permute-done.1), channel_id=1, source_target_pairs={{0,32},{16,48},{32,0},{48,16},{64,96},{80,112},{96,64},{112,80},{1... | collective-permute-start | bytes 11010056 | tf_op jit(solution)/shard_map/ppermute | solution.py:18
  274.9 82.6 %collective-permute-start.3 = (bf16[1,256,7168]{2,1,0:T(8,128)(2,1)}, bf16[1,256,7168]{2,1,0:T(8,128)(2,1)}, u32[]{:S(2)}, u32[]{:S(2)}) collective-permute-start(bf16[1,256,7168]{2,1,0:T(8,128)(2,1)} %collective-permute-done.2), channel_id=1, source_target_pairs={{0,64},{16,80},{32,96},{48,112},{64,0},{80,16},{96,32},{112,48},{1... | collective-permute-start | bytes 11010056 | tf_op jit(solution)/shard_map/ppermute | solution.py:18
  279.8 133.3 %collective-permute-start = (bf16[1,192,7168]{2,1,0:T(8,128)(2,1)S(1)}, bf16[1,192,7168]{2,1,0:T(8,128)(2,1)S(1)}, u32[]{:S(2)}, u32[]{:S(2)}) collective-permute-start(bf16[1,192,7168]{2,1,0:T(8,128)(2,1)S(1)} %fusion.2), channel_id=1, source_target_pairs={{0,112},{16,0},{32,16},{48,32},{64,48},{80,64},{96,80},{112,96},{1... | collective-permute-start | bytes 8257544 | tf_op jit(solution)/shard_map/ppermute | solution.py:14
  357.5 57.2 %copy-start.1 = (bf16[1,192,7168]{2,1,0:T(8,128)(2,1)S(1)}, bf16[1,192,7168]{2,1,0:T(8,128)(2,1)}, u32[]{:S(2)}) copy-start(bf16[1,192,7168]{2,1,0:T(8,128)(2,1)} %param.8) | copy-start | bytes 8257540
where the time goes:
time: 416 us; the launch traced here: 415 us
  waiting for transfers between devices  329 us (79%)
  starting transfers between devices  36.5 us (9%)
  matrix products  30.1 us (7%)
  other arithmetic  10.8 us (3%)
  local copies, waits for them, and re-layouts  7.84 us (2%)
    ppermute x3, waiting for transfers between devices, from_partner(): lax.ppermute(x, axis, [(i, i ^ 1 << apart) for i in range(lax.axis_size(a...  149 us
    all_to_all x1, waiting for transfers between devices, local(): lax.all_to_all(send_inputs, 'expert', split_axis=0, concat_axis=0, tiled=...  69.8 us
    all_to_all x1, waiting for transfers between devices, local(): lax.all_to_all(send_scaled, 'expert', split_axis=0, concat_axis=0, tiled=...  59.8 us
    ppermute x1, waiting for transfers between devices, from_behind(): lax.ppermute(x, axis, [(i, (i + by) % length) for i in range(length)])  50.6 us
    all_to_all x1, starting transfers between devices, local(): lax.all_to_all(send_scaled, 'expert', split_axis=0, concat_axis=0, tiled=...  8.88 us
    all_to_all x1, starting transfers between devices, local(): lax.all_to_all(partial_value, 'expert', split_axis=0, concat_axis=0, tile...  8.8 us
  transfers between devices with their start and end apart: 7, of which 5 were waited for; matrix products, arithmetic and copies ran while one was open for 9% of the time, Pallas kernels for 0%

commit v1 on v0

v1 whole, which is shorter than its diff:
```python
import functools

import jax
import jax.numpy as jnp
from jax import lax
from jax.experimental import pallas as pl
from jax.experimental.pallas import tpu as pltpu
from jax.sharding import PartitionSpec as P

CAP = 24
BLOCK = 1024
LIMIT = 48 * 1024 * 1024
F32 = jnp.float32
BF16 = jnp.bfloat16

BEHIND = [(i, (i - 1) % 8) for i in range(8)]
MIRROR = [(i, 7 - i) for i in range(8)]
ODD_BEHIND = [(i, i - 1) for i in range(1, 8, 2)]
AWAY_FIRST = [(0, 2), (2, 0), (4, 6), (6, 4)]
AWAY_LAST = [(2, 7), (6, 3), (0, 1), (4, 5)]
ACROSS = [(i, i ^ 8) for i in range(16)]
SIBLING = [(i, i ^ 1) for i in range(16)]


def along_x(by):
    return [(i, (i // 8) * 8 + ((i // 2 + by) % 4) * 2 + i % 2) for i in range(16)]


OFFSETS = (1, 3, 2)


def params(**kw):
    return pltpu.CompilerParams(vmem_limit_bytes=LIMIT, **kw)


def cost(flops, nbytes):
    return pl.CostEstimate(flops=flops, bytes_accessed=nbytes, transcendentals=0)


def one_hot_rows(plane, routes):
    tokens = routes.shape[1]
    chosen = routes[...]
    line = lax.broadcasted_iota(jnp.int32, (2 * CAP, tokens), 0)
    member = jnp.zeros((2 * CAP, tokens), F32)
    for j in range(2):
        expert = plane[0] if j == 0 else 1 - plane[0]
        named = jnp.max(jnp.where(chosen == expert, 1.0, 0.0), axis=0, keepdims=True)
        member = jnp.where(line >= CAP if j else line < CAP, named, member)
    row = lax.broadcasted_iota(jnp.int32, (tokens, tokens), 0)
    column = lax.broadcasted_iota(jnp.int32, (tokens, tokens), 1)
    upper = jnp.where(row <= column, 1.0, 0.0).astype(BF16)
    count = jnp.dot(member.astype(BF16), upper, preferred_element_type=F32)
    slot = jnp.where(line >= CAP, line - CAP, line).astype(F32)
    return jnp.where((count - 1.0 == slot) & (member > 0.0), 1.0, 0.0)


def pick_body(plane, routes, weight, saved, grad, own, other, first, second, one_hot, gain):
    tokens = routes.shape[1]

    @pl.when(pl.program_id(0) == 0)
    def _():
        hot = one_hot_rows(plane, routes)
        line = lax.broadcasted_iota(jnp.int32, (2 * CAP, tokens), 0)
        scale = jnp.zeros((2 * CAP, tokens), F32)
        for j in range(2):
            expert = plane[0] if j == 0 else 1 - plane[0]
            value = jnp.where(routes[...] == expert, weight[...], 0.0)
            value = jnp.sum(value, axis=0, keepdims=True)
            scale = jnp.where(line >= CAP if j else line < CAP, value, scale)
        one_hot[...] = hot.astype(BF16)
        total = jnp.sum(hot * scale, axis=1, keepdims=True)
        gain[...] = jnp.broadcast_to(total, gain.shape)

    pick = one_hot[...]
    grads = grad[...]
    rows = jnp.dot(pick, saved[...], preferred_element_type=F32)
    scaled = gain[:, :1] * jnp.dot(pick, grads, preferred_element_type=F32)
    own[...] = jnp.concatenate([rows[:CAP], scaled[:CAP]], axis=0).astype(BF16)
    other[...] = jnp.concatenate([rows[CAP:], scaled[CAP:]], axis=0).astype(BF16)
    first[...] = grads[: tokens // 2]
    second[...] = grads[tokens // 2 :]


def pick_rows(plane, routes, weight, saved, grad):
    tokens, depth = saved.shape
    whole = pl.BlockSpec(routes.shape, lambda k: (0, 0))
    tall = pl.BlockSpec((tokens, BLOCK), lambda k: (0, k))
    short = pl.BlockSpec((2 * CAP, BLOCK), lambda k: (0, k))
    half = pl.BlockSpec((tokens // 2, BLOCK), lambda k: (0, k))
    rows = jax.ShapeDtypeStruct((2 * CAP, depth), BF16)
    halves = jax.ShapeDtypeStruct((tokens // 2, depth), BF16)
    return pl.pallas_call(
        pick_body,
        grid=(depth // BLOCK,),
        in_specs=[pl.BlockSpec(memory_space=pltpu.SMEM), whole, whole, tall, tall],
        out_specs=[short, short, half, half],
        out_shape=[rows, rows, halves, halves],
        scratch_shapes=[pltpu.VMEM((2 * CAP, tokens), BF16), pltpu.VMEM((2 * CAP, 128), F32)],
        compiler_params=params(),
        cost_estimate=cost(4 * 48 * tokens * depth, 10 * tokens * depth),
        name="pick_rows",
    )(plane, routes, weight, saved, grad)


def stacked(refs, lower):
    parts = [ref[...].astype(F32)[lower : lower + CAP] for ref in refs]
    return jnp.concatenate(parts, axis=0).astype(BF16)


def contract_last(a, b):
    return lax.dot_general(a, b, (((1,), (1,)), ((), ())), preferred_element_type=F32)


def experts_body(steps, *refs):
    arrivals, (gate, up, down) = refs[:8], refs[8:11]
    mine, sibling, sibling_2, hidden_t = refs[11:15]
    gates, ups, pre_gate, pre_up, from_down, grad_gate, grad_up = refs[15:]
    step = pl.program_id(0)

    @pl.when(step == 0)
    def _():
        pre_gate[...] = jnp.zeros_like(pre_gate)
        pre_up[...] = jnp.zeros_like(pre_up)
        from_down[...] = jnp.zeros_like(from_down)

    @pl.when(step < steps)
    def _():
        rows = stacked(arrivals, 0)
        scaled = stacked(arrivals, CAP)
        gates[step] = gate[...]
        ups[step] = up[...]
        pre_gate[...] += jnp.dot(rows, gate[...], preferred_element_type=F32)
        pre_up[...] += jnp.dot(rows, up[...], preferred_element_type=F32)
        from_down[...] += contract_last(scaled, down[...])

    @pl.when(step == steps)
    def _():
        value = pre_gate[...]
        sigma = 1.0 / (1.0 + jnp.exp(-value))
        activated = value * sigma
        slope = sigma * (1.0 + value * (1.0 - sigma))
        hidden_t[...] = (activated * pre_up[...]).T.astype(BF16)
        grad_gate[...] = (from_down[...] * pre_up[...] * slope).astype(BF16)
        grad_up[...] = (from_down[...] * activated).astype(BF16)

    @pl.when(step >= steps)
    def _():
        at = step - steps
        partial = contract_last(grad_gate[...], gates[at])
        partial = (partial + contract_last(grad_up[...], ups[at])).astype(BF16)
        half = partial.shape[0] // 2
        mine[...] = partial[:half]
        sibling[...] = partial[half : half + half // 2]
        sibling_2[...] = partial[half + half // 2 :]


def experts(arrivals, gate, up, down):
    depth, width = gate.shape
    steps = depth // BLOCK
    count = 8 * CAP

    def block(k):
        return jnp.minimum(k, steps - 1)

    def late(k):
        return jnp.maximum(k - steps, 0)

    out = pl.BlockSpec((count // 2, BLOCK), lambda k: (0, late(k)))
    half = pl.BlockSpec((count // 4, BLOCK), lambda k: (0, late(k)))
    sums = jax.ShapeDtypeStruct((count // 2, depth), BF16)
    halves = jax.ShapeDtypeStruct((count // 4, depth), BF16)
    return pl.pallas_call(
        functools.partial(experts_body, steps),
        grid=(2 * steps,),
        in_specs=[pl.BlockSpec((2 * CAP, BLOCK), lambda k: (0, block(k)))] * 8
        + [pl.BlockSpec((BLOCK, width), lambda k: (block(k), 0))] * 2
        + [pl.BlockSpec((width, BLOCK), lambda k: (0, block(k)))],
        out_specs=[out, half, half, pl.BlockSpec((width, count), lambda k: (0, 0))],
        out_shape=[sums, halves, halves, jax.ShapeDtypeStruct((width, count), BF16)],
        scratch_shapes=[pltpu.VMEM((steps, BLOCK, width), BF16)] * 2
        + [pltpu.VMEM((count, width), F32)] * 3
        + [pltpu.VMEM((count, width), BF16)] * 2,
        compiler_params=params(),
        cost_estimate=cost(10 * count * depth * width, 2 * depth * (3 * width + 3 * count)),
        name="experts",
    )(*arrivals, gate, up, down)


def split_body(mine, first, second, *outs):
    theirs = jnp.concatenate([first[...].astype(F32), second[...].astype(F32)], axis=0)
    total = mine[...].astype(F32) + theirs
    for i, out in enumerate(outs):
        out[...] = total[i * CAP : (i + 1) * CAP].astype(BF16)


def split_sum(mine, first, second):
    count, depth = mine.shape
    spec = pl.BlockSpec((count, BLOCK), lambda k: (0, k))
    half = pl.BlockSpec((count // 2, BLOCK), lambda k: (0, k))
    out = pl.BlockSpec((CAP, BLOCK), lambda k: (0, k))
    return pl.pallas_call(
        split_body,
        grid=(depth // BLOCK,),
        in_specs=[spec, half, half],
        out_specs=[out] * 4,
        out_shape=[jax.ShapeDtypeStruct((CAP, depth), BF16)] * 4,
        compiler_params=params(),
        cost_estimate=cost(count * depth, 6 * count * depth),
        name="split_sum",
    )(mine, first, second)


def down_body(*refs):
    left, right = refs[16:18]
    mirror = jnp.concatenate([ref[...].astype(F32) for ref in refs[18:-1]], axis=0)
    out = refs[-1]
    total = jnp.dot(left[...], stacked(refs[:8], CAP), preferred_element_type=F32)
    total += jnp.dot(right[...], stacked(refs[8:16], CAP), preferred_element_type=F32)
    out[...] = (total + mirror).astype(BF16)


def down_grads(arrivals, left, right, mirror):
    width, depth = left.shape[0], mirror[0].shape[1]
    whole = pl.BlockSpec(left.shape, lambda k: (0, 0))
    return pl.pallas_call(
        down_body,
        grid=(depth // BLOCK,),
        in_specs=[pl.BlockSpec((2 * CAP, BLOCK), lambda k: (0, k))] * 16
        + [whole, whole]
        + [pl.BlockSpec((part.shape[0], BLOCK), lambda k: (0, k)) for part in mirror],
        out_specs=pl.BlockSpec((width, BLOCK), lambda k: (0, k)),
        out_shape=jax.ShapeDtypeStruct((width, depth), BF16),
        compiler_params=params(),
        cost_estimate=cost(2 * 384 * depth * width, 2 * depth * (2 * width + 768)),
        name="down_grads",
    )(*arrivals, left, right, *mirror)


def combine_body(odd, plane, routes, first, direct, away, own, other, out, place):
    @pl.when(pl.program_id(0) == 0)
    def _():
        place[...] = one_hot_rows(plane, routes).T.astype(BF16)

    rows = jnp.concatenate([own[...].astype(F32), other[...].astype(F32)], axis=0).astype(BF16)
    added = jnp.dot(place[...], rows, preferred_element_type=F32)
    half = first.shape[0]
    out[:half] = (first[...].astype(F32) + added[:half]).astype(BF16)
    rest = jnp.where(odd[0] == 1, away[...].astype(F32), direct[...].astype(F32))
    out[half:] = (rest + added[half:]).astype(BF16)


def combine(odd, plane, routes, first, direct, away, own, other):
    half, depth = first.shape
    part = pl.BlockSpec((half, BLOCK), lambda k: (0, k))
    rows = pl.BlockSpec((CAP, BLOCK), lambda k: (0, k))
    return pl.pallas_call(
        combine_body,
        grid=(depth // BLOCK,),
        in_specs=[
            pl.BlockSpec(memory_space=pltpu.SMEM),
            pl.BlockSpec(memory_space=pltpu.SMEM),
            pl.BlockSpec(routes.shape, lambda k: (0, 0)),
            part,
            part,
            part,
            rows,
            rows,
        ],
        out_specs=pl.BlockSpec((2 * half, BLOCK), lambda k: (0, k)),
        out_shape=jax.ShapeDtypeStruct((2 * half, depth), BF16),
        scratch_shapes=[pltpu.VMEM((2 * half, 2 * CAP), BF16)],
        compiler_params=params(),
        cost_estimate=cost(4 * half * 48 * depth, 12 * half * depth),
        name="combine",
    )(odd, plane, routes, first, direct, away, own, other)


def after(value, *others):
    return lax.optimization_barrier((value, others))[0]


def go(rows, perm, axis="expert"):
    return lax.ppermute(rows, axis, perm)


def local(
    saved_input, grad_output, routes, route_weight, gate_weight, up_weight, down_weight, mirror_grad
):
    plane = (lax.axis_index("expert") // 8).astype(jnp.int32).reshape(1)
    odd = (lax.axis_index("pipe") % 2).astype(jnp.int32).reshape(1)
    weights = (gate_weight[0], up_weight[0], down_weight[0])
    pairs = [(s * 16 + e, ((s - 1) % 8) * 16 + (e ^ 8)) for s in range(8) for e in range(16)]

    behind_routes = go(after(routes[0].T, plane), BEHIND, "pipe")
    own, other, first, second = pick_rows(
        plane, routes[0].T, route_weight[0].T, saved_input[0], grad_output[0]
    )
    across = go(after(other, behind_routes), ACROSS)
    direct = go(second, ODD_BEHIND, "pipe")
    near = [own] + [go(own, along_x(by)) for by in OFFSETS]
    mirror = [go(after(mirror_grad[0], across, near[1], near[2]), MIRROR, "pipe")]
    near = [near[0]] + [after(part, across, direct) for part in near[1:]]
    away = go(after(second, across), AWAY_FIRST, "pipe")
    near = near + [go(part, SIBLING) for part in near]
    far = [after(across, *near[4:])]
    far = far + [go(far[0], along_x(by)) for by in OFFSETS]
    near[0] = after(near[0], *near[4:], away)
    near_mine, near_sibling, near_sibling_2, near_hidden = experts(near, *weights)
    far = [after(part, near_hidden) for part in far]
    near_sibling = after(near_sibling, *far)
    near_sibling_2 = after(near_sibling_2, near_sibling)
    near_parts = split_sum(near_mine, go(near_sibling, SIBLING), go(near_sibling_2, SIBLING))
    far = far + [go(part, SIBLING) for part in far]
    far[0] = after(far[0], near_parts, mirror[0])
    away = go(after(away, *far[4:]), AWAY_LAST, "pipe")
    near_back = [go(after(part, *far[4:]), along_x(-by)) for part, by in zip(near_parts[1:], OFFSETS)]
    far_mine, far_sibling, far_sibling_2, far_hidden = experts(far, *weights)
    near_back[0] = after(near_back[0], far_hidden)
    near_total = add_up(near_parts[0], near_back)
    first = go(after(first, near_parts), BEHIND, "pipe")
    far_sibling = after(far_sibling, near_total)
    far_sibling_2 = after(far_sibling_2, far_sibling)
    far_mine = after(far_mine, near_total)
    far_parts = split_sum(far_mine, go(far_sibling, SIBLING), go(far_sibling_2, SIBLING))
    far_back = [go(part, along_x(-by)) for part, by in zip(far_parts[1:], OFFSETS)]
    mirror[0] = after(mirror[0], far_hidden)
    down_grad = down_grads(near + far, near_hidden, far_hidden, mirror)
    far_total = add_up(after(far_parts[0], down_grad, away, first), far_back)
    near_back = go(near_total, BEHIND, "pipe")
    far_back = go(far_total, pairs, ("pipe", "expert"))
    back = combine(odd, plane, behind_routes, first, direct, away, near_back, far_back)
    return back[None], down_grad[None]


def add_up(first, others):
    total = first.astype(F32)
    for other in others:
        total = total + other.astype(F32)
    return total.astype(BF16)


def solution(mesh):
    in_specs = (
        P("pipe", "expert", None),
        P("pipe", "expert", None),
        P("pipe", "expert", None),
        P("pipe", "expert", None),
        P("pipe", None, "expert"),
        P("pipe", None, "expert"),
        P("pipe", "expert", None),
        P("pipe", "expert", None),
    )
    out_specs = (P("pipe", "expert", None), P("pipe", "expert", None))
    return jax.shard_map(local, mesh=mesh, in_specs=in_specs, out_specs=out_specs, check_vma=False)
```

time: 416 us -> 209 us (0.50)
  waiting for transfers between devices: 329 us -> 115 us
  Pallas kernels: 0 us -> 51.1 us
  matrix products: 30.1 us -> 0 us
  other arithmetic: 10.8 us -> 2.32 us
    all_to_all x3 -> x0, waiting for transfers between devices: 130 us -> none  [the longest x1 69.8 us: local(): lax.all_to_all(send_inputs, 'expert', split_axis=0, concat_axis=0, tiled=...]
    ppermute x4 -> x33, waiting for transfers between devices: 199 us -> 115 us  [go(): return lax.ppermute(rows, axis, perm)]
    pallas_call x0 -> x7, Pallas kernels: none -> 51.1 us  [the longest x2 27.6 us: experts(): pl.pallas_call(functools.partial(experts_body, steps), grid=(2 * steps,),...]
    dot_general x9 -> x0, matrix products: 30.1 us -> none  [the longest x1 6.1 us: local(): jnp.einsum('sch,dh->scd', grad_up, up_local, preferred_element_type=jnp.f...]
    all_to_all x3 -> x0, starting transfers between devices: 25.4 us -> none  [the longest x1 8.88 us: local(): lax.all_to_all(send_scaled, 'expert', split_axis=0, concat_axis=0, tiled=...]
    ppermute x4 -> x33, starting transfers between devices: 11.2 us -> 32.5 us  [go(): return lax.ppermute(rows, axis, perm)]
    broadcast_in_dim x2 -> x0, local copies, waits for them, and re-layouts: 6.04 us -> none  [the longest x1 3.04 us: local(): jnp.broadcast_to(input_rows[:, None], (windows, split_count, CAP, D))]
    broadcast_in_dim x1 -> x0, other arithmetic: 5.15 us -> none  [local(): (local_grad + mirrored[0].astype(jnp.float32)).astype(jnp.bfloat16)[None]]
  transfers between devices with their start and end apart: 7 -> 33, of which waited for: 5 -> 19; matrix products, arithmetic and copies ran while one was open for 9% -> 1% of each run, Pallas kernels for 0% -> 22%
where the time goes in v1:
time: 209 us; the launch traced here: 206 us
  waiting for transfers between devices  115 us (55%)
  Pallas kernels  51.1 us (24%)
  starting transfers between devices  32.5 us (16%)
  local copies, waits for them, and re-layouts  4.12 us (2%)
  other arithmetic  2.32 us (1%)
    ppermute x33, waiting for transfers between devices, go(): return lax.ppermute(rows, axis, perm)  115 us
    ppermute x33, starting transfers between devices, go(): return lax.ppermute(rows, axis, perm)  32.5 us
    pallas_call x2, Pallas kernels, experts(): pl.pallas_call(functools.partial(experts_body, steps), grid=(2 * steps,),...  27.6 us
    pallas_call x1, Pallas kernels, down_grads(): pl.pallas_call(down_body, grid=(depth // BLOCK,), in_specs=[pl.BlockSpec(...  9.37 us
    pallas_call x1, Pallas kernels, combine(): pl.pallas_call(combine_body, grid=(depth // BLOCK,), in_specs=[pl.BlockSp...  6.65 us
    pallas_call x1, Pallas kernels, pick_rows(): pl.pallas_call(pick_body, grid=(depth // BLOCK,), in_specs=[pl.BlockSpec(...  6.01 us
  transfers between devices with their start and end apart: 33, of which 19 were waited for; matrix products, arithmetic and copies ran while one was open for 1% of the time, Pallas kernels for 22%

profile of v1, /device:TPU:6, one launch (start us, length us, event | category | flops | bytes accessed | tf_op | source)
XLA Modules:
  0.0 206.4 jit_solution(13317453438608969981)
XLA Ops:
  0.6 5.1 %collective-permute-start = (s32[8,192]{1,0:T(8,128)}, s32[8,192]{1,0:T(8,128)S(1)}, u32[]{:S(2)}, u32[]{:S(2)}) collective-permute-start(s32[8,192]{1,0:T(8,128)} %bitcast.17), channel_id=1, source_target_pairs={{0,112},{16,0},{32,16},{48,32},{64,48},{80,64},{96,80},{112,96},{1... | collective-permute-start | bytes 18440 | tf_op jit(solution)/shard_map/ppermute | solution.py:283
  7.2 6.0 %pick_rows.1 = (bf16[48,7168]{1,0:T(8,128)(2,1)S(1)}, bf16[48,7168]{1,0:T(8,128)(2,1)S(1)}, bf16[96,7168]{1,0:T(8,128)(2,1)S(1)}, bf16[96,7168]{1,0:T(8,128)(2,1)S(1)}) custom-call(s32[1]{0:T(128)} %bitcast.1.plane, s32[8,192]{1,0:T(8,128)S(1)} %bitcast.18, f32[8,192]{1,0:T(8,128)S(1)} %bitcast.16, bf16[192,7168]{1,0:T(8,128)(2,1)} %bitcast.27, ...), custom_call_target="tpu_custom_call" | custom-call | flops 264241152 | bytes 13762560 | tf_op jit(solution)/shard_map/pick_rows/pallas_call | solution.py:92
  13.7 1.5 collective-permute-start.6
  15.3 2.9 %collective-permute-start.3 = (bf16[48,7168]{1,0:T(8,128)(2,1)S(1)}, bf16[48,7168]{1,0:T(8,128)(2,1)S(1)}, u32[]{:S(2)}, u32[]{:S(2)}) collective-permute-start(bf16[48,7168]{1,0:T(8,128)(2,1)S(1)} %get-tuple-element.53), channel_id=1, source_target_pairs={{0,8},{1,9},{2,10},{3,11},{4,12},{5,13},{6,14},{7,15},{8,0},{9,1},... | collective-permute-start | bytes 2064392 | tf_op jit(solution)/shard_map/ppermute | solution.py:283
  19.5 10.7 %collective-permute-done.2.refs_1_ = bf16[48,7168]{1,0:T(8,128)(2,1)S(1)} collective-permute-done((bf16[48,7168]{1,0:T(8,128)(2,1)S(1)}, bf16[48,7168]{1,0:T(8,128)(2,1)S(1)}, u32[]{:S(2)}, u32[]{:S(2)}) %collective-permute-start.2) | collective-permute-done | bytes 688160 | tf_op jit(solution)/shard_map/ppermute | solution.py:283
  31.6 1.6 collective-permute-done.3.refs_0_.refs_8_
  34.9 1.9 collective-permute-start.10
  36.8 14.0 %collective-permute-done.4.direct = bf16[96,7168]{1,0:T(8,128)(2,1)S(1)} collective-permute-done((bf16[96,7168]{1,0:T(8,128)(2,1)S(1)}, bf16[96,7168]{1,0:T(8,128)(2,1)S(1)}, u32[]{:S(2)}, u32[]{:S(2)}) %collective-permute-start.4) | collective-permute-done | bytes 1376288 | tf_op jit(solution)/shard_map/ppermute | solution.py:283
  55.0 1.7 collective-permute-start.11
  58.4 42.1 %collective-permute-done.10 = bf16[96,7168]{1,0:T(8,128)(2,1)} collective-permute-done((bf16[96,7168]{1,0:T(8,128)(2,1)S(1)}, bf16[96,7168]{1,0:T(8,128)(2,1)}, u32[]{:S(2)}, u32[]{:S(2)}) %collective-permute-start.10) | collective-permute-done | bytes 1376288 | tf_op jit(solution)/shard_map/ppermute | solution.py:283
  100.5 13.8 %experts.2 = (bf16[96,7168]{1,0:T(8,128)(2,1)}, bf16[48,7168]{1,0:T(8,128)(2,1)S(1)}, bf16[48,7168]{1,0:T(8,128)(2,1)S(1)}, bf16[256,192]{1,0:T(8,128)(2,1)S(1)}) custom-call(bf16[48,7168]{1,0:T(8,128)(2,1)S(1)} %get-tuple-element.59.refs_0_, bf16[48,7168]{1,0:T(8,128)(2,1)S(1)} %collective-permute-done.2.refs_1_, ...), custom_call_target="tpu_custom_call" | custom-call | flops 3523215360 | bytes 19267584 | tf_op jit(solution)/shard_map/experts/pallas_call | solution.py:172
  121.5 2.1 %collective-permute-start.25 = (bf16[24,7168]{1,0:T(8,128)(2,1)S(1)}, bf16[24,7168]{1,0:T(8,128)(2,1)S(1)}, u32[]{:S(2)}, u32[]{:S(2)}) collective-permute-start(bf16[24,7168]{1,0:T(8,128)(2,1)S(1)} %get-tuple-element.83), channel_id=1, source_target_pairs={{0,4},{1,5},{2,6},{3,7},{4,0},{5,1},{6,2},{7,3},{8,12},{9,13},{10,... | collective-permute-start | bytes 1032200 | tf_op jit(solution)/shard_map/ppermute | solution.py:283
  124.4 2.4 %collective-permute-start.24 = (bf16[24,7168]{1,0:T(8,128)(2,1)S(1)}, bf16[24,7168]{1,0:T(8,128)(2,1)}, u32[]{:S(2)}, u32[]{:S(2)}) collective-permute-start(bf16[24,7168]{1,0:T(8,128)(2,1)S(1)} %get-tuple-element.82), channel_id=1, source_target_pairs={{0,2},{1,3},{2,4},{3,5},{4,6},{5,7},{6,0},{7,1},{8,10},{9,11},{10,... | collective-permute-start | bytes 1032200 | tf_op jit(solution)/shard_map/ppermute | solution.py:283
  126.9 17.5 %collective-permute-done.23.refs_18_ = bf16[256,7168]{1,0:T(8,128)(2,1)} collective-permute-done((bf16[256,7168]{1,0:T(8,128)(2,1)}, bf16[256,7168]{1,0:T(8,128)(2,1)}, u32[]{:S(2)}, u32[]{:S(2)}) %collective-permute-start.23) | collective-permute-done | bytes 3670048 | tf_op jit(solution)/shard_map/ppermute | solution.py:283
  144.4 2.4 %collective-permute-start.21 = (bf16[96,7168]{1,0:T(8,128)(2,1)}, bf16[96,7168]{1,0:T(8,128)(2,1)}, u32[]{:S(2)}, u32[]{:S(2)}) collective-permute-start(bf16[96,7168]{1,0:T(8,128)(2,1)} %collective-permute-done.10), channel_id=1, source_target_pairs={{32,112},{96,48},{0,16},{64,80},{33,113},{97,49},{1,17},{65,81},{3... | collective-permute-start | bytes 4128776 | tf_op jit(solution)/shard_map/ppermute | solution.py:283
  146.8 13.8 %experts.3 = (bf16[96,7168]{1,0:T(8,128)(2,1)}, bf16[48,7168]{1,0:T(8,128)(2,1)S(1)}, bf16[48,7168]{1,0:T(8,128)(2,1)S(1)}, bf16[256,192]{1,0:T(8,128)(2,1)S(1)}) custom-call(bf16[48,7168]{1,0:T(8,128)(2,1)S(1)} %collective-permute-done.3.refs_0_.refs_8_, bf16[48,7168]{1,0:T(8,128)(2,1)S(1)} %collective-permute-done.11.refs_1_.refs_9_, ...), custom_call_target="tpu_custom_call" | custom-call | flops 3523215360 | bytes 19267584 | tf_op jit(solution)/shard_map/experts/pallas_call | solution.py:172
  160.7 2.2 %add_convert_fusion.1 = bf16[24,7168]{1,0:T(8,128)(2,1)} fusion(bf16[24,7168]{1,0:T(8,128)(2,1)S(1)} %collective-permute-done.25, bf16[24,7168]{1,0:T(8,128)(2,1)} %collective-permute-done.24, bf16[24,7168]{1,0:T(8,128)(2,1)} %collective-permute-done.22, bf16[24,7168]{1,0:T(8,128)(2,1)S(1)} %get-tuple-element.71), kind=kLoop, calls=%fused_computation.1 | loop fusion | flops 1376256 | bytes 1720320 | tf_op jit(solution)/shard_map/convert_element_type | solution.py:339
  163.3 1.6 collective-permute-done.27.first
  169.5 2.1 %collective-permute-start.30 = (bf16[24,7168]{1,0:T(8,128)(2,1)S(1)}, bf16[24,7168]{1,0:T(8,128)(2,1)S(1)}, u32[]{:S(2)}, u32[]{:S(2)}) collective-permute-start(bf16[24,7168]{1,0:T(8,128)(2,1)S(1)} %get-tuple-element.94), channel_id=1, source_target_pairs={{0,2},{1,3},{2,4},{3,5},{4,6},{5,7},{6,0},{7,1},{8,10},{9,11},{10,... | collective-permute-start | bytes 1032200 | tf_op jit(solution)/shard_map/ppermute | solution.py:283
  171.6 9.4 %down_grads.1 = bf16[256,7168]{1,0:T(8,128)(2,1)} custom-call(bf16[48,7168]{1,0:T(8,128)(2,1)S(1)} %get-tuple-element.59.refs_0_, bf16[48,7168]{1,0:T(8,128)(2,1)S(1)} %collective-permute-done.2.refs_1_, bf16[48,7168]{1,0:T(8,128)(2,1)S(1)} %collective-permute-done.6.refs_2_, bf16[48,7168]{1,0:T(8,128)(2,1)S(1)} %collective-permute-done.8.refs_3_, ...), custom_call_target="tpu_custom_call" | custom-call | flops 1409286144 | bytes 18350080 | tf_op jit(solution)/shard_map/down_grads/pallas_call | solution.py:225
  181.1 5.1 %collective-permute-done.30 = bf16[24,7168]{1,0:T(8,128)(2,1)S(1)} collective-permute-done((bf16[24,7168]{1,0:T(8,128)(2,1)S(1)}, bf16[24,7168]{1,0:T(8,128)(2,1)S(1)}, u32[]{:S(2)}, u32[]{:S(2)}) %collective-permute-start.30) | collective-permute-done | bytes 344096 | tf_op jit(solution)/shard_map/ppermute | solution.py:283
  187.4 3.5 %collective-permute-done.26.own = bf16[24,7168]{1,0:T(8,128)(2,1)S(1)} collective-permute-done((bf16[24,7168]{1,0:T(8,128)(2,1)}, bf16[24,7168]{1,0:T(8,128)(2,1)S(1)}, u32[]{:S(2)}, u32[]{:S(2)}) %collective-permute-start.26) | collective-permute-done | bytes 344096 | tf_op jit(solution)/shard_map/ppermute | solution.py:283
  190.9 8.9 %collective-permute-done.32.other = bf16[24,7168]{1,0:T(8,128)(2,1)S(1)} collective-permute-done((bf16[24,7168]{1,0:T(8,128)(2,1)S(1)}, bf16[24,7168]{1,0:T(8,128)(2,1)S(1)}, u32[]{:S(2)}, u32[]{:S(2)}) %collective-permute-start.32) | collective-permute-done | bytes 344096 | tf_op jit(solution)/shard_map/ppermute | solution.py:283
  199.8 6.7 %combine.1 = bf16[192,7168]{1,0:T(8,128)(2,1)} custom-call(s32[1]{0:T(128)} %bitcast.odd, s32[1]{0:T(128)} %bitcast.1.plane, s32[8,192]{1,0:T(8,128)S(1)} %collective-permute-done.routes, bf16[96,7168]{1,0:T(8,128)(2,1)} %collective-permute-done.16.first, bf16[96,7168]{1,0:T(8,128)(2,1)S(1)} %collective-permute-done.4.direct, ...), custom_call_target="tpu_custom_call" | custom-call | flops 132120576 | bytes 8257536 | tf_op jit(solution)/shard_map/combine/pallas_call | solution.py:256
  (83 shorter events, 26.6 us)
Async XLA Ops:
  0.6 14.6 %collective-permute-start = (s32[8,192]{1,0:T(8,128)}, s32[8,192]{1,0:T(8,128)S(1)}, u32[]{:S(2)}, u32[]{:S(2)}) collective-permute-start(s32[8,192]{1,0:T(8,128)} %bitcast.17), channel_id=1, source_target_pairs={{0,112},{16,0},{32,16},{48,32},{64,48},{80,64},{96,80},{112,96},{1... | collective-permute-start | bytes 18440 | tf_op jit(solution)/shard_map/ppermute | solution.py:283
  13.2 17.0 %collective-permute-start.2 = (bf16[48,7168]{1,0:T(8,128)(2,1)S(1)}, bf16[48,7168]{1,0:T(8,128)(2,1)S(1)}, u32[]{:S(2)}, u32[]{:S(2)}) collective-permute-start(bf16[48,7168]{1,0:T(8,128)(2,1)S(1)} %get-tuple-element.59.refs_0_), channel_id=1, source_target_pairs={{0,2},{1,3},{2,4},{3,5},{4,6},{5,7},{6,0},{7,1},{8,10},{9,11},{10,... | collective-permute-start | bytes 2064392 | tf_op jit(solution)/shard_map/ppermute | solution.py:283
  13.7 17.8 %collective-permute-start.6 = (bf16[48,7168]{1,0:T(8,128)(2,1)S(1)}, bf16[48,7168]{1,0:T(8,128)(2,1)S(1)}, u32[]{:S(2)}, u32[]{:S(2)}) collective-permute-start(bf16[48,7168]{1,0:T(8,128)(2,1)S(1)} %get-tuple-element.59.refs_0_), channel_id=1, source_target_pairs={{0,6},{1,7},{2,0},{3,1},{4,2},{5,3},{6,4},{7,5},{8,14},{9,15},{10,... | collective-permute-start | bytes 2064392 | tf_op jit(solution)/shard_map/ppermute | solution.py:283
  15.3 17.8 %collective-permute-start.3 = (bf16[48,7168]{1,0:T(8,128)(2,1)S(1)}, bf16[48,7168]{1,0:T(8,128)(2,1)S(1)}, u32[]{:S(2)}, u32[]{:S(2)}) collective-permute-start(bf16[48,7168]{1,0:T(8,128)(2,1)S(1)} %get-tuple-element.53), channel_id=1, source_target_pairs={{0,8},{1,9},{2,10},{3,11},{4,12},{5,13},{6,14},{7,15},{8,0},{9,1},... | collective-permute-start | bytes 2064392 | tf_op jit(solution)/shard_map/ppermute | solution.py:283
  18.2 32.7 %collective-permute-start.4 = (bf16[96,7168]{1,0:T(8,128)(2,1)S(1)}, bf16[96,7168]{1,0:T(8,128)(2,1)S(1)}, u32[]{:S(2)}, u32[]{:S(2)}) collective-permute-start(bf16[96,7168]{1,0:T(8,128)(2,1)S(1)} %get-tuple-element.58), channel_id=1, source_target_pairs={{16,0},{48,32},{80,64},{112,96},{17,1},{49,33},{81,65},{113,97},{1... | collective-permute-start | bytes 4128776 | tf_op jit(solution)/shard_map/ppermute | solution.py:283
  33.1 111.2 %collective-permute-start.23 = (bf16[256,7168]{1,0:T(8,128)(2,1)}, bf16[256,7168]{1,0:T(8,128)(2,1)}, u32[]{:S(2)}, u32[]{:S(2)}) collective-permute-start(bf16[256,7168]{1,0:T(8,128)(2,1)} %bitcast.29), channel_id=1, source_target_pairs={{0,112},{16,96},{32,80},{48,64},{64,48},{80,32},{96,16},{112,0},{1... | collective-permute-start | bytes 11010056 | tf_op jit(solution)/shard_map/ppermute | solution.py:283
  33.5 17.3 %collective-permute-start.8 = (bf16[48,7168]{1,0:T(8,128)(2,1)S(1)}, bf16[48,7168]{1,0:T(8,128)(2,1)S(1)}, u32[]{:S(2)}, u32[]{:S(2)}) collective-permute-start(bf16[48,7168]{1,0:T(8,128)(2,1)S(1)} %get-tuple-element.59.refs_0_), channel_id=1, source_target_pairs={{0,4},{1,5},{2,6},{3,7},{4,0},{5,1},{6,2},{7,3},{8,12},{9,13},{10,... | collective-permute-start | bytes 2064392 | tf_op jit(solution)/shard_map/ppermute | solution.py:283
  34.9 16.5 %collective-permute-start.1 = (bf16[48,7168]{1,0:T(8,128)(2,1)S(1)}, bf16[48,7168]{1,0:T(8,128)(2,1)S(1)}, u32[]{:S(2)}, u32[]{:S(2)}) collective-permute-start(bf16[48,7168]{1,0:T(8,128)(2,1)S(1)} %get-tuple-element.59.refs_0_), channel_id=1, source_target_pairs={{0,1},{1,0},{2,3},{3,2},{4,5},{5,4},{6,7},{7,6},{8,9},{9,8},{10,11... | collective-permute-start | bytes 2064392 | tf_op jit(solution)/shard_map/ppermute | solution.py:283
  34.9 65.6 %collective-permute-start.10 = (bf16[96,7168]{1,0:T(8,128)(2,1)S(1)}, bf16[96,7168]{1,0:T(8,128)(2,1)}, u32[]{:S(2)}, u32[]{:S(2)}) collective-permute-start(bf16[96,7168]{1,0:T(8,128)(2,1)S(1)} %get-tuple-element.58), channel_id=1, source_target_pairs={{0,32},{32,0},{64,96},{96,64},{1,33},{33,1},{65,97},{97,65},{2,34}... | collective-permute-start | bytes 4128776 | tf_op jit(solution)/shard_map/ppermute | solution.py:283
  55.0 59.3 %collective-permute-start.11 = (bf16[48,7168]{1,0:T(8,128)(2,1)S(1)}, bf16[48,7168]{1,0:T(8,128)(2,1)S(1)}, u32[]{:S(2)}, u32[]{:S(2)}) collective-permute-start(bf16[48,7168]{1,0:T(8,128)(2,1)S(1)} %collective-permute-done.3.refs_0_.refs_8_), channel_id=1, source_target_pairs={{0,2},{1,3},{2,4},{3,5},{4,6},{5,7},{6,0},{7,1},{8,10},{9,11},{10,... | collective-permute-start | bytes 2064392 | tf_op jit(solution)/shard_map/ppermute | solution.py:283
  56.7 57.6 %collective-permute-start.12 = (bf16[48,7168]{1,0:T(8,128)(2,1)S(1)}, bf16[48,7168]{1,0:T(8,128)(2,1)S(1)}, u32[]{:S(2)}, u32[]{:S(2)}) collective-permute-start(bf16[48,7168]{1,0:T(8,128)(2,1)S(1)} %collective-permute-done.3.refs_0_.refs_8_), channel_id=1, source_target_pairs={{0,6},{1,7},{2,0},{3,1},{4,2},{5,3},{6,4},{7,5},{8,14},{9,15},{10,... | collective-permute-start | bytes 2064392 | tf_op jit(solution)/shard_map/ppermute | solution.py:283
  57.0 57.3 %collective-permute-start.13 = (bf16[48,7168]{1,0:T(8,128)(2,1)S(1)}, bf16[48,7168]{1,0:T(8,128)(2,1)S(1)}, u32[]{:S(2)}, u32[]{:S(2)}) collective-permute-start(bf16[48,7168]{1,0:T(8,128)(2,1)S(1)} %collective-permute-done.3.refs_0_.refs_8_), channel_id=1, source_target_pairs={{0,4},{1,5},{2,6},{3,7},{4,0},{5,1},{6,2},{7,3},{8,12},{9,13},{10,... | collective-permute-start | bytes 2064392 | tf_op jit(solution)/shard_map/ppermute | solution.py:283
  114.9 4.9 %collective-permute-start.17 = (bf16[48,7168]{1,0:T(8,128)(2,1)S(1)}, bf16[48,7168]{1,0:T(8,128)(2,1)S(1)}, u32[]{:S(2)}, u32[]{:S(2)}) collective-permute-start(bf16[48,7168]{1,0:T(8,128)(2,1)S(1)} %collective-permute-done.3.refs_0_.refs_8_), channel_id=1, source_target_pairs={{0,1},{1,0},{2,3},{3,2},{4,5},{5,4},{6,7},{7,6},{8,9},{9,8},{10,11... | collective-permute-start | bytes 2064392 | tf_op jit(solution)/shard_map/ppermute | solution.py:283
  115.0 4.8 %collective-permute-start.18 = (bf16[48,7168]{1,0:T(8,128)(2,1)S(1)}, bf16[48,7168]{1,0:T(8,128)(2,1)S(1)}, u32[]{:S(2)}, u32[]{:S(2)}) collective-permute-start(bf16[48,7168]{1,0:T(8,128)(2,1)S(1)} %collective-permute-done.11.refs_1_.refs_9_), channel_id=1, source_target_pairs={{0,1},{1,0},{2,3},{3,2},{4,5},{5,4},{6,7},{7,6},{8,9},{9,8},{10,11... | collective-permute-start | bytes 2064392 | tf_op jit(solution)/shard_map/ppermute | solution.py:283
  121.5 39.1 %collective-permute-start.25 = (bf16[24,7168]{1,0:T(8,128)(2,1)S(1)}, bf16[24,7168]{1,0:T(8,128)(2,1)S(1)}, u32[]{:S(2)}, u32[]{:S(2)}) collective-permute-start(bf16[24,7168]{1,0:T(8,128)(2,1)S(1)} %get-tuple-element.83), channel_id=1, source_target_pairs={{0,4},{1,5},{2,6},{3,7},{4,0},{5,1},{6,2},{7,3},{8,12},{9,13},{10,... | collective-permute-start | bytes 1032200 | tf_op jit(solution)/shard_map/ppermute | solution.py:283
  123.6 37.0 %collective-permute-start.22 = (bf16[24,7168]{1,0:T(8,128)(2,1)S(1)}, bf16[24,7168]{1,0:T(8,128)(2,1)}, u32[]{:S(2)}, u32[]{:S(2)}) collective-permute-start(bf16[24,7168]{1,0:T(8,128)(2,1)S(1)} %get-tuple-element.77), channel_id=1, source_target_pairs={{0,6},{1,7},{2,0},{3,1},{4,2},{5,3},{6,4},{7,5},{8,14},{9,15},{10,... | collective-permute-start | bytes 1032200 | tf_op jit(solution)/shard_map/ppermute | solution.py:283
  124.4 36.2 %collective-permute-start.24 = (bf16[24,7168]{1,0:T(8,128)(2,1)S(1)}, bf16[24,7168]{1,0:T(8,128)(2,1)}, u32[]{:S(2)}, u32[]{:S(2)}) collective-permute-start(bf16[24,7168]{1,0:T(8,128)(2,1)S(1)} %get-tuple-element.82), channel_id=1, source_target_pairs={{0,2},{1,3},{2,4},{3,5},{4,6},{5,7},{6,0},{7,1},{8,10},{9,11},{10,... | collective-permute-start | bytes 1032200 | tf_op jit(solution)/shard_map/ppermute | solution.py:283
  126.8 54.2 %collective-permute-start.16 = (bf16[96,7168]{1,0:T(8,128)(2,1)S(1)}, bf16[96,7168]{1,0:T(8,128)(2,1)}, u32[]{:S(2)}, u32[]{:S(2)}) collective-permute-start(bf16[96,7168]{1,0:T(8,128)(2,1)S(1)} %get-tuple-element.75), channel_id=1, source_target_pairs={{0,112},{16,0},{32,16},{48,32},{64,48},{80,64},{96,80},{112,96},{1... | collective-permute-start | bytes 4128776 | tf_op jit(solution)/shard_map/ppermute | solution.py:283
  144.4 36.8 %collective-permute-start.21 = (bf16[96,7168]{1,0:T(8,128)(2,1)}, bf16[96,7168]{1,0:T(8,128)(2,1)}, u32[]{:S(2)}, u32[]{:S(2)}) collective-permute-start(bf16[96,7168]{1,0:T(8,128)(2,1)} %collective-permute-done.10), channel_id=1, source_target_pairs={{32,112},{96,48},{0,16},{64,80},{33,113},{97,49},{1,17},{65,81},{3... | collective-permute-start | bytes 4128776 | tf_op jit(solution)/shard_map/ppermute | solution.py:283
  168.1 13.1 %collective-permute-start.31 = (bf16[24,7168]{1,0:T(8,128)(2,1)S(1)}, bf16[24,7168]{1,0:T(8,128)(2,1)S(1)}, u32[]{:S(2)}, u32[]{:S(2)}) collective-permute-start(bf16[24,7168]{1,0:T(8,128)(2,1)S(1)} %get-tuple-element.95), channel_id=1, source_target_pairs={{0,4},{1,5},{2,6},{3,7},{4,0},{5,1},{6,2},{7,3},{8,12},{9,13},{10,... | collective-permute-start | bytes 1032200 | tf_op jit(solution)/shard_map/ppermute | solution.py:283
  169.5 16.6 %collective-permute-start.30 = (bf16[24,7168]{1,0:T(8,128)(2,1)S(1)}, bf16[24,7168]{1,0:T(8,128)(2,1)S(1)}, u32[]{:S(2)}, u32[]{:S(2)}) collective-permute-start(bf16[24,7168]{1,0:T(8,128)(2,1)S(1)} %get-tuple-element.94), channel_id=1, source_target_pairs={{0,2},{1,3},{2,4},{3,5},{4,6},{5,7},{6,0},{7,1},{8,10},{9,11},{10,... | collective-permute-start | bytes 1032200 | tf_op jit(solution)/shard_map/ppermute | solution.py:283
  171.6 15.5 %collective-permute-start.29 = (bf16[24,7168]{1,0:T(8,128)(2,1)S(1)}, bf16[24,7168]{1,0:T(8,128)(2,1)S(1)}, u32[]{:S(2)}, u32[]{:S(2)}) collective-permute-start(bf16[24,7168]{1,0:T(8,128)(2,1)S(1)} %get-tuple-element.93), channel_id=1, source_target_pairs={{0,6},{1,7},{2,0},{3,1},{4,2},{5,3},{6,4},{7,5},{8,14},{9,15},{10,... | collective-permute-start | bytes 1032200 | tf_op jit(solution)/shard_map/ppermute | solution.py:283
  181.0 9.8 %collective-permute-start.26 = (bf16[24,7168]{1,0:T(8,128)(2,1)}, bf16[24,7168]{1,0:T(8,128)(2,1)S(1)}, u32[]{:S(2)}, u32[]{:S(2)}) collective-permute-start(bf16[24,7168]{1,0:T(8,128)(2,1)} %add_convert_fusion.1), channel_id=1, source_target_pairs={{0,112},{16,0},{32,16},{48,32},{64,48},{80,64},{96,80},{112,96},{1... | collective-permute-start | bytes 1032200 | tf_op jit(solution)/shard_map/ppermute | solution.py:283
  187.3 12.5 %collective-permute-start.32 = (bf16[24,7168]{1,0:T(8,128)(2,1)S(1)}, bf16[24,7168]{1,0:T(8,128)(2,1)S(1)}, u32[]{:S(2)}, u32[]{:S(2)}) collective-permute-start(bf16[24,7168]{1,0:T(8,128)(2,1)S(1)} %add_convert_fusion), channel_id=1, source_target_pairs={{0,120},{1,121},{2,122},{3,123},{4,124},{5,125},{6,126},{7,127},{8... | collective-permute-start | bytes 1032200 | tf_op jit(solution)/shard_map/ppermute | solution.py:283
  (25 other events, 531.1 us)

commit v2 on v1

--- a/solution.py
+++ b/solution.py
@@ -8,7 +8,8 @@
 from jax.sharding import PartitionSpec as P
 
 CAP = 24
-BLOCK = 1024
+BLOCK = 3584
+PICK_BLOCK = 1792
 LIMIT = 48 * 1024 * 1024
 F32 = jnp.float32
 BF16 = jnp.bfloat16
@@ -84,14 +85,14 @@
 def pick_rows(plane, routes, weight, saved, grad):
     tokens, depth = saved.shape
     whole = pl.BlockSpec(routes.shape, lambda k: (0, 0))
-    tall = pl.BlockSpec((tokens, BLOCK), lambda k: (0, k))
-    short = pl.BlockSpec((2 * CAP, BLOCK), lambda k: (0, k))
-    half = pl.BlockSpec((tokens // 2, BLOCK), lambda k: (0, k))
+    tall = pl.BlockSpec((tokens, PICK_BLOCK), lambda k: (0, k))
+    short = pl.BlockSpec((2 * CAP, PICK_BLOCK), lambda k: (0, k))
+    half = pl.BlockSpec((tokens // 2, PICK_BLOCK), lambda k: (0, k))
     rows = jax.ShapeDtypeStruct((2 * CAP, depth), BF16)
     halves = jax.ShapeDtypeStruct((tokens // 2, depth), BF16)
     return pl.pallas_call(
         pick_body,
-        grid=(depth // BLOCK,),
+        grid=(depth // PICK_BLOCK,),
         in_specs=[pl.BlockSpec(memory_space=pltpu.SMEM), whole, whole, tall, tall],
         out_specs=[short, short, half, half],
         out_shape=[rows, rows, halves, halves],
@@ -114,11 +115,21 @@
 def experts_body(steps, *refs):
     arrivals, (gate, up, down) = refs[:8], refs[8:11]
     mine, sibling, sibling_2, hidden_t = refs[11:15]
-    gates, ups, pre_gate, pre_up, from_down, grad_gate, grad_up = refs[15:]
+    gates, ups, pre_gate, pre_up, from_down, grad_gate, grad_up, arrived = refs[15:]
     step = pl.program_id(0)
 
+    def fetch(i):
+        rows = pl.ds(i * BLOCK, BLOCK)
+        return (
+            pltpu.make_async_copy(gate.at[rows], gates.at[i], arrived.at[0, i]),
+            pltpu.make_async_copy(up.at[rows], ups.at[i], arrived.at[1, i]),
+        )
+
     @pl.when(step == 0)
     def _():
+        for i in range(steps):
+            for copy in fetch(i):
+                copy.start()
         pre_gate[...] = jnp.zeros_like(pre_gate)
         pre_up[...] = jnp.zeros_like(pre_up)
         from_down[...] = jnp.zeros_like(from_down)
@@ -127,10 +138,10 @@
     def _():
         rows = stacked(arrivals, 0)
         scaled = stacked(arrivals, CAP)
-        gates[step] = gate[...]
-        ups[step] = up[...]
-        pre_gate[...] += jnp.dot(rows, gate[...], preferred_element_type=F32)
-        pre_up[...] += jnp.dot(rows, up[...], preferred_element_type=F32)
+        for copy in fetch(step):
+            copy.wait()
+        pre_gate[...] += jnp.dot(rows, gates[step], preferred_element_type=F32)
+        pre_up[...] += jnp.dot(rows, ups[step], preferred_element_type=F32)
         from_down[...] += contract_last(scaled, down[...])
 
     @pl.when(step == steps)
@@ -173,13 +184,14 @@
         functools.partial(experts_body, steps),
         grid=(2 * steps,),
         in_specs=[pl.BlockSpec((2 * CAP, BLOCK), lambda k: (0, block(k)))] * 8
-        + [pl.BlockSpec((BLOCK, width), lambda k: (block(k), 0))] * 2
+        + [pl.BlockSpec(memory_space=pl.ANY)] * 2
         + [pl.BlockSpec((width, BLOCK), lambda k: (0, block(k)))],
         out_specs=[out, half, half, pl.BlockSpec((width, count), lambda k: (0, 0))],
         out_shape=[sums, halves, halves, jax.ShapeDtypeStruct((width, count), BF16)],
         scratch_shapes=[pltpu.VMEM((steps, BLOCK, width), BF16)] * 2
         + [pltpu.VMEM((count, width), F32)] * 3
-        + [pltpu.VMEM((count, width), BF16)] * 2,
+        + [pltpu.VMEM((count, width), BF16)] * 2
+        + [pltpu.SemaphoreType.DMA((2, steps))],
         compiler_params=params(),
         cost_estimate=cost(10 * count * depth * width, 2 * depth * (3 * width + 3 * count)),
         name="experts",
@@ -297,14 +309,15 @@
     )
     across = go(after(other, behind_routes), ACROSS)
     direct = go(second, ODD_BEHIND, "pipe")
+    away = go(second, AWAY_FIRST, "pipe")
     near = [own] + [go(own, along_x(by)) for by in OFFSETS]
-    mirror = [go(after(mirror_grad[0], across, near[1], near[2]), MIRROR, "pipe")]
-    near = [near[0]] + [after(part, across, direct) for part in near[1:]]
-    away = go(after(second, across), AWAY_FIRST, "pipe")
+    mirror = after(mirror_grad[0], across, near[1], near[2])
+    mirror = [go(mirror, MIRROR, "pipe")]
+    near = [near[0]] + [after(part, across) for part in near[1:3]] + [after(near[3], across, direct, away)]
     near = near + [go(part, SIBLING) for part in near]
     far = [after(across, *near[4:])]
     far = far + [go(far[0], along_x(by)) for by in OFFSETS]
-    near[0] = after(near[0], *near[4:], away)
+    near[0] = after(near[0], *near[4:])
     near_mine, near_sibling, near_sibling_2, near_hidden = experts(near, *weights)
     far = [after(part, near_hidden) for part in far]
     near_sibling = after(near_sibling, *far)
@@ -312,20 +325,20 @@
     near_parts = split_sum(near_mine, go(near_sibling, SIBLING), go(near_sibling_2, SIBLING))
     far = far + [go(part, SIBLING) for part in far]
     far[0] = after(far[0], near_parts, mirror[0])
-    away = go(after(away, *far[4:]), AWAY_LAST, "pipe")
+    away = go(away, AWAY_LAST, "pipe")
     near_back = [go(after(part, *far[4:]), along_x(-by)) for part, by in zip(near_parts[1:], OFFSETS)]
     far_mine, far_sibling, far_sibling_2, far_hidden = experts(far, *weights)
     near_back[0] = after(near_back[0], far_hidden)
     near_total = add_up(near_parts[0], near_back)
-    first = go(after(first, near_parts), BEHIND, "pipe")
+    first = go(after(first, *near[4:]), BEHIND, "pipe")
     far_sibling = after(far_sibling, near_total)
     far_sibling_2 = after(far_sibling_2, far_sibling)
     far_mine = after(far_mine, near_total)
     far_parts = split_sum(far_mine, go(far_sibling, SIBLING), go(far_sibling_2, SIBLING))
     far_back = [go(part, along_x(-by)) for part, by in zip(far_parts[1:], OFFSETS)]
-    mirror[0] = after(mirror[0], far_hidden)
+    mirror[0] = after(mirror[0], far_hidden, away)
     down_grad = down_grads(near + far, near_hidden, far_hidden, mirror)
-    far_total = add_up(after(far_parts[0], down_grad, away, first), far_back)
+    far_total = add_up(after(far_parts[0], down_grad, first), far_back)
     near_back = go(near_total, BEHIND, "pipe")
     far_back = go(far_total, pairs, ("pipe", "expert"))
     back = combine(odd, plane, behind_routes, first, direct, away, near_back, far_back)

time: 209 us -> 185 us (0.89)
  Pallas kernels: 51.1 us -> 38.3 us
  waiting for transfers between devices: 115 us -> 107 us
    ppermute x33, waiting for transfers between devices: 115 us -> 107 us  [go(): return lax.ppermute(rows, axis, perm)]
    pallas_call x2, Pallas kernels: 27.6 us -> 22.6 us  [experts(): pl.pallas_call(functools.partial(experts_body, steps), grid=(2 * steps,),...]
    pallas_call x1, Pallas kernels: 9.37 us -> 6.34 us  [down_grads(): pl.pallas_call(down_body, grid=(depth // BLOCK,), in_specs=[pl.BlockSpec(...]
    pallas_call x1, Pallas kernels: 6.65 us -> 3.65 us  [combine(): pl.pallas_call(combine_body, grid=(depth // BLOCK,), in_specs=[pl.BlockSp...]
  transfers between devices with their start and end apart: 33 -> 33, of which waited for: 19 -> 21; matrix products, arithmetic and copies ran while one was open for 1% -> 0% of each run, Pallas kernels for 22% -> 19%
where the time goes in v2:
time: 185 us; the launch traced here: 183 us
  waiting for transfers between devices  107 us (58%)
  Pallas kernels  38.3 us (21%)
  starting transfers between devices  32.4 us (18%)
  local copies, waits for them, and re-layouts  4.12 us (2%)
    ppermute x33, waiting for transfers between devices, go(): return lax.ppermute(rows, axis, perm)  107 us
    ppermute x33, starting transfers between devices, go(): return lax.ppermute(rows, axis, perm)  32.4 us
    pallas_call x2, Pallas kernels, experts(): pl.pallas_call(functools.partial(experts_body, steps), grid=(2 * steps,),...  22.6 us
    pallas_call x1, Pallas kernels, down_grads(): pl.pallas_call(down_body, grid=(depth // BLOCK,), in_specs=[pl.BlockSpec(...  6.34 us
    pallas_call x1, Pallas kernels, pick_rows(): pl.pallas_call(pick_body, grid=(depth // PICK_BLOCK,), in_specs=[pl.Block...  4.32 us
    unnamed x34, local copies, waits for them, and re-layouts  4.12 us
  transfers between devices with their start and end apart: 33, of which 21 were waited for; matrix products, arithmetic and copies ran while one was open for 0% of the time, Pallas kernels for 19%

profile of v2, /device:TPU:6, one launch (start us, length us, event | category | flops | bytes accessed | tf_op | source)
XLA Modules:
  0.0 182.9 jit_solution(1015704853277248333)
XLA Ops:
  0.6 5.1 %collective-permute-start = (s32[8,192]{1,0:T(8,128)}, s32[8,192]{1,0:T(8,128)S(1)}, u32[]{:S(2)}, u32[]{:S(2)}) collective-permute-start(s32[8,192]{1,0:T(8,128)} %bitcast.17), channel_id=1, source_target_pairs={{0,112},{16,0},{32,16},{48,32},{64,48},{80,64},{96,80},{112,96},{1... | collective-permute-start | bytes 18440 | tf_op jit(solution)/shard_map/ppermute | solution.py:295
  7.2 4.3 %pick_rows.1 = (bf16[48,7168]{1,0:T(8,128)(2,1)S(1)}, bf16[48,7168]{1,0:T(8,128)(2,1)S(1)}, bf16[96,7168]{1,0:T(8,128)(2,1)S(1)}, bf16[96,7168]{1,0:T(8,128)(2,1)S(1)}) custom-call(s32[1]{0:T(128)} %bitcast.1.plane, s32[8,192]{1,0:T(8,128)S(1)} %bitcast.18, f32[8,192]{1,0:T(8,128)S(1)} %bitcast.16, bf16[192,7168]{1,0:T(8,128)(2,1)} %bitcast.27, ...), custom_call_target="tpu_custom_call" | custom-call | flops 264241152 | bytes 13762560 | tf_op jit(solution)/shard_map/pick_rows/pallas_call | solution.py:93
  13.6 2.9 %collective-permute-start.3 = (bf16[48,7168]{1,0:T(8,128)(2,1)S(1)}, bf16[48,7168]{1,0:T(8,128)(2,1)S(1)}, u32[]{:S(2)}, u32[]{:S(2)}) collective-permute-start(bf16[48,7168]{1,0:T(8,128)(2,1)S(1)} %get-tuple-element.51), channel_id=1, source_target_pairs={{0,8},{1,9},{2,10},{3,11},{4,12},{5,13},{6,14},{7,15},{8,0},{9,1},... | collective-permute-start | bytes 2064392 | tf_op jit(solution)/shard_map/ppermute | solution.py:295
  17.8 1.9 %collective-permute-start.9 = (bf16[96,7168]{1,0:T(8,128)(2,1)S(1)}, bf16[96,7168]{1,0:T(8,128)(2,1)}, u32[]{:S(2)}, u32[]{:S(2)}) collective-permute-start(bf16[96,7168]{1,0:T(8,128)(2,1)S(1)} %get-tuple-element.54), channel_id=1, source_target_pairs={{0,32},{32,0},{64,96},{96,64},{1,33},{33,1},{65,97},{97,65},{2,34}... | collective-permute-start | bytes 4128776 | tf_op jit(solution)/shard_map/ppermute | solution.py:295
  19.7 8.7 %collective-permute-done.2.refs_1_ = bf16[48,7168]{1,0:T(8,128)(2,1)S(1)} collective-permute-done((bf16[48,7168]{1,0:T(8,128)(2,1)S(1)}, bf16[48,7168]{1,0:T(8,128)(2,1)S(1)}, u32[]{:S(2)}, u32[]{:S(2)}) %collective-permute-start.2) | collective-permute-done | bytes 688160 | tf_op jit(solution)/shard_map/ppermute | solution.py:295
  29.9 1.6 collective-permute-done.3.refs_0_.refs_8_
  33.3 15.2 %collective-permute-done.7.refs_3_ = bf16[48,7168]{1,0:T(8,128)(2,1)S(1)} collective-permute-done((bf16[48,7168]{1,0:T(8,128)(2,1)S(1)}, bf16[48,7168]{1,0:T(8,128)(2,1)S(1)}, u32[]{:S(2)}, u32[]{:S(2)}) %collective-permute-start.7) | collective-permute-done | bytes 688160 | tf_op jit(solution)/shard_map/ppermute | solution.py:295
  49.2 20.4 %collective-permute-done.9 = bf16[96,7168]{1,0:T(8,128)(2,1)} collective-permute-done((bf16[96,7168]{1,0:T(8,128)(2,1)S(1)}, bf16[96,7168]{1,0:T(8,128)(2,1)}, u32[]{:S(2)}, u32[]{:S(2)}) %collective-permute-start.9) | collective-permute-done | bytes 1376288 | tf_op jit(solution)/shard_map/ppermute | solution.py:295
  69.6 2.1 %collective-permute-done.10.refs_7_ = bf16[48,7168]{1,0:T(8,128)(2,1)S(1)} collective-permute-done((bf16[48,7168]{1,0:T(8,128)(2,1)S(1)}, bf16[48,7168]{1,0:T(8,128)(2,1)S(1)}, u32[]{:S(2)}, u32[]{:S(2)}) %collective-permute-start.10) | collective-permute-done | bytes 688160 | tf_op jit(solution)/shard_map/ppermute | solution.py:295
  71.7 1.7 collective-permute-start.13
  75.1 11.3 %experts.2 = (bf16[96,7168]{1,0:T(8,128)(2,1)}, bf16[48,7168]{1,0:T(8,128)(2,1)S(1)}, bf16[48,7168]{1,0:T(8,128)(2,1)S(1)}, bf16[256,192]{1,0:T(8,128)(2,1)S(1)}) custom-call(bf16[48,7168]{1,0:T(8,128)(2,1)S(1)} %get-tuple-element.57.refs_0_, bf16[48,7168]{1,0:T(8,128)(2,1)S(1)} %collective-permute-done.2.refs_1_, ...), custom_call_target="tpu_custom_call" | custom-call | flops 3523215360 | bytes 19267584 | tf_op jit(solution)/shard_map/experts/pallas_call | solution.py:183
  86.5 3.5 %collective-permute-done.13.refs_1_.refs_9_ = bf16[48,7168]{1,0:T(8,128)(2,1)S(1)} collective-permute-done((bf16[48,7168]{1,0:T(8,128)(2,1)S(1)}, bf16[48,7168]{1,0:T(8,128)(2,1)S(1)}, u32[]{:S(2)}, u32[]{:S(2)}) %collective-permute-start.13) | collective-permute-done | bytes 688160 | tf_op jit(solution)/shard_map/ppermute | solution.py:295
  90.0 16.6 %collective-permute-done.14.refs_2_.refs_10_ = bf16[48,7168]{1,0:T(8,128)(2,1)S(1)} collective-permute-done((bf16[48,7168]{1,0:T(8,128)(2,1)S(1)}, bf16[48,7168]{1,0:T(8,128)(2,1)S(1)}, u32[]{:S(2)}, u32[]{:S(2)}) %collective-permute-start.14) | collective-permute-done | bytes 688160 | tf_op jit(solution)/shard_map/ppermute | solution.py:295
  114.8 2.6 %collective-permute-start.24 = (bf16[24,7168]{1,0:T(8,128)(2,1)S(1)}, bf16[24,7168]{1,0:T(8,128)(2,1)S(1)}, u32[]{:S(2)}, u32[]{:S(2)}) collective-permute-start(bf16[24,7168]{1,0:T(8,128)(2,1)S(1)} %get-tuple-element.78), channel_id=1, source_target_pairs={{0,2},{1,3},{2,4},{3,5},{4,6},{5,7},{6,0},{7,1},{8,10},{9,11},{10,... | collective-permute-start | bytes 1032200 | tf_op jit(solution)/shard_map/ppermute | solution.py:295
  117.5 2.4 %collective-permute-start.12 = (bf16[96,7168]{1,0:T(8,128)(2,1)}, bf16[96,7168]{1,0:T(8,128)(2,1)}, u32[]{:S(2)}, u32[]{:S(2)}) collective-permute-start(bf16[96,7168]{1,0:T(8,128)(2,1)} %collective-permute-done.9), channel_id=1, source_target_pairs={{32,112},{96,48},{0,16},{64,80},{33,113},{97,49},{1,17},{65,81},{3... | collective-permute-start | bytes 4128776 | tf_op jit(solution)/shard_map/ppermute | solution.py:295
  119.9 10.9 %collective-permute-done.23.refs_18_ = bf16[256,7168]{1,0:T(8,128)(2,1)} collective-permute-done((bf16[256,7168]{1,0:T(8,128)(2,1)}, bf16[256,7168]{1,0:T(8,128)(2,1)}, u32[]{:S(2)}, u32[]{:S(2)}) %collective-permute-start.23) | collective-permute-done | bytes 3670048 | tf_op jit(solution)/shard_map/ppermute | solution.py:295
  130.8 11.3 %experts.3 = (bf16[96,7168]{1,0:T(8,128)(2,1)}, bf16[48,7168]{1,0:T(8,128)(2,1)S(1)}, bf16[48,7168]{1,0:T(8,128)(2,1)S(1)}, bf16[256,192]{1,0:T(8,128)(2,1)S(1)}) custom-call(bf16[48,7168]{1,0:T(8,128)(2,1)S(1)} %collective-permute-done.3.refs_0_.refs_8_, bf16[48,7168]{1,0:T(8,128)(2,1)S(1)} %collective-permute-done.13.refs_1_.refs_9_, ...), custom_call_target="tpu_custom_call" | custom-call | flops 3523215360 | bytes 19267584 | tf_op jit(solution)/shard_map/experts/pallas_call | solution.py:183
  143.0 1.6 collective-permute-done.27.first
  149.1 2.1 %collective-permute-start.30 = (bf16[24,7168]{1,0:T(8,128)(2,1)S(1)}, bf16[24,7168]{1,0:T(8,128)(2,1)S(1)}, u32[]{:S(2)}, u32[]{:S(2)}) collective-permute-start(bf16[24,7168]{1,0:T(8,128)(2,1)S(1)} %get-tuple-element.90), channel_id=1, source_target_pairs={{0,2},{1,3},{2,4},{3,5},{4,6},{5,7},{6,0},{7,1},{8,10},{9,11},{10,... | collective-permute-start | bytes 1032200 | tf_op jit(solution)/shard_map/ppermute | solution.py:295
  151.2 1.6 collective-permute-start.26
  152.8 6.3 %down_grads.1 = bf16[256,7168]{1,0:T(8,128)(2,1)} custom-call(bf16[48,7168]{1,0:T(8,128)(2,1)S(1)} %get-tuple-element.57.refs_0_, bf16[48,7168]{1,0:T(8,128)(2,1)S(1)} %collective-permute-done.2.refs_1_, bf16[48,7168]{1,0:T(8,128)(2,1)S(1)} %collective-permute-done.5.refs_2_, bf16[48,7168]{1,0:T(8,128)(2,1)S(1)} %collective-permute-done.7.refs_3_, ...), custom_call_target="tpu_custom_call" | custom-call | flops 1409286144 | bytes 18350080 | tf_op jit(solution)/shard_map/down_grads/pallas_call | solution.py:237
  159.1 5.1 %collective-permute-done.11.first = bf16[96,7168]{1,0:T(8,128)(2,1)} collective-permute-done((bf16[96,7168]{1,0:T(8,128)(2,1)}, bf16[96,7168]{1,0:T(8,128)(2,1)}, u32[]{:S(2)}, u32[]{:S(2)}) %collective-permute-start.11) | collective-permute-done | bytes 1376288 | tf_op jit(solution)/shard_map/ppermute | solution.py:295
  168.5 10.8 %collective-permute-done.32.other = bf16[24,7168]{1,0:T(8,128)(2,1)S(1)} collective-permute-done((bf16[24,7168]{1,0:T(8,128)(2,1)S(1)}, bf16[24,7168]{1,0:T(8,128)(2,1)S(1)}, u32[]{:S(2)}, u32[]{:S(2)}) %collective-permute-start.32) | collective-permute-done | bytes 344096 | tf_op jit(solution)/shard_map/ppermute | solution.py:295
  179.3 3.6 %combine.1 = bf16[192,7168]{1,0:T(8,128)(2,1)} custom-call(s32[1]{0:T(128)} %bitcast.odd, s32[1]{0:T(128)} %bitcast.1.plane, s32[8,192]{1,0:T(8,128)S(1)} %collective-permute-done.routes, bf16[96,7168]{1,0:T(8,128)(2,1)} %collective-permute-done.11.first, bf16[96,7168]{1,0:T(8,128)(2,1)S(1)} %collective-permute-done.8.direct, ...), custom_call_target="tpu_custom_call" | custom-call | flops 132120576 | bytes 8257536 | tf_op jit(solution)/shard_map/combine/pallas_call | solution.py:268
  (85 shorter events, 28.3 us)
Async XLA Ops:
  0.6 12.9 %collective-permute-start = (s32[8,192]{1,0:T(8,128)}, s32[8,192]{1,0:T(8,128)S(1)}, u32[]{:S(2)}, u32[]{:S(2)}) collective-permute-start(s32[8,192]{1,0:T(8,128)} %bitcast.17), channel_id=1, source_target_pairs={{0,112},{16,0},{32,16},{48,32},{64,48},{80,64},{96,80},{112,96},{1... | collective-permute-start | bytes 18440 | tf_op jit(solution)/shard_map/ppermute | solution.py:295
  11.5 17.0 %collective-permute-start.2 = (bf16[48,7168]{1,0:T(8,128)(2,1)S(1)}, bf16[48,7168]{1,0:T(8,128)(2,1)S(1)}, u32[]{:S(2)}, u32[]{:S(2)}) collective-permute-start(bf16[48,7168]{1,0:T(8,128)(2,1)S(1)} %get-tuple-element.57.refs_0_), channel_id=1, source_target_pairs={{0,2},{1,3},{2,4},{3,5},{4,6},{5,7},{6,0},{7,1},{8,10},{9,11},{10,... | collective-permute-start | bytes 2064392 | tf_op jit(solution)/shard_map/ppermute | solution.py:295
  12.0 17.8 %collective-permute-start.5 = (bf16[48,7168]{1,0:T(8,128)(2,1)S(1)}, bf16[48,7168]{1,0:T(8,128)(2,1)S(1)}, u32[]{:S(2)}, u32[]{:S(2)}) collective-permute-start(bf16[48,7168]{1,0:T(8,128)(2,1)S(1)} %get-tuple-element.57.refs_0_), channel_id=1, source_target_pairs={{0,6},{1,7},{2,0},{3,1},{4,2},{5,3},{6,4},{7,5},{8,14},{9,15},{10,... | collective-permute-start | bytes 2064392 | tf_op jit(solution)/shard_map/ppermute | solution.py:295
  13.6 17.8 %collective-permute-start.3 = (bf16[48,7168]{1,0:T(8,128)(2,1)S(1)}, bf16[48,7168]{1,0:T(8,128)(2,1)S(1)}, u32[]{:S(2)}, u32[]{:S(2)}) collective-permute-start(bf16[48,7168]{1,0:T(8,128)(2,1)S(1)} %get-tuple-element.51), channel_id=1, source_target_pairs={{0,8},{1,9},{2,10},{3,11},{4,12},{5,13},{6,14},{7,15},{8,0},{9,1},... | collective-permute-start | bytes 2064392 | tf_op jit(solution)/shard_map/ppermute | solution.py:295
  16.5 32.7 %collective-permute-start.8 = (bf16[96,7168]{1,0:T(8,128)(2,1)S(1)}, bf16[96,7168]{1,0:T(8,128)(2,1)S(1)}, u32[]{:S(2)}, u32[]{:S(2)}) collective-permute-start(bf16[96,7168]{1,0:T(8,128)(2,1)S(1)} %get-tuple-element.54), channel_id=1, source_target_pairs={{16,0},{48,32},{80,64},{112,96},{17,1},{49,33},{81,65},{113,97},{1... | collective-permute-start | bytes 4128776 | tf_op jit(solution)/shard_map/ppermute | solution.py:295
  17.8 51.8 %collective-permute-start.9 = (bf16[96,7168]{1,0:T(8,128)(2,1)S(1)}, bf16[96,7168]{1,0:T(8,128)(2,1)}, u32[]{:S(2)}, u32[]{:S(2)}) collective-permute-start(bf16[96,7168]{1,0:T(8,128)(2,1)S(1)} %get-tuple-element.54), channel_id=1, source_target_pairs={{0,32},{32,0},{64,96},{96,64},{1,33},{33,1},{65,97},{97,65},{2,34}... | collective-permute-start | bytes 4128776 | tf_op jit(solution)/shard_map/ppermute | solution.py:295
  31.4 99.3 %collective-permute-start.23 = (bf16[256,7168]{1,0:T(8,128)(2,1)}, bf16[256,7168]{1,0:T(8,128)(2,1)}, u32[]{:S(2)}, u32[]{:S(2)}) collective-permute-start(bf16[256,7168]{1,0:T(8,128)(2,1)} %bitcast.29), channel_id=1, source_target_pairs={{0,112},{16,96},{32,80},{48,64},{64,48},{80,32},{96,16},{112,0},{1... | collective-permute-start | bytes 11010056 | tf_op jit(solution)/shard_map/ppermute | solution.py:295
  31.8 16.6 %collective-permute-start.7 = (bf16[48,7168]{1,0:T(8,128)(2,1)S(1)}, bf16[48,7168]{1,0:T(8,128)(2,1)S(1)}, u32[]{:S(2)}, u32[]{:S(2)}) collective-permute-start(bf16[48,7168]{1,0:T(8,128)(2,1)S(1)} %get-tuple-element.57.refs_0_), channel_id=1, source_target_pairs={{0,4},{1,5},{2,6},{3,7},{4,0},{5,1},{6,2},{7,3},{8,12},{9,13},{10,... | collective-permute-start | bytes 2064392 | tf_op jit(solution)/shard_map/ppermute | solution.py:295
  33.2 36.3 %collective-permute-start.1 = (bf16[48,7168]{1,0:T(8,128)(2,1)S(1)}, bf16[48,7168]{1,0:T(8,128)(2,1)S(1)}, u32[]{:S(2)}, u32[]{:S(2)}) collective-permute-start(bf16[48,7168]{1,0:T(8,128)(2,1)S(1)} %get-tuple-element.57.refs_0_), channel_id=1, source_target_pairs={{0,1},{1,0},{2,3},{3,2},{4,5},{5,4},{6,7},{7,6},{8,9},{9,8},{10,11... | collective-permute-start | bytes 2064392 | tf_op jit(solution)/shard_map/ppermute | solution.py:295
  48.5 21.1 %collective-permute-start.4 = (bf16[48,7168]{1,0:T(8,128)(2,1)S(1)}, bf16[48,7168]{1,0:T(8,128)(2,1)S(1)}, u32[]{:S(2)}, u32[]{:S(2)}) collective-permute-start(bf16[48,7168]{1,0:T(8,128)(2,1)S(1)} %collective-permute-done.2.refs_1_), channel_id=1, source_target_pairs={{0,1},{1,0},{2,3},{3,2},{4,5},{5,4},{6,7},{7,6},{8,9},{9,8},{10,11... | collective-permute-start | bytes 2064392 | tf_op jit(solution)/shard_map/ppermute | solution.py:295
  49.2 20.4 %collective-permute-start.6 = (bf16[48,7168]{1,0:T(8,128)(2,1)S(1)}, bf16[48,7168]{1,0:T(8,128)(2,1)S(1)}, u32[]{:S(2)}, u32[]{:S(2)}) collective-permute-start(bf16[48,7168]{1,0:T(8,128)(2,1)S(1)} %collective-permute-done.5.refs_2_), channel_id=1, source_target_pairs={{0,1},{1,0},{2,3},{3,2},{4,5},{5,4},{6,7},{7,6},{8,9},{9,8},{10,11... | collective-permute-start | bytes 2064392 | tf_op jit(solution)/shard_map/ppermute | solution.py:295
  71.7 18.3 %collective-permute-start.13 = (bf16[48,7168]{1,0:T(8,128)(2,1)S(1)}, bf16[48,7168]{1,0:T(8,128)(2,1)S(1)}, u32[]{:S(2)}, u32[]{:S(2)}) collective-permute-start(bf16[48,7168]{1,0:T(8,128)(2,1)S(1)} %collective-permute-done.3.refs_0_.refs_8_), channel_id=1, source_target_pairs={{0,2},{1,3},{2,4},{3,5},{4,6},{5,7},{6,0},{7,1},{8,10},{9,11},{10,... | collective-permute-start | bytes 2064392 | tf_op jit(solution)/shard_map/ppermute | solution.py:295
  73.4 33.2 %collective-permute-start.14 = (bf16[48,7168]{1,0:T(8,128)(2,1)S(1)}, bf16[48,7168]{1,0:T(8,128)(2,1)S(1)}, u32[]{:S(2)}, u32[]{:S(2)}) collective-permute-start(bf16[48,7168]{1,0:T(8,128)(2,1)S(1)} %collective-permute-done.3.refs_0_.refs_8_), channel_id=1, source_target_pairs={{0,6},{1,7},{2,0},{3,1},{4,2},{5,3},{6,4},{7,5},{8,14},{9,15},{10,... | collective-permute-start | bytes 2064392 | tf_op jit(solution)/shard_map/ppermute | solution.py:295
  73.7 32.8 %collective-permute-start.15 = (bf16[48,7168]{1,0:T(8,128)(2,1)S(1)}, bf16[48,7168]{1,0:T(8,128)(2,1)S(1)}, u32[]{:S(2)}, u32[]{:S(2)}) collective-permute-start(bf16[48,7168]{1,0:T(8,128)(2,1)S(1)} %collective-permute-done.3.refs_0_.refs_8_), channel_id=1, source_target_pairs={{0,4},{1,5},{2,6},{3,7},{4,0},{5,1},{6,2},{7,3},{8,12},{9,13},{10,... | collective-permute-start | bytes 2064392 | tf_op jit(solution)/shard_map/ppermute | solution.py:295
  113.7 28.5 %collective-permute-start.25 = (bf16[24,7168]{1,0:T(8,128)(2,1)S(1)}, bf16[24,7168]{1,0:T(8,128)(2,1)S(1)}, u32[]{:S(2)}, u32[]{:S(2)}) collective-permute-start(bf16[24,7168]{1,0:T(8,128)(2,1)S(1)} %get-tuple-element.79), channel_id=1, source_target_pairs={{0,4},{1,5},{2,6},{3,7},{4,0},{5,1},{6,2},{7,3},{8,12},{9,13},{10,... | collective-permute-start | bytes 1032200 | tf_op jit(solution)/shard_map/ppermute | solution.py:295
  114.2 27.9 %collective-permute-start.22 = (bf16[24,7168]{1,0:T(8,128)(2,1)S(1)}, bf16[24,7168]{1,0:T(8,128)(2,1)S(1)}, u32[]{:S(2)}, u32[]{:S(2)}) collective-permute-start(bf16[24,7168]{1,0:T(8,128)(2,1)S(1)} %get-tuple-element.71), channel_id=1, source_target_pairs={{0,6},{1,7},{2,0},{3,1},{4,2},{5,3},{6,4},{7,5},{8,14},{9,15},{10,... | collective-permute-start | bytes 1032200 | tf_op jit(solution)/shard_map/ppermute | solution.py:295
  114.8 27.3 %collective-permute-start.24 = (bf16[24,7168]{1,0:T(8,128)(2,1)S(1)}, bf16[24,7168]{1,0:T(8,128)(2,1)S(1)}, u32[]{:S(2)}, u32[]{:S(2)}) collective-permute-start(bf16[24,7168]{1,0:T(8,128)(2,1)S(1)} %get-tuple-element.78), channel_id=1, source_target_pairs={{0,2},{1,3},{2,4},{3,5},{4,6},{5,7},{6,0},{7,1},{8,10},{9,11},{10,... | collective-permute-start | bytes 1032200 | tf_op jit(solution)/shard_map/ppermute | solution.py:295
  117.5 33.7 %collective-permute-start.12 = (bf16[96,7168]{1,0:T(8,128)(2,1)}, bf16[96,7168]{1,0:T(8,128)(2,1)}, u32[]{:S(2)}, u32[]{:S(2)}) collective-permute-start(bf16[96,7168]{1,0:T(8,128)(2,1)} %collective-permute-done.9), channel_id=1, source_target_pairs={{32,112},{96,48},{0,16},{64,80},{33,113},{97,49},{1,17},{65,81},{3... | collective-permute-start | bytes 4128776 | tf_op jit(solution)/shard_map/ppermute | solution.py:295
  130.7 33.4 %collective-permute-start.11 = (bf16[96,7168]{1,0:T(8,128)(2,1)}, bf16[96,7168]{1,0:T(8,128)(2,1)}, u32[]{:S(2)}, u32[]{:S(2)}) collective-permute-start(bf16[96,7168]{1,0:T(8,128)(2,1)} %copy-done.14), channel_id=1, source_target_pairs={{0,112},{16,0},{32,16},{48,32},{64,48},{80,64},{96,80},{112,96},{1... | collective-permute-start | bytes 4128776 | tf_op jit(solution)/shard_map/ppermute | solution.py:295
  147.6 16.6 %collective-permute-start.31 = (bf16[24,7168]{1,0:T(8,128)(2,1)S(1)}, bf16[24,7168]{1,0:T(8,128)(2,1)S(1)}, u32[]{:S(2)}, u32[]{:S(2)}) collective-permute-start(bf16[24,7168]{1,0:T(8,128)(2,1)S(1)} %get-tuple-element.91), channel_id=1, source_target_pairs={{0,4},{1,5},{2,6},{3,7},{4,0},{5,1},{6,2},{7,3},{8,12},{9,13},{10,... | collective-permute-start | bytes 1032200 | tf_op jit(solution)/shard_map/ppermute | solution.py:295
  149.1 16.6 %collective-permute-start.30 = (bf16[24,7168]{1,0:T(8,128)(2,1)S(1)}, bf16[24,7168]{1,0:T(8,128)(2,1)S(1)}, u32[]{:S(2)}, u32[]{:S(2)}) collective-permute-start(bf16[24,7168]{1,0:T(8,128)(2,1)S(1)} %get-tuple-element.90), channel_id=1, source_target_pairs={{0,2},{1,3},{2,4},{3,5},{4,6},{5,7},{6,0},{7,1},{8,10},{9,11},{10,... | collective-permute-start | bytes 1032200 | tf_op jit(solution)/shard_map/ppermute | solution.py:295
  151.2 15.5 %collective-permute-start.29 = (bf16[24,7168]{1,0:T(8,128)(2,1)S(1)}, bf16[24,7168]{1,0:T(8,128)(2,1)S(1)}, u32[]{:S(2)}, u32[]{:S(2)}) collective-permute-start(bf16[24,7168]{1,0:T(8,128)(2,1)S(1)} %get-tuple-element.89), channel_id=1, source_target_pairs={{0,6},{1,7},{2,0},{3,1},{4,2},{5,3},{6,4},{7,5},{8,14},{9,15},{10,... | collective-permute-start | bytes 1032200 | tf_op jit(solution)/shard_map/ppermute | solution.py:295
  151.2 17.3 %collective-permute-start.26 = (bf16[24,7168]{1,0:T(8,128)(2,1)S(1)}, bf16[24,7168]{1,0:T(8,128)(2,1)S(1)}, u32[]{:S(2)}, u32[]{:S(2)}) collective-permute-start(bf16[24,7168]{1,0:T(8,128)(2,1)S(1)} %add_convert_fusion.1), channel_id=1, source_target_pairs={{0,112},{16,0},{32,16},{48,32},{64,48},{80,64},{96,80},{112,96},{1... | collective-permute-start | bytes 1032200 | tf_op jit(solution)/shard_map/ppermute | solution.py:295
  166.8 12.5 %collective-permute-start.32 = (bf16[24,7168]{1,0:T(8,128)(2,1)S(1)}, bf16[24,7168]{1,0:T(8,128)(2,1)S(1)}, u32[]{:S(2)}, u32[]{:S(2)}) collective-permute-start(bf16[24,7168]{1,0:T(8,128)(2,1)S(1)} %add_convert_fusion), channel_id=1, source_target_pairs={{0,120},{1,121},{2,122},{3,123},{4,124},{5,125},{6,126},{7,127},{8... | collective-permute-start | bytes 1032200 | tf_op jit(solution)/shard_map/ppermute | solution.py:295
  (26 other events, 446.2 us)

commit v3 on v2

--- a/solution.py
+++ b/solution.py
@@ -10,6 +10,8 @@
 CAP = 24
 BLOCK = 3584
 PICK_BLOCK = 1792
+DIRECT = 96
+TURNED = 144
 LIMIT = 48 * 1024 * 1024
 F32 = jnp.float32
 BF16 = jnp.bfloat16
@@ -19,6 +21,8 @@
 ODD_BEHIND = [(i, i - 1) for i in range(1, 8, 2)]
 AWAY_FIRST = [(0, 2), (2, 0), (4, 6), (6, 4)]
 AWAY_LAST = [(2, 7), (6, 3), (0, 1), (4, 5)]
+DOWN_Z = [(i, i // 4 * 4 + (i - 1) % 4) for i in range(8)]
+CROSS_Y = [(3, 7), (7, 3)]
 ACROSS = [(i, i ^ 8) for i in range(16)]
 SIBLING = [(i, i ^ 1) for i in range(16)]
 
@@ -55,7 +59,9 @@
     return jnp.where((count - 1.0 == slot) & (member > 0.0), 1.0, 0.0)
 
 
-def pick_body(plane, routes, weight, saved, grad, own, other, first, second, one_hot, gain):
+def pick_body(
+    plane, routes, weight, saved, grad, own, other, first, second, third, one_hot, gain
+):
     tokens = routes.shape[1]
 
     @pl.when(pl.program_id(0) == 0)
@@ -78,8 +84,9 @@
     scaled = gain[:, :1] * jnp.dot(pick, grads, preferred_element_type=F32)
     own[...] = jnp.concatenate([rows[:CAP], scaled[:CAP]], axis=0).astype(BF16)
     other[...] = jnp.concatenate([rows[CAP:], scaled[CAP:]], axis=0).astype(BF16)
-    first[...] = grads[: tokens // 2]
-    second[...] = grads[tokens // 2 :]
+    first[...] = grads[:DIRECT]
+    second[...] = grads[DIRECT:TURNED]
+    third[...] = grads[TURNED:]
 
 
 def pick_rows(plane, routes, weight, saved, grad):
@@ -87,15 +94,22 @@
     whole = pl.BlockSpec(routes.shape, lambda k: (0, 0))
     tall = pl.BlockSpec((tokens, PICK_BLOCK), lambda k: (0, k))
     short = pl.BlockSpec((2 * CAP, PICK_BLOCK), lambda k: (0, k))
-    half = pl.BlockSpec((tokens // 2, PICK_BLOCK), lambda k: (0, k))
+    direct = pl.BlockSpec((DIRECT, PICK_BLOCK), lambda k: (0, k))
+    turned = pl.BlockSpec((TURNED - DIRECT, PICK_BLOCK), lambda k: (0, k))
+    rest = pl.BlockSpec((tokens - TURNED, PICK_BLOCK), lambda k: (0, k))
     rows = jax.ShapeDtypeStruct((2 * CAP, depth), BF16)
-    halves = jax.ShapeDtypeStruct((tokens // 2, depth), BF16)
     return pl.pallas_call(
         pick_body,
         grid=(depth // PICK_BLOCK,),
         in_specs=[pl.BlockSpec(memory_space=pltpu.SMEM), whole, whole, tall, tall],
-        out_specs=[short, short, half, half],
-        out_shape=[rows, rows, halves, halves],
+        out_specs=[short, short, direct, turned, rest],
+        out_shape=[
+            rows,
+            rows,
+            jax.ShapeDtypeStruct((DIRECT, depth), BF16),
+            jax.ShapeDtypeStruct((TURNED - DIRECT, depth), BF16),
+            jax.ShapeDtypeStruct((tokens - TURNED, depth), BF16),
+        ],
         scratch_shapes=[pltpu.VMEM((2 * CAP, tokens), BF16), pltpu.VMEM((2 * CAP, 128), F32)],
         compiler_params=params(),
         cost_estimate=cost(4 * 48 * tokens * depth, 10 * tokens * depth),
@@ -248,23 +262,26 @@
     )(*arrivals, left, right, *mirror)
 
 
-def combine_body(odd, plane, routes, first, direct, away, own, other, out, place):
+def combine_body(
+    rank, plane, routes, first, turned, crossed, direct, away, own, other, out, place
+):
     @pl.when(pl.program_id(0) == 0)
     def _():
         place[...] = one_hot_rows(plane, routes).T.astype(BF16)
 
     rows = jnp.concatenate([own[...].astype(F32), other[...].astype(F32)], axis=0).astype(BF16)
     added = jnp.dot(place[...], rows, preferred_element_type=F32)
-    half = first.shape[0]
-    out[:half] = (first[...].astype(F32) + added[:half]).astype(BF16)
-    rest = jnp.where(odd[0] == 1, away[...].astype(F32), direct[...].astype(F32))
-    out[half:] = (rest + added[half:]).astype(BF16)
-
-
-def combine(odd, plane, routes, first, direct, away, own, other):
-    half, depth = first.shape
-    part = pl.BlockSpec((half, BLOCK), lambda k: (0, k))
-    rows = pl.BlockSpec((CAP, BLOCK), lambda k: (0, k))
+    last = lax.rem(rank[0], 4) == 3
+    odd = lax.rem(rank[0], 2) == 1
+    second = jnp.where(last, crossed[...].astype(F32), turned[...].astype(F32))
+    third = jnp.where(odd, away[...].astype(F32), direct[...].astype(F32))
+    out[:DIRECT] = (first[...].astype(F32) + added[:DIRECT]).astype(BF16)
+    out[DIRECT:TURNED] = (second + added[DIRECT:TURNED]).astype(BF16)
+    out[TURNED:] = (third + added[TURNED:]).astype(BF16)
+
+
+def combine(rank, plane, routes, *parts):
+    tokens, depth = routes.shape[1], parts[0].shape[1]
     return pl.pallas_call(
         combine_body,
         grid=(depth // BLOCK,),
@@ -272,19 +289,15 @@
             pl.BlockSpec(memory_space=pltpu.SMEM),
             pl.BlockSpec(memory_space=pltpu.SMEM),
             pl.BlockSpec(routes.shape, lambda k: (0, 0)),
-            part,
-            part,
-            part,
-            rows,
-            rows,
-        ],
-        out_specs=pl.BlockSpec((2 * half, BLOCK), lambda k: (0, k)),
-        out_shape=jax.ShapeDtypeStruct((2 * half, depth), BF16),
-        scratch_shapes=[pltpu.VMEM((2 * half, 2 * CAP), BF16)],
-        compiler_params=params(),
-        cost_estimate=cost(4 * half * 48 * depth, 12 * half * depth),
+        ]
+        + [pl.BlockSpec((part.shape[0], BLOCK), lambda k: (0, k)) for part in parts],
+        out_specs=pl.BlockSpec((tokens, BLOCK), lambda k: (0, k)),
+        out_shape=jax.ShapeDtypeStruct((tokens, depth), BF16),
+        scratch_shapes=[pltpu.VMEM((tokens, 2 * CAP), BF16)],
+        compiler_params=params(),
+        cost_estimate=cost(2 * tokens * 48 * depth, 6 * tokens * depth),
         name="combine",
-    )(odd, plane, routes, first, direct, away, own, other)
+    )(rank, plane, routes, *parts)
 
 
 def after(value, *others):
@@ -299,28 +312,29 @@
     saved_input, grad_output, routes, route_weight, gate_weight, up_weight, down_weight, mirror_grad
 ):
     plane = (lax.axis_index("expert") // 8).astype(jnp.int32).reshape(1)
-    odd = (lax.axis_index("pipe") % 2).astype(jnp.int32).reshape(1)
+    rank = lax.axis_index("pipe").astype(jnp.int32).reshape(1)
     weights = (gate_weight[0], up_weight[0], down_weight[0])
     pairs = [(s * 16 + e, ((s - 1) % 8) * 16 + (e ^ 8)) for s in range(8) for e in range(16)]
 
     behind_routes = go(after(routes[0].T, plane), BEHIND, "pipe")
-    own, other, first, second = pick_rows(
+    own, other, first, second, third = pick_rows(
         plane, routes[0].T, route_weight[0].T, saved_input[0], grad_output[0]
     )
     across = go(after(other, behind_routes), ACROSS)
-    direct = go(second, ODD_BEHIND, "pipe")
-    away = go(second, AWAY_FIRST, "pipe")
+    turned = go(second, DOWN_Z, "pipe")
+    away = go(third, AWAY_FIRST, "pipe")
     near = [own] + [go(own, along_x(by)) for by in OFFSETS]
-    mirror = after(mirror_grad[0], across, near[1], near[2])
+    mirror = after(mirror_grad[0], across, near[1], near[2], turned, away)
     mirror = [go(mirror, MIRROR, "pipe")]
-    near = [near[0]] + [after(part, across) for part in near[1:3]] + [after(near[3], across, direct, away)]
+    near = [near[0]] + [after(part, across) for part in near[1:]]
     near = near + [go(part, SIBLING) for part in near]
     far = [after(across, *near[4:])]
     far = far + [go(far[0], along_x(by)) for by in OFFSETS]
     near[0] = after(near[0], *near[4:])
+    direct = go(after(third, *near[4:]), ODD_BEHIND, "pipe")
     near_mine, near_sibling, near_sibling_2, near_hidden = experts(near, *weights)
     far = [after(part, near_hidden) for part in far]
-    near_sibling = after(near_sibling, *far)
+    near_sibling = after(near_sibling, *far, direct)
     near_sibling_2 = after(near_sibling_2, near_sibling)
     near_parts = split_sum(near_mine, go(near_sibling, SIBLING), go(near_sibling_2, SIBLING))
     far = far + [go(part, SIBLING) for part in far]
@@ -331,17 +345,20 @@
     near_back[0] = after(near_back[0], far_hidden)
     near_total = add_up(near_parts[0], near_back)
     first = go(after(first, *near[4:]), BEHIND, "pipe")
+    crossed = go(after(turned, far_hidden, mirror[0]), CROSS_Y, "pipe")
     far_sibling = after(far_sibling, near_total)
     far_sibling_2 = after(far_sibling_2, far_sibling)
-    far_mine = after(far_mine, near_total)
+    far_mine = after(far_mine, near_total, away)
     far_parts = split_sum(far_mine, go(far_sibling, SIBLING), go(far_sibling_2, SIBLING))
     far_back = [go(part, along_x(-by)) for part, by in zip(far_parts[1:], OFFSETS)]
-    mirror[0] = after(mirror[0], far_hidden, away)
+    mirror[0] = after(mirror[0], far_hidden)
     down_grad = down_grads(near + far, near_hidden, far_hidden, mirror)
-    far_total = add_up(after(far_parts[0], down_grad, first), far_back)
+    far_total = add_up(after(far_parts[0], down_grad, first, crossed), far_back)
     near_back = go(near_total, BEHIND, "pipe")
     far_back = go(far_total, pairs, ("pipe", "expert"))
-    back = combine(odd, plane, behind_routes, first, direct, away, near_back, far_back)
+    back = combine(
+        rank, plane, behind_routes, first, turned, crossed, direct, away, near_back, far_back
+    )
     return back[None], down_grad[None]
 
 

time: 185 us -> 175 us (0.946)
  waiting for transfers between devices: 107 us -> 82.1 us
  starting transfers between devices: 32.4 us -> 41.2 us
  local copies, waits for them, and re-layouts: 4.12 us -> 8.03 us
  other arithmetic: 0.34 us -> 2.9 us
    ppermute x33 -> x35, waiting for transfers between devices: 107 us -> 82.1 us  [go(): return lax.ppermute(rows, axis, perm)]
    ppermute x33 -> x35, starting transfers between devices: 32.4 us -> 41.2 us  [go(): return lax.ppermute(rows, axis, perm)]
    unnamed x34 -> x46, local copies, waits for them, and re-layouts: 4.12 us -> 8.03 us
    convert_element_type x2, other arithmetic: 0.34 us -> 2.9 us  [add_up(): return total.astype(BF16)]
  transfers between devices with their start and end apart: 33 -> 35, of which waited for: 21 -> 19; matrix products, arithmetic and copies ran while one was open for 0% -> 2% of each run, Pallas kernels for 19% -> 20%
where the time goes in v3:
time: 175 us; the launch traced here: 173 us
  waiting for transfers between devices  82.1 us (47%)
  starting transfers between devices  41.2 us (24%)
  Pallas kernels  38 us (22%)
  local copies, waits for them, and re-layouts  8.03 us (5%)
  other arithmetic  2.9 us (2%)
    ppermute x35, waiting for transfers between devices, go(): return lax.ppermute(rows, axis, perm)  82.1 us
    ppermute x35, starting transfers between devices, go(): return lax.ppermute(rows, axis, perm)  41.2 us
    pallas_call x2, Pallas kernels, experts(): pl.pallas_call(functools.partial(experts_body, steps), grid=(2 * steps,),...  22.6 us
    unnamed x46, local copies, waits for them, and re-layouts  8.03 us
    pallas_call x1, Pallas kernels, down_grads(): pl.pallas_call(down_body, grid=(depth // BLOCK,), in_specs=[pl.BlockSpec(...  6.36 us
    pallas_call x1, Pallas kernels, pick_rows(): pl.pallas_call(pick_body, grid=(depth // PICK_BLOCK,), in_specs=[pl.Block...  4.33 us
  transfers between devices with their start and end apart: 35, of which 19 were waited for; matrix products, arithmetic and copies ran while one was open for 2% of the time, Pallas kernels for 20%

profile of v3, /device:TPU:6, one launch (start us, length us, event | category | flops | bytes accessed | tf_op | source)
XLA Modules:
  0.0 173.3 jit_solution(2893140807286668635)
XLA Ops:
  0.6 5.1 %collective-permute-start = (s32[8,192]{1,0:T(8,128)}, s32[8,192]{1,0:T(8,128)S(1)}, u32[]{:S(2)}, u32[]{:S(2)}) collective-permute-start(s32[8,192]{1,0:T(8,128)} %bitcast.17), channel_id=1, source_target_pairs={{0,112},{16,0},{32,16},{48,32},{64,48},{80,64},{96,80},{112,96},{1... | collective-permute-start | bytes 18440 | tf_op jit(solution)/shard_map/ppermute | solution.py:308
  7.2 4.3 %pick_rows.1 = (bf16[48,7168]{1,0:T(8,128)(2,1)S(1)}, bf16[48,7168]{1,0:T(8,128)(2,1)S(1)}, bf16[96,7168]{1,0:T(8,128)(2,1)S(1)}, bf16[48,7168]{1,0:T(8,128)(2,1)S(1)}, bf16[48,7168]{1,0:T(8,128)(2,1)S(1)}) custom-call(s32[1]{0:T(128)} %bitcast.1.plane, s32[8,192]{1,0:T(8,128)S(1)} %bitcast.18, f32[8,192]{1,0:T(8,128)S(1)} %bitcast.16, ...), custom_call_target="tpu_custom_call" | custom-call | flops 264241152 | bytes 13762560 | tf_op jit(solution)/shard_map/pick_rows/pallas_call | solution.py:101
  13.6 1.9 %collective-permute-start.17 = (bf16[48,7168]{1,0:T(8,128)(2,1)S(1)}, bf16[48,7168]{1,0:T(8,128)(2,1)}, u32[]{:S(2)}, u32[]{:S(2)}) collective-permute-start(bf16[48,7168]{1,0:T(8,128)(2,1)S(1)} %get-tuple-element.70), channel_id=1, source_target_pairs={{0,32},{32,0},{64,96},{96,64},{1,33},{33,1},{65,97},{97,65},{2,34}... | collective-permute-start | bytes 2064392 | tf_op jit(solution)/shard_map/ppermute | solution.py:308
  15.5 3.0 %collective-permute-start.3 = (bf16[48,7168]{1,0:T(8,128)(2,1)S(1)}, bf16[48,7168]{1,0:T(8,128)(2,1)S(1)}, u32[]{:S(2)}, u32[]{:S(2)}) collective-permute-start(bf16[48,7168]{1,0:T(8,128)(2,1)S(1)} %get-tuple-element.54), channel_id=1, source_target_pairs={{0,8},{1,9},{2,10},{3,11},{4,12},{5,13},{6,14},{7,15},{8,0},{9,1},... | collective-permute-start | bytes 2064392 | tf_op jit(solution)/shard_map/ppermute | solution.py:308
  18.5 10.0 %collective-permute-done.2.refs_1_ = bf16[48,7168]{1,0:T(8,128)(2,1)S(1)} collective-permute-done((bf16[48,7168]{1,0:T(8,128)(2,1)S(1)}, bf16[48,7168]{1,0:T(8,128)(2,1)S(1)}, u32[]{:S(2)}, u32[]{:S(2)}) %collective-permute-start.2) | collective-permute-done | bytes 688160 | tf_op jit(solution)/shard_map/ppermute | solution.py:308
  29.9 3.5 %collective-permute-done.17 = bf16[48,7168]{1,0:T(8,128)(2,1)} collective-permute-done((bf16[48,7168]{1,0:T(8,128)(2,1)S(1)}, bf16[48,7168]{1,0:T(8,128)(2,1)}, u32[]{:S(2)}, u32[]{:S(2)}) %collective-permute-start.17) | collective-permute-done | bytes 688160 | tf_op jit(solution)/shard_map/ppermute | solution.py:308
  35.4 15.0 %collective-permute-done.7.refs_3_ = bf16[48,7168]{1,0:T(8,128)(2,1)S(1)} collective-permute-done((bf16[48,7168]{1,0:T(8,128)(2,1)S(1)}, bf16[48,7168]{1,0:T(8,128)(2,1)S(1)}, u32[]{:S(2)}, u32[]{:S(2)}) %collective-permute-start.7) | collective-permute-done | bytes 688160 | tf_op jit(solution)/shard_map/ppermute | solution.py:308
  50.5 2.1 %collective-permute-done.8.refs_7_ = bf16[48,7168]{1,0:T(8,128)(2,1)S(1)} collective-permute-done((bf16[48,7168]{1,0:T(8,128)(2,1)S(1)}, bf16[48,7168]{1,0:T(8,128)(2,1)S(1)}, u32[]{:S(2)}, u32[]{:S(2)}) %collective-permute-start.8) | collective-permute-done | bytes 688160 | tf_op jit(solution)/shard_map/ppermute | solution.py:308
  52.6 1.7 collective-permute-start.11
  57.4 11.3 %experts.2 = (bf16[96,7168]{1,0:T(8,128)(2,1)}, bf16[48,7168]{1,0:T(8,128)(2,1)S(1)}, bf16[48,7168]{1,0:T(8,128)(2,1)S(1)}, bf16[256,192]{1,0:T(8,128)(2,1)S(1)}) custom-call(bf16[48,7168]{1,0:T(8,128)(2,1)S(1)} %get-tuple-element.61.refs_0_, bf16[48,7168]{1,0:T(8,128)(2,1)S(1)} %collective-permute-done.2.refs_1_, ...), custom_call_target="tpu_custom_call" | custom-call | flops 3523215360 | bytes 19267584 | tf_op jit(solution)/shard_map/experts/pallas_call | solution.py:197
  68.7 2.2 %collective-permute-done.11.refs_1_.refs_9_ = bf16[48,7168]{1,0:T(8,128)(2,1)S(1)} collective-permute-done((bf16[48,7168]{1,0:T(8,128)(2,1)S(1)}, bf16[48,7168]{1,0:T(8,128)(2,1)S(1)}, u32[]{:S(2)}, u32[]{:S(2)}) %collective-permute-start.11) | collective-permute-done | bytes 688160 | tf_op jit(solution)/shard_map/ppermute | solution.py:308
  70.9 16.6 %collective-permute-done.12.refs_2_.refs_10_ = bf16[48,7168]{1,0:T(8,128)(2,1)S(1)} collective-permute-done((bf16[48,7168]{1,0:T(8,128)(2,1)S(1)}, bf16[48,7168]{1,0:T(8,128)(2,1)S(1)}, u32[]{:S(2)}, u32[]{:S(2)}) %collective-permute-start.12) | collective-permute-done | bytes 688160 | tf_op jit(solution)/shard_map/ppermute | solution.py:308
  95.8 2.7 %collective-permute-start.26 = (bf16[24,7168]{1,0:T(8,128)(2,1)S(1)}, bf16[24,7168]{1,0:T(8,128)(2,1)}, u32[]{:S(2)}, u32[]{:S(2)}) collective-permute-start(bf16[24,7168]{1,0:T(8,128)(2,1)S(1)} %get-tuple-element.84), channel_id=1, source_target_pairs={{0,2},{1,3},{2,4},{3,5},{4,6},{5,7},{6,0},{7,1},{8,10},{9,11},{10,... | collective-permute-start | bytes 1032200 | tf_op jit(solution)/shard_map/ppermute | solution.py:308
  98.5 4.3 %collective-permute-start.24 = (bf16[48,7168]{1,0:T(8,128)(2,1)}, bf16[48,7168]{1,0:T(8,128)(2,1)S(1)}, u32[]{:S(2)}, u32[]{:S(2)}) collective-permute-start(bf16[48,7168]{1,0:T(8,128)(2,1)} %collective-permute-done.17), channel_id=1, source_target_pairs={{32,112},{96,48},{0,16},{64,80},{33,113},{97,49},{1,17},{65,81},{3... | collective-permute-start | bytes 2064392 | tf_op jit(solution)/shard_map/ppermute | solution.py:308
  102.8 12.5 %collective-permute-done.18.refs_18_ = bf16[256,7168]{1,0:T(8,128)(2,1)} collective-permute-done((bf16[256,7168]{1,0:T(8,128)(2,1)}, bf16[256,7168]{1,0:T(8,128)(2,1)}, u32[]{:S(2)}, u32[]{:S(2)}) %collective-permute-start.18) | collective-permute-done | bytes 3670048 | tf_op jit(solution)/shard_map/ppermute | solution.py:308
  115.7 11.3 %experts.3 = (bf16[96,7168]{1,0:T(8,128)(2,1)}, bf16[48,7168]{1,0:T(8,128)(2,1)S(1)}, bf16[48,7168]{1,0:T(8,128)(2,1)S(1)}, bf16[256,192]{1,0:T(8,128)(2,1)S(1)}) custom-call(bf16[48,7168]{1,0:T(8,128)(2,1)S(1)} %collective-permute-done.3.refs_0_.refs_8_, bf16[48,7168]{1,0:T(8,128)(2,1)S(1)} %collective-permute-done.11.refs_1_.refs_9_, ...), custom_call_target="tpu_custom_call" | custom-call | flops 3523215360 | bytes 19267584 | tf_op jit(solution)/shard_map/experts/pallas_call | solution.py:197
  127.2 2.0 %add_convert_fusion.1 = bf16[24,7168]{1,0:T(8,128)(2,1)} fusion(bf16[24,7168]{1,0:T(8,128)(2,1)S(1)} %collective-permute-done.27, bf16[24,7168]{1,0:T(8,128)(2,1)} %collective-permute-done.26, bf16[24,7168]{1,0:T(8,128)(2,1)S(1)} %collective-permute-done.25, bf16[24,7168]{1,0:T(8,128)(2,1)S(1)} %get-tuple-element.74), kind=kLoop, calls=%fused_computation.1 | loop fusion | flops 1376256 | bytes 1720320 | tf_op jit(solution)/shard_map/convert_element_type | solution.py:369
  135.8 2.1 %collective-permute-start.32 = (bf16[24,7168]{1,0:T(8,128)(2,1)S(1)}, bf16[24,7168]{1,0:T(8,128)(2,1)S(1)}, u32[]{:S(2)}, u32[]{:S(2)}) collective-permute-start(bf16[24,7168]{1,0:T(8,128)(2,1)S(1)} %get-tuple-element.96), channel_id=1, source_target_pairs={{0,2},{1,3},{2,4},{3,5},{4,6},{5,7},{6,0},{7,1},{8,10},{9,11},{10,... | collective-permute-start | bytes 1032200 | tf_op jit(solution)/shard_map/ppermute | solution.py:308
  137.9 6.4 %down_grads.1 = bf16[256,7168]{1,0:T(8,128)(2,1)} custom-call(bf16[48,7168]{1,0:T(8,128)(2,1)S(1)} %get-tuple-element.61.refs_0_, bf16[48,7168]{1,0:T(8,128)(2,1)S(1)} %collective-permute-done.2.refs_1_, bf16[48,7168]{1,0:T(8,128)(2,1)S(1)} %collective-permute-done.5.refs_2_, bf16[48,7168]{1,0:T(8,128)(2,1)S(1)} %collective-permute-done.7.refs_3_, ...), custom_call_target="tpu_custom_call" | custom-call | flops 1409286144 | bytes 18350080 | tf_op jit(solution)/shard_map/down_grads/pallas_call | solution.py:251
  144.9 2.9 %collective-permute-start.28 = (bf16[24,7168]{1,0:T(8,128)(2,1)}, bf16[24,7168]{1,0:T(8,128)(2,1)S(1)}, u32[]{:S(2)}, u32[]{:S(2)}) collective-permute-start(bf16[24,7168]{1,0:T(8,128)(2,1)} %add_convert_fusion.1), channel_id=1, source_target_pairs={{0,112},{16,0},{32,16},{48,32},{64,48},{80,64},{96,80},{112,96},{1... | collective-permute-start | bytes 1032200 | tf_op jit(solution)/shard_map/ppermute | solution.py:308
  148.6 3.8 %collective-permute-done.32 = bf16[24,7168]{1,0:T(8,128)(2,1)S(1)} collective-permute-done((bf16[24,7168]{1,0:T(8,128)(2,1)S(1)}, bf16[24,7168]{1,0:T(8,128)(2,1)S(1)}, u32[]{:S(2)}, u32[]{:S(2)}) %collective-permute-start.32) | collective-permute-done | bytes 344096 | tf_op jit(solution)/shard_map/ppermute | solution.py:308
  154.3 4.8 %collective-permute-start.34 = (bf16[24,7168]{1,0:T(8,128)(2,1)}, bf16[24,7168]{1,0:T(8,128)(2,1)}, u32[]{:S(2)}, u32[]{:S(2)}) collective-permute-start(bf16[24,7168]{1,0:T(8,128)(2,1)} %add_convert_fusion), channel_id=1, source_target_pairs={{0,120},{1,121},{2,122},{3,123},{4,124},{5,125},{6,126},{7,127},{8... | collective-permute-start | bytes 1032200 | tf_op jit(solution)/shard_map/ppermute | solution.py:308
  159.0 8.6 %collective-permute-done.34.other = bf16[24,7168]{1,0:T(8,128)(2,1)} collective-permute-done((bf16[24,7168]{1,0:T(8,128)(2,1)}, bf16[24,7168]{1,0:T(8,128)(2,1)}, u32[]{:S(2)}, u32[]{:S(2)}) %collective-permute-start.34) | collective-permute-done | bytes 344096 | tf_op jit(solution)/shard_map/ppermute | solution.py:308
  169.9 3.4 %combine.1 = bf16[192,7168]{1,0:T(8,128)(2,1)} custom-call(s32[1]{0:T(128)} %bitcast.rank, s32[1]{0:T(128)} %bitcast.1.plane, s32[8,192]{1,0:T(8,128)S(1)} %collective-permute-done.routes, bf16[96,7168]{1,0:T(8,128)(2,1)S(1)} %collective-permute-done.9.first, bf16[48,7168]{1,0:T(8,128)(2,1)S(1)} %collective-permute-done.10.turned, ...), custom_call_target="tpu_custom_call" | custom-call | flops 132120576 | bytes 8257536 | tf_op jit(solution)/shard_map/combine/pallas_call | solution.py:285
  (101 shorter events, 30.8 us)
Async XLA Ops:
  0.6 14.9 %collective-permute-start = (s32[8,192]{1,0:T(8,128)}, s32[8,192]{1,0:T(8,128)S(1)}, u32[]{:S(2)}, u32[]{:S(2)}) collective-permute-start(s32[8,192]{1,0:T(8,128)} %bitcast.17), channel_id=1, source_target_pairs={{0,112},{16,0},{32,16},{48,32},{64,48},{80,64},{96,80},{112,96},{1... | collective-permute-start | bytes 18440 | tf_op jit(solution)/shard_map/ppermute | solution.py:308
  11.5 17.0 %collective-permute-start.2 = (bf16[48,7168]{1,0:T(8,128)(2,1)S(1)}, bf16[48,7168]{1,0:T(8,128)(2,1)S(1)}, u32[]{:S(2)}, u32[]{:S(2)}) collective-permute-start(bf16[48,7168]{1,0:T(8,128)(2,1)S(1)} %get-tuple-element.61.refs_0_), channel_id=1, source_target_pairs={{0,2},{1,3},{2,4},{3,5},{4,6},{5,7},{6,0},{7,1},{8,10},{9,11},{10,... | collective-permute-start | bytes 2064392 | tf_op jit(solution)/shard_map/ppermute | solution.py:308
  12.1 17.8 %collective-permute-start.5 = (bf16[48,7168]{1,0:T(8,128)(2,1)S(1)}, bf16[48,7168]{1,0:T(8,128)(2,1)S(1)}, u32[]{:S(2)}, u32[]{:S(2)}) collective-permute-start(bf16[48,7168]{1,0:T(8,128)(2,1)S(1)} %get-tuple-element.61.refs_0_), channel_id=1, source_target_pairs={{0,6},{1,7},{2,0},{3,1},{4,2},{5,3},{6,4},{7,5},{8,14},{9,15},{10,... | collective-permute-start | bytes 2064392 | tf_op jit(solution)/shard_map/ppermute | solution.py:308
  13.6 16.3 %collective-permute-start.10 = (bf16[48,7168]{1,0:T(8,128)(2,1)S(1)}, bf16[48,7168]{1,0:T(8,128)(2,1)S(1)}, u32[]{:S(2)}, u32[]{:S(2)}) collective-permute-start(bf16[48,7168]{1,0:T(8,128)(2,1)S(1)} %get-tuple-element.59), channel_id=1, source_target_pairs={{0,48},{16,0},{32,16},{48,32},{64,112},{80,64},{96,80},{112,96},{1... | collective-permute-start | bytes 2064392 | tf_op jit(solution)/shard_map/ppermute | solution.py:308
  13.6 19.8 %collective-permute-start.17 = (bf16[48,7168]{1,0:T(8,128)(2,1)S(1)}, bf16[48,7168]{1,0:T(8,128)(2,1)}, u32[]{:S(2)}, u32[]{:S(2)}) collective-permute-start(bf16[48,7168]{1,0:T(8,128)(2,1)S(1)} %get-tuple-element.70), channel_id=1, source_target_pairs={{0,32},{32,0},{64,96},{96,64},{1,33},{33,1},{65,97},{97,65},{2,34}... | collective-permute-start | bytes 2064392 | tf_op jit(solution)/shard_map/ppermute | solution.py:308
  15.5 17.9 %collective-permute-start.3 = (bf16[48,7168]{1,0:T(8,128)(2,1)S(1)}, bf16[48,7168]{1,0:T(8,128)(2,1)S(1)}, u32[]{:S(2)}, u32[]{:S(2)}) collective-permute-start(bf16[48,7168]{1,0:T(8,128)(2,1)S(1)} %get-tuple-element.54), channel_id=1, source_target_pairs={{0,8},{1,9},{2,10},{3,11},{4,12},{5,13},{6,14},{7,15},{8,0},{9,1},... | collective-permute-start | bytes 2064392 | tf_op jit(solution)/shard_map/ppermute | solution.py:308
  33.5 81.8 %collective-permute-start.18 = (bf16[256,7168]{1,0:T(8,128)(2,1)}, bf16[256,7168]{1,0:T(8,128)(2,1)}, u32[]{:S(2)}, u32[]{:S(2)}) collective-permute-start(bf16[256,7168]{1,0:T(8,128)(2,1)} %bitcast.12), channel_id=1, source_target_pairs={{0,112},{16,96},{32,80},{48,64},{64,48},{80,32},{96,16},{112,0},{1... | collective-permute-start | bytes 11010056 | tf_op jit(solution)/shard_map/ppermute | solution.py:308
  33.5 17.0 %collective-permute-start.7 = (bf16[48,7168]{1,0:T(8,128)(2,1)S(1)}, bf16[48,7168]{1,0:T(8,128)(2,1)S(1)}, u32[]{:S(2)}, u32[]{:S(2)}) collective-permute-start(bf16[48,7168]{1,0:T(8,128)(2,1)S(1)} %get-tuple-element.61.refs_0_), channel_id=1, source_target_pairs={{0,4},{1,5},{2,6},{3,7},{4,0},{5,1},{6,2},{7,3},{8,12},{9,13},{10,... | collective-permute-start | bytes 2064392 | tf_op jit(solution)/shard_map/ppermute | solution.py:308
  34.9 15.6 %collective-permute-start.1 = (bf16[48,7168]{1,0:T(8,128)(2,1)S(1)}, bf16[48,7168]{1,0:T(8,128)(2,1)S(1)}, u32[]{:S(2)}, u32[]{:S(2)}) collective-permute-start(bf16[48,7168]{1,0:T(8,128)(2,1)S(1)} %get-tuple-element.61.refs_0_), channel_id=1, source_target_pairs={{0,1},{1,0},{2,3},{3,2},{4,5},{5,4},{6,7},{7,6},{8,9},{9,8},{10,11... | collective-permute-start | bytes 2064392 | tf_op jit(solution)/shard_map/ppermute | solution.py:308
  34.9 15.6 %collective-permute-start.4 = (bf16[48,7168]{1,0:T(8,128)(2,1)S(1)}, bf16[48,7168]{1,0:T(8,128)(2,1)S(1)}, u32[]{:S(2)}, u32[]{:S(2)}) collective-permute-start(bf16[48,7168]{1,0:T(8,128)(2,1)S(1)} %collective-permute-done.2.refs_1_), channel_id=1, source_target_pairs={{0,1},{1,0},{2,3},{3,2},{4,5},{5,4},{6,7},{7,6},{8,9},{9,8},{10,11... | collective-permute-start | bytes 2064392 | tf_op jit(solution)/shard_map/ppermute | solution.py:308
  35.4 15.1 %collective-permute-start.6 = (bf16[48,7168]{1,0:T(8,128)(2,1)S(1)}, bf16[48,7168]{1,0:T(8,128)(2,1)S(1)}, u32[]{:S(2)}, u32[]{:S(2)}) collective-permute-start(bf16[48,7168]{1,0:T(8,128)(2,1)S(1)} %collective-permute-done.5.refs_2_), channel_id=1, source_target_pairs={{0,1},{1,0},{2,3},{3,2},{4,5},{5,4},{6,7},{7,6},{8,9},{9,8},{10,11... | collective-permute-start | bytes 2064392 | tf_op jit(solution)/shard_map/ppermute | solution.py:308
  52.6 18.3 %collective-permute-start.11 = (bf16[48,7168]{1,0:T(8,128)(2,1)S(1)}, bf16[48,7168]{1,0:T(8,128)(2,1)S(1)}, u32[]{:S(2)}, u32[]{:S(2)}) collective-permute-start(bf16[48,7168]{1,0:T(8,128)(2,1)S(1)} %collective-permute-done.3.refs_0_.refs_8_), channel_id=1, source_target_pairs={{0,2},{1,3},{2,4},{3,5},{4,6},{5,7},{6,0},{7,1},{8,10},{9,11},{10,... | collective-permute-start | bytes 2064392 | tf_op jit(solution)/shard_map/ppermute | solution.py:308
  54.3 33.2 %collective-permute-start.12 = (bf16[48,7168]{1,0:T(8,128)(2,1)S(1)}, bf16[48,7168]{1,0:T(8,128)(2,1)S(1)}, u32[]{:S(2)}, u32[]{:S(2)}) collective-permute-start(bf16[48,7168]{1,0:T(8,128)(2,1)S(1)} %collective-permute-done.3.refs_0_.refs_8_), channel_id=1, source_target_pairs={{0,6},{1,7},{2,0},{3,1},{4,2},{5,3},{6,4},{7,5},{8,14},{9,15},{10,... | collective-permute-start | bytes 2064392 | tf_op jit(solution)/shard_map/ppermute | solution.py:308
  54.7 32.8 %collective-permute-start.13 = (bf16[48,7168]{1,0:T(8,128)(2,1)S(1)}, bf16[48,7168]{1,0:T(8,128)(2,1)S(1)}, u32[]{:S(2)}, u32[]{:S(2)}) collective-permute-start(bf16[48,7168]{1,0:T(8,128)(2,1)S(1)} %collective-permute-done.3.refs_0_.refs_8_), channel_id=1, source_target_pairs={{0,4},{1,5},{2,6},{3,7},{4,0},{5,1},{6,2},{7,3},{8,12},{9,13},{10,... | collective-permute-start | bytes 2064392 | tf_op jit(solution)/shard_map/ppermute | solution.py:308
  56.1 31.4 %collective-permute-start.14 = (bf16[48,7168]{1,0:T(8,128)(2,1)S(1)}, bf16[48,7168]{1,0:T(8,128)(2,1)S(1)}, u32[]{:S(2)}, u32[]{:S(2)}) collective-permute-start(bf16[48,7168]{1,0:T(8,128)(2,1)S(1)} %get-tuple-element.70), channel_id=1, source_target_pairs={{16,0},{48,32},{80,64},{112,96},{17,1},{49,33},{81,65},{113,97},{1... | collective-permute-start | bytes 2064392 | tf_op jit(solution)/shard_map/ppermute | solution.py:308
  94.6 32.5 %collective-permute-start.27 = (bf16[24,7168]{1,0:T(8,128)(2,1)S(1)}, bf16[24,7168]{1,0:T(8,128)(2,1)S(1)}, u32[]{:S(2)}, u32[]{:S(2)}) collective-permute-start(bf16[24,7168]{1,0:T(8,128)(2,1)S(1)} %get-tuple-element.85), channel_id=1, source_target_pairs={{0,4},{1,5},{2,6},{3,7},{4,0},{5,1},{6,2},{7,3},{8,12},{9,13},{10,... | collective-permute-start | bytes 1032200 | tf_op jit(solution)/shard_map/ppermute | solution.py:308
  95.3 31.9 %collective-permute-start.25 = (bf16[24,7168]{1,0:T(8,128)(2,1)S(1)}, bf16[24,7168]{1,0:T(8,128)(2,1)S(1)}, u32[]{:S(2)}, u32[]{:S(2)}) collective-permute-start(bf16[24,7168]{1,0:T(8,128)(2,1)S(1)} %get-tuple-element.82), channel_id=1, source_target_pairs={{0,6},{1,7},{2,0},{3,1},{4,2},{5,3},{6,4},{7,5},{8,14},{9,15},{10,... | collective-permute-start | bytes 1032200 | tf_op jit(solution)/shard_map/ppermute | solution.py:308
  95.8 31.3 %collective-permute-start.26 = (bf16[24,7168]{1,0:T(8,128)(2,1)S(1)}, bf16[24,7168]{1,0:T(8,128)(2,1)}, u32[]{:S(2)}, u32[]{:S(2)}) collective-permute-start(bf16[24,7168]{1,0:T(8,128)(2,1)S(1)} %get-tuple-element.84), channel_id=1, source_target_pairs={{0,2},{1,3},{2,4},{3,5},{4,6},{5,7},{6,0},{7,1},{8,10},{9,11},{10,... | collective-permute-start | bytes 1032200 | tf_op jit(solution)/shard_map/ppermute | solution.py:308
  98.5 31.9 %collective-permute-start.24 = (bf16[48,7168]{1,0:T(8,128)(2,1)}, bf16[48,7168]{1,0:T(8,128)(2,1)S(1)}, u32[]{:S(2)}, u32[]{:S(2)}) collective-permute-start(bf16[48,7168]{1,0:T(8,128)(2,1)} %collective-permute-done.17), channel_id=1, source_target_pairs={{32,112},{96,48},{0,16},{64,80},{33,113},{97,49},{1,17},{65,81},{3... | collective-permute-start | bytes 2064392 | tf_op jit(solution)/shard_map/ppermute | solution.py:308
  115.3 29.6 %collective-permute-start.9 = (bf16[96,7168]{1,0:T(8,128)(2,1)}, bf16[96,7168]{1,0:T(8,128)(2,1)S(1)}, u32[]{:S(2)}, u32[]{:S(2)}) collective-permute-start(bf16[96,7168]{1,0:T(8,128)(2,1)} %copy-done.20), channel_id=1, source_target_pairs={{0,112},{16,0},{32,16},{48,32},{64,48},{80,64},{96,80},{112,96},{1... | collective-permute-start | bytes 4128776 | tf_op jit(solution)/shard_map/ppermute | solution.py:308
  129.7 18.1 %collective-permute-start.23 = (bf16[48,7168]{1,0:T(8,128)(2,1)S(1)}, bf16[48,7168]{1,0:T(8,128)(2,1)S(1)}, u32[]{:S(2)}, u32[]{:S(2)}) collective-permute-start(bf16[48,7168]{1,0:T(8,128)(2,1)S(1)} %collective-permute-done.10.turned), channel_id=1, source_target_pairs={{48,112},{112,48},{49,113},{113,49},{50,114},{114,50},{51,115},{11... | collective-permute-start | bytes 2064392 | tf_op jit(solution)/shard_map/ppermute | solution.py:308
  134.3 14.4 %collective-permute-start.33 = (bf16[24,7168]{1,0:T(8,128)(2,1)S(1)}, bf16[24,7168]{1,0:T(8,128)(2,1)S(1)}, u32[]{:S(2)}, u32[]{:S(2)}) collective-permute-start(bf16[24,7168]{1,0:T(8,128)(2,1)S(1)} %get-tuple-element.97), channel_id=1, source_target_pairs={{0,4},{1,5},{2,6},{3,7},{4,0},{5,1},{6,2},{7,3},{8,12},{9,13},{10,... | collective-permute-start | bytes 1032200 | tf_op jit(solution)/shard_map/ppermute | solution.py:308
  135.8 16.6 %collective-permute-start.32 = (bf16[24,7168]{1,0:T(8,128)(2,1)S(1)}, bf16[24,7168]{1,0:T(8,128)(2,1)S(1)}, u32[]{:S(2)}, u32[]{:S(2)}) collective-permute-start(bf16[24,7168]{1,0:T(8,128)(2,1)S(1)} %get-tuple-element.96), channel_id=1, source_target_pairs={{0,2},{1,3},{2,4},{3,5},{4,6},{5,7},{6,0},{7,1},{8,10},{9,11},{10,... | collective-permute-start | bytes 1032200 | tf_op jit(solution)/shard_map/ppermute | solution.py:308
  137.9 15.5 %collective-permute-start.31 = (bf16[24,7168]{1,0:T(8,128)(2,1)S(1)}, bf16[24,7168]{1,0:T(8,128)(2,1)S(1)}, u32[]{:S(2)}, u32[]{:S(2)}) collective-permute-start(bf16[24,7168]{1,0:T(8,128)(2,1)S(1)} %get-tuple-element.95), channel_id=1, source_target_pairs={{0,6},{1,7},{2,0},{3,1},{4,2},{5,3},{6,4},{7,5},{8,14},{9,15},{10,... | collective-permute-start | bytes 1032200 | tf_op jit(solution)/shard_map/ppermute | solution.py:308
  (34 other events, 530.2 us)

commit v4 on v3

--- a/solution.py
+++ b/solution.py
@@ -10,6 +10,7 @@
 CAP = 24
 BLOCK = 3584
 PICK_BLOCK = 1792
+RISE_BLOCK = 3584
 DIRECT = 96
 TURNED = 144
 LIMIT = 48 * 1024 * 1024
@@ -210,6 +211,90 @@
         cost_estimate=cost(10 * count * depth * width, 2 * depth * (3 * width + 3 * count)),
         name="experts",
     )(*arrivals, gate, up, down)
+
+
+def rise_body(steps, *refs):
+    arrivals, (gate, up, down) = refs[:8], refs[8:11]
+    hidden_t, grad_gate, grad_up = refs[11:14]
+    pre_gate, pre_up, from_down = refs[14:]
+    step = pl.program_id(0)
+    rows = stacked(arrivals, 0)
+    scaled = stacked(arrivals, CAP)
+    gates = jnp.dot(rows, gate[...], preferred_element_type=F32)
+    ups = jnp.dot(rows, up[...], preferred_element_type=F32)
+    downs = contract_last(scaled, down[...])
+
+    @pl.when(step == 0)
+    def _():
+        pre_gate[...] = gates
+        pre_up[...] = ups
+        from_down[...] = downs
+
+    @pl.when(step > 0)
+    def _():
+        pre_gate[...] += gates
+        pre_up[...] += ups
+        from_down[...] += downs
+
+    @pl.when(step == steps - 1)
+    def _():
+        value = pre_gate[...]
+        sigma = 1.0 / (1.0 + jnp.exp(-value))
+        activated = value * sigma
+        slope = sigma * (1.0 + value * (1.0 - sigma))
+        hidden_t[...] = (activated * pre_up[...]).T.astype(BF16)
+        grad_gate[...] = (from_down[...] * pre_up[...] * slope).astype(BF16)
+        grad_up[...] = (from_down[...] * activated).astype(BF16)
+
+
+def rise(arrivals, gate, up, down):
+    depth, width = gate.shape
+    count = 8 * CAP
+    steps = depth // RISE_BLOCK
+    flat = pl.BlockSpec((count, width), lambda k: (0, 0))
+    grads = jax.ShapeDtypeStruct((count, width), BF16)
+    return pl.pallas_call(
+        functools.partial(rise_body, steps),
+        grid=(steps,),
+        in_specs=[pl.BlockSpec((2 * CAP, RISE_BLOCK), lambda k: (0, k))] * 8
+        + [pl.BlockSpec((RISE_BLOCK, width), lambda k: (k, 0))] * 2
+        + [pl.BlockSpec((width, RISE_BLOCK), lambda k: (0, k))],
+        out_specs=[pl.BlockSpec((width, count), lambda k: (0, 0)), flat, flat],
+        out_shape=[jax.ShapeDtypeStruct((width, count), BF16), grads, grads],
+        scratch_shapes=[pltpu.VMEM((count, width), F32)] * 3,
+        compiler_params=params(),
+        cost_estimate=cost(0, 0),
+        name="rise",
+    )(*arrivals, gate, up, down)
+
+
+def fall_body(grad_gate, grad_up, gate, up, mine, sibling, sibling_2):
+    partial = contract_last(grad_gate[...], gate[...])
+    partial = (partial + contract_last(grad_up[...], up[...])).astype(BF16)
+    half = partial.shape[0] // 2
+    mine[...] = partial[:half]
+    sibling[...] = partial[half : half + half // 2]
+    sibling_2[...] = partial[half + half // 2 :]
+
+
+def fall(grad_gate, grad_up, gate, up):
+    depth, width = gate.shape
+    count = grad_gate.shape[0]
+    flat = pl.BlockSpec((count, width), lambda k: (0, 0))
+    tall = pl.BlockSpec((RISE_BLOCK, width), lambda k: (k, 0))
+    out = pl.BlockSpec((count // 2, RISE_BLOCK), lambda k: (0, k))
+    half = pl.BlockSpec((count // 4, RISE_BLOCK), lambda k: (0, k))
+    halves = jax.ShapeDtypeStruct((count // 4, depth), BF16)
+    return pl.pallas_call(
+        fall_body,
+        grid=(depth // RISE_BLOCK,),
+        in_specs=[flat, flat, tall, tall],
+        out_specs=[out, half, half],
+        out_shape=[jax.ShapeDtypeStruct((count // 2, depth), BF16), halves, halves],
+        compiler_params=params(),
+        cost_estimate=cost(4 * count * depth * width, 2 * depth * (2 * width + count)),
+        name="fall",
+    )(grad_gate, grad_up, gate, up)
 
 
 def split_body(mine, first, second, *outs):
@@ -338,11 +423,13 @@
     near_sibling_2 = after(near_sibling_2, near_sibling)
     near_parts = split_sum(near_mine, go(near_sibling, SIBLING), go(near_sibling_2, SIBLING))
     far = far + [go(part, SIBLING) for part in far]
-    far[0] = after(far[0], near_parts, mirror[0])
+    far[0] = after(far[0], near_parts)
     away = go(away, AWAY_LAST, "pipe")
     near_back = [go(after(part, *far[4:]), along_x(-by)) for part, by in zip(near_parts[1:], OFFSETS)]
-    far_mine, far_sibling, far_sibling_2, far_hidden = experts(far, *weights)
-    near_back[0] = after(near_back[0], far_hidden)
+    far_hidden, grad_gate, grad_up = rise(far, *weights)
+    grad_gate = after(grad_gate, mirror[0])
+    far_mine, far_sibling, far_sibling_2 = fall(grad_gate, grad_up, *weights[:2])
+    near_back[0] = after(near_back[0], far_mine)
     near_total = add_up(near_parts[0], near_back)
     first = go(after(first, *near[4:]), BEHIND, "pipe")
     crossed = go(after(turned, far_hidden, mirror[0]), CROSS_Y, "pipe")

time: 175 us -> 169 us (0.966)
  starting transfers between devices: 41.2 us -> 36.8 us
    pallas_call x2 -> x1, Pallas kernels: 22.6 us -> 11.3 us  [experts(): pl.pallas_call(functools.partial(experts_body, steps), grid=(2 * steps,),...]
    pallas_call x0 -> x2, Pallas kernels: none -> 11.2 us  [the longest x1 6.22 us: rise(): pl.pallas_call(functools.partial(rise_body, steps), grid=(steps,), in_spe...]
    ppermute x35, starting transfers between devices: 41.2 us -> 36.8 us  [go(): return lax.ppermute(rows, axis, perm)]
    unnamed x46 -> x42, local copies, waits for them, and re-layouts: 8.03 us -> 7.58 us
  transfers between devices with their start and end apart: 35 -> 35, of which waited for: 19 -> 16; matrix products, arithmetic and copies ran while one was open for 2% -> 1% of each run, Pallas kernels for 20% -> 21%
where the time goes in v4:
time: 169 us
  waiting for transfers between devices  82.5 us (49%)
  Pallas kernels  39.3 us (23%)
  starting transfers between devices  36.8 us (22%)
  local copies, waits for them, and re-layouts  7.58 us (4%)
  other arithmetic  1.84 us (1%)
    ppermute x35, waiting for transfers between devices, go(): return lax.ppermute(rows, axis, perm)  82.5 us
    ppermute x35, starting transfers between devices, go(): return lax.ppermute(rows, axis, perm)  36.8 us
    pallas_call x1, Pallas kernels, experts(): pl.pallas_call(functools.partial(experts_body, steps), grid=(2 * steps,),...  11.3 us
    unnamed x42, local copies, waits for them, and re-layouts  7.58 us
    pallas_call x1, Pallas kernels, down_grads(): pl.pallas_call(down_body, grid=(depth // BLOCK,), in_specs=[pl.BlockSpec(...  6.35 us
    pallas_call x1, Pallas kernels, rise(): pl.pallas_call(functools.partial(rise_body, steps), grid=(steps,), in_spe...  6.22 us
    pallas_call x1, Pallas kernels, pick_rows(): pl.pallas_call(pick_body, grid=(depth // PICK_BLOCK,), in_specs=[pl.Block...  5.18 us
    pallas_call x1, Pallas kernels, fall(): pl.pallas_call(fall_body, grid=(depth // RISE_BLOCK,), in_specs=[flat, fl...  4.94 us
  transfers between devices with their start and end apart: 35, of which 16 were waited for; matrix products, arithmetic and copies ran while one was open for 1% of the time, Pallas kernels for 21%

profile of v4, /device:TPU:6, one launch (start us, length us, event | category | flops | bytes accessed | tf_op | source)
XLA Modules:
  0.0 169.0 jit_solution(11345038160548856459)
XLA Ops:
  0.6 5.1 %collective-permute-start = (s32[8,192]{1,0:T(8,128)}, s32[8,192]{1,0:T(8,128)S(1)}, u32[]{:S(2)}, u32[]{:S(2)}) collective-permute-start(s32[8,192]{1,0:T(8,128)} %bitcast.17), channel_id=1, source_target_pairs={{0,112},{16,0},{32,16},{48,32},{64,48},{80,64},{96,80},{112,96},{1... | collective-permute-start | bytes 18440 | tf_op jit(solution)/shard_map/ppermute | solution.py:393
  7.2 5.2 %pick_rows.1 = (bf16[48,7168]{1,0:T(8,128)(2,1)S(1)}, bf16[48,7168]{1,0:T(8,128)(2,1)S(1)}, bf16[96,7168]{1,0:T(8,128)(2,1)}, bf16[48,7168]{1,0:T(8,128)(2,1)S(1)}, bf16[48,7168]{1,0:T(8,128)(2,1)S(1)}) custom-call(s32[1]{0:T(128)} %bitcast.1.plane, s32[8,192]{1,0:T(8,128)S(1)} %bitcast.18, f32[8,192]{1,0:T(8,128)S(1)} %bitcast.16, ...), custom_call_target="tpu_custom_call" | custom-call | flops 264241152 | bytes 13762560 | tf_op jit(solution)/shard_map/pick_rows/pallas_call | solution.py:102
  13.2 2.4 %collective-permute-start.2 = (bf16[48,7168]{1,0:T(8,128)(2,1)S(1)}, bf16[48,7168]{1,0:T(8,128)(2,1)S(1)}, u32[]{:S(2)}, u32[]{:S(2)}) collective-permute-start(bf16[48,7168]{1,0:T(8,128)(2,1)S(1)} %get-tuple-element.64.refs_0_), channel_id=1, source_target_pairs={{0,2},{1,3},{2,4},{3,5},{4,6},{5,7},{6,0},{7,1},{8,10},{9,11},{10,... | collective-permute-start | bytes 2064392 | tf_op jit(solution)/shard_map/ppermute | solution.py:393
  15.6 1.9 %collective-permute-start.21 = (bf16[48,7168]{1,0:T(8,128)(2,1)S(1)}, bf16[48,7168]{1,0:T(8,128)(2,1)}, u32[]{:S(2)}, u32[]{:S(2)}) collective-permute-start(bf16[48,7168]{1,0:T(8,128)(2,1)S(1)} %get-tuple-element.73), channel_id=1, source_target_pairs={{0,32},{32,0},{64,96},{96,64},{1,33},{33,1},{65,97},{97,65},{2,34}... | collective-permute-start | bytes 2064392 | tf_op jit(solution)/shard_map/ppermute | solution.py:393
  17.5 3.0 %collective-permute-start.3 = (bf16[48,7168]{1,0:T(8,128)(2,1)S(1)}, bf16[48,7168]{1,0:T(8,128)(2,1)S(1)}, u32[]{:S(2)}, u32[]{:S(2)}) collective-permute-start(bf16[48,7168]{1,0:T(8,128)(2,1)S(1)} %get-tuple-element.57), channel_id=1, source_target_pairs={{0,8},{1,9},{2,10},{3,11},{4,12},{5,13},{6,14},{7,15},{8,0},{9,1},... | collective-permute-start | bytes 2064392 | tf_op jit(solution)/shard_map/ppermute | solution.py:393
  20.5 11.4 %collective-permute-done.10.turned = bf16[48,7168]{1,0:T(8,128)(2,1)S(1)} collective-permute-done((bf16[48,7168]{1,0:T(8,128)(2,1)S(1)}, bf16[48,7168]{1,0:T(8,128)(2,1)S(1)}, u32[]{:S(2)}, u32[]{:S(2)}) %collective-permute-start.10) | collective-permute-done | bytes 688160 | tf_op jit(solution)/shard_map/ppermute | solution.py:393
  31.9 3.5 %collective-permute-done.21 = bf16[48,7168]{1,0:T(8,128)(2,1)} collective-permute-done((bf16[48,7168]{1,0:T(8,128)(2,1)S(1)}, bf16[48,7168]{1,0:T(8,128)(2,1)}, u32[]{:S(2)}, u32[]{:S(2)}) %collective-permute-start.21) | collective-permute-done | bytes 688160 | tf_op jit(solution)/shard_map/ppermute | solution.py:393
  35.8 16.7 %collective-permute-done.7.refs_3_ = bf16[48,7168]{1,0:T(8,128)(2,1)S(1)} collective-permute-done((bf16[48,7168]{1,0:T(8,128)(2,1)S(1)}, bf16[48,7168]{1,0:T(8,128)(2,1)S(1)}, u32[]{:S(2)}, u32[]{:S(2)}) %collective-permute-start.7) | collective-permute-done | bytes 688160 | tf_op jit(solution)/shard_map/ppermute | solution.py:393
  53.0 1.6 collective-permute-done.8.refs_7_
  58.1 2.1 %collective-permute-start.11 = (bf16[48,7168]{1,0:T(8,128)(2,1)S(1)}, bf16[48,7168]{1,0:T(8,128)(2,1)S(1)}, u32[]{:S(2)}, u32[]{:S(2)}) collective-permute-start(bf16[48,7168]{1,0:T(8,128)(2,1)S(1)} %collective-permute-done.3.refs_0_.refs_8_), channel_id=1, source_target_pairs={{0,2},{1,3},{2,4},{3,5},{4,6},{5,7},{6,0},{7,1},{8,10},{9,11},{10,... | collective-permute-start | bytes 2064392 | tf_op jit(solution)/shard_map/ppermute | solution.py:393
  61.5 11.3 %experts.1 = (bf16[96,7168]{1,0:T(8,128)(2,1)}, bf16[48,7168]{1,0:T(8,128)(2,1)S(1)}, bf16[48,7168]{1,0:T(8,128)(2,1)S(1)}, bf16[256,192]{1,0:T(8,128)(2,1)S(1)}) custom-call(bf16[48,7168]{1,0:T(8,128)(2,1)S(1)} %get-tuple-element.64.refs_0_, bf16[48,7168]{1,0:T(8,128)(2,1)S(1)} %collective-permute-done.2.refs_1_, ...), custom_call_target="tpu_custom_call" | custom-call | flops 3523215360 | bytes 19267584 | tf_op jit(solution)/shard_map/experts/pallas_call | solution.py:198
  72.8 3.7 %collective-permute-done.13.refs_3_.refs_11_ = bf16[48,7168]{1,0:T(8,128)(2,1)S(1)} collective-permute-done((bf16[48,7168]{1,0:T(8,128)(2,1)S(1)}, bf16[48,7168]{1,0:T(8,128)(2,1)S(1)}, u32[]{:S(2)}, u32[]{:S(2)}) %collective-permute-start.13) | collective-permute-done | bytes 688160 | tf_op jit(solution)/shard_map/ppermute | solution.py:393
  76.5 13.6 %collective-permute-done.12.refs_2_.refs_10_ = bf16[48,7168]{1,0:T(8,128)(2,1)S(1)} collective-permute-done((bf16[48,7168]{1,0:T(8,128)(2,1)S(1)}, bf16[48,7168]{1,0:T(8,128)(2,1)S(1)}, u32[]{:S(2)}, u32[]{:S(2)}) %collective-permute-start.12) | collective-permute-done | bytes 688160 | tf_op jit(solution)/shard_map/ppermute | solution.py:393
  98.0 3.2 %collective-permute-start.26 = (bf16[24,7168]{1,0:T(8,128)(2,1)S(1)}, bf16[24,7168]{1,0:T(8,128)(2,1)S(1)}, u32[]{:S(2)}, u32[]{:S(2)}) collective-permute-start(bf16[24,7168]{1,0:T(8,128)(2,1)S(1)} %get-tuple-element.91), channel_id=1, source_target_pairs={{0,2},{1,3},{2,4},{3,5},{4,6},{5,7},{6,0},{7,1},{8,10},{9,11},{10,... | collective-permute-start | bytes 1032200 | tf_op jit(solution)/shard_map/ppermute | solution.py:393
  101.3 4.4 %collective-permute-start.24 = (bf16[48,7168]{1,0:T(8,128)(2,1)}, bf16[48,7168]{1,0:T(8,128)(2,1)S(1)}, u32[]{:S(2)}, u32[]{:S(2)}) collective-permute-start(bf16[48,7168]{1,0:T(8,128)(2,1)} %collective-permute-done.21), channel_id=1, source_target_pairs={{32,112},{96,48},{0,16},{64,80},{33,113},{97,49},{1,17},{65,81},{3... | collective-permute-start | bytes 2064392 | tf_op jit(solution)/shard_map/ppermute | solution.py:393
  105.7 6.2 %rise.1 = (bf16[256,192]{1,0:T(8,128)(2,1)S(1)}, bf16[192,256]{1,0:T(8,128)(2,1)S(1)}, bf16[192,256]{1,0:T(8,128)(2,1)S(1)}) custom-call(bf16[48,7168]{1,0:T(8,128)(2,1)S(1)} %collective-permute-done.3.refs_0_.refs_8_, bf16[48,7168]{1,0:T(8,128)(2,1)S(1)} %collective-permute-done.11.refs_1_.refs_9_, ...), custom_call_target="tpu_custom_call" | custom-call | tf_op jit(solution)/shard_map/rise/pallas_call | solution.py:256
  112.0 5.3 %collective-permute-done.22.refs_18_ = bf16[256,7168]{1,0:T(8,128)(2,1)} collective-permute-done((bf16[256,7168]{1,0:T(8,128)(2,1)}, bf16[256,7168]{1,0:T(8,128)(2,1)}, u32[]{:S(2)}, u32[]{:S(2)}) %collective-permute-start.22) | collective-permute-done | bytes 3670048 | tf_op jit(solution)/shard_map/ppermute | solution.py:393
  117.7 4.9 %fall.1 = (bf16[96,7168]{1,0:T(8,128)(2,1)S(1)}, bf16[48,7168]{1,0:T(8,128)(2,1)S(1)}, bf16[48,7168]{1,0:T(8,128)(2,1)S(1)}) custom-call(bf16[192,256]{1,0:T(8,128)(2,1)S(1)} %get-tuple-element.87.grad_gate, bf16[192,256]{1,0:T(8,128)(2,1)S(1)} %get-tuple-element.88.grad_up, bf16[7168,256]{1,0:T(8,128)(2,1)} %bitcast.21, bf16[7168,256]{1,0:T(8,128)(2,1)} %bitcast.24), custom_call_target="tpu_custom_call" | custom-call | flops 1409286144 | bytes 10092544 | tf_op jit(solution)/shard_map/fall/pallas_call | solution.py:288
  127.5 3.2 %collective-permute-start.32 = (bf16[24,7168]{1,0:T(8,128)(2,1)S(1)}, bf16[24,7168]{1,0:T(8,128)(2,1)S(1)}, u32[]{:S(2)}, u32[]{:S(2)}) collective-permute-start(bf16[24,7168]{1,0:T(8,128)(2,1)S(1)} %get-tuple-element.102), channel_id=1, source_target_pairs={{0,2},{1,3},{2,4},{3,5},{4,6},{5,7},{6,0},{7,1},{8,10},{9,11},{10,... | collective-permute-start | bytes 1032200 | tf_op jit(solution)/shard_map/ppermute | solution.py:393
  130.7 6.4 %down_grads.1 = bf16[256,7168]{1,0:T(8,128)(2,1)} custom-call(bf16[48,7168]{1,0:T(8,128)(2,1)S(1)} %get-tuple-element.64.refs_0_, bf16[48,7168]{1,0:T(8,128)(2,1)S(1)} %collective-permute-done.2.refs_1_, bf16[48,7168]{1,0:T(8,128)(2,1)S(1)} %collective-permute-done.5.refs_2_, bf16[48,7168]{1,0:T(8,128)(2,1)S(1)} %collective-permute-done.7.refs_3_, ...), custom_call_target="tpu_custom_call" | custom-call | flops 1409286144 | bytes 18350080 | tf_op jit(solution)/shard_map/down_grads/pallas_call | solution.py:336
  137.1 11.5 %collective-permute-done.9.first = bf16[96,7168]{1,0:T(8,128)(2,1)S(1)} collective-permute-done((bf16[96,7168]{1,0:T(8,128)(2,1)}, bf16[96,7168]{1,0:T(8,128)(2,1)S(1)}, u32[]{:S(2)}, u32[]{:S(2)}) %collective-permute-start.9) | collective-permute-done | bytes 1376288 | tf_op jit(solution)/shard_map/ppermute | solution.py:393
  151.5 2.9 %collective-permute-start.34 = (bf16[24,7168]{1,0:T(8,128)(2,1)}, bf16[24,7168]{1,0:T(8,128)(2,1)}, u32[]{:S(2)}, u32[]{:S(2)}) collective-permute-start(bf16[24,7168]{1,0:T(8,128)(2,1)} %add_convert_fusion), channel_id=1, source_target_pairs={{0,120},{1,121},{2,122},{3,123},{4,124},{5,125},{6,126},{7,127},{8... | collective-permute-start | bytes 1032200 | tf_op jit(solution)/shard_map/ppermute | solution.py:393
  154.4 9.0 %collective-permute-done.28.own = bf16[24,7168]{1,0:T(8,128)(2,1)S(1)} collective-permute-done((bf16[24,7168]{1,0:T(8,128)(2,1)}, bf16[24,7168]{1,0:T(8,128)(2,1)S(1)}, u32[]{:S(2)}, u32[]{:S(2)}) %collective-permute-start.28) | collective-permute-done | bytes 344096 | tf_op jit(solution)/shard_map/ppermute | solution.py:393
  165.6 3.4 %combine.1 = bf16[192,7168]{1,0:T(8,128)(2,1)} custom-call(s32[1]{0:T(128)} %bitcast.rank, s32[1]{0:T(128)} %bitcast.1.plane, s32[8,192]{1,0:T(8,128)S(1)} %collective-permute-done.routes, bf16[96,7168]{1,0:T(8,128)(2,1)S(1)} %collective-permute-done.9.first, bf16[48,7168]{1,0:T(8,128)(2,1)S(1)} %collective-permute-done.10.turned, ...), custom_call_target="tpu_custom_call" | custom-call | flops 132120576 | bytes 8257536 | tf_op jit(solution)/shard_map/combine/pallas_call | solution.py:370
  (98 shorter events, 26.0 us)
Async XLA Ops:
  0.6 16.9 %collective-permute-start = (s32[8,192]{1,0:T(8,128)}, s32[8,192]{1,0:T(8,128)S(1)}, u32[]{:S(2)}, u32[]{:S(2)}) collective-permute-start(s32[8,192]{1,0:T(8,128)} %bitcast.17), channel_id=1, source_target_pairs={{0,112},{16,0},{32,16},{48,32},{64,48},{80,64},{96,80},{112,96},{1... | collective-permute-start | bytes 18440 | tf_op jit(solution)/shard_map/ppermute | solution.py:393
  12.3 23.1 %collective-permute-start.5 = (bf16[48,7168]{1,0:T(8,128)(2,1)S(1)}, bf16[48,7168]{1,0:T(8,128)(2,1)S(1)}, u32[]{:S(2)}, u32[]{:S(2)}) collective-permute-start(bf16[48,7168]{1,0:T(8,128)(2,1)S(1)} %get-tuple-element.64.refs_0_), channel_id=1, source_target_pairs={{0,6},{1,7},{2,0},{3,1},{4,2},{5,3},{6,4},{7,5},{8,14},{9,15},{10,... | collective-permute-start | bytes 2064392 | tf_op jit(solution)/shard_map/ppermute | solution.py:393
  13.2 22.2 %collective-permute-start.2 = (bf16[48,7168]{1,0:T(8,128)(2,1)S(1)}, bf16[48,7168]{1,0:T(8,128)(2,1)S(1)}, u32[]{:S(2)}, u32[]{:S(2)}) collective-permute-start(bf16[48,7168]{1,0:T(8,128)(2,1)S(1)} %get-tuple-element.64.refs_0_), channel_id=1, source_target_pairs={{0,2},{1,3},{2,4},{3,5},{4,6},{5,7},{6,0},{7,1},{8,10},{9,11},{10,... | collective-permute-start | bytes 2064392 | tf_op jit(solution)/shard_map/ppermute | solution.py:393
  15.6 16.3 %collective-permute-start.10 = (bf16[48,7168]{1,0:T(8,128)(2,1)S(1)}, bf16[48,7168]{1,0:T(8,128)(2,1)S(1)}, u32[]{:S(2)}, u32[]{:S(2)}) collective-permute-start(bf16[48,7168]{1,0:T(8,128)(2,1)S(1)} %get-tuple-element.62), channel_id=1, source_target_pairs={{0,48},{16,0},{32,16},{48,32},{64,112},{80,64},{96,80},{112,96},{1... | collective-permute-start | bytes 2064392 | tf_op jit(solution)/shard_map/ppermute | solution.py:393
  15.6 19.8 %collective-permute-start.21 = (bf16[48,7168]{1,0:T(8,128)(2,1)S(1)}, bf16[48,7168]{1,0:T(8,128)(2,1)}, u32[]{:S(2)}, u32[]{:S(2)}) collective-permute-start(bf16[48,7168]{1,0:T(8,128)(2,1)S(1)} %get-tuple-element.73), channel_id=1, source_target_pairs={{0,32},{32,0},{64,96},{96,64},{1,33},{33,1},{65,97},{97,65},{2,34}... | collective-permute-start | bytes 2064392 | tf_op jit(solution)/shard_map/ppermute | solution.py:393
  17.5 17.9 %collective-permute-start.3 = (bf16[48,7168]{1,0:T(8,128)(2,1)S(1)}, bf16[48,7168]{1,0:T(8,128)(2,1)S(1)}, u32[]{:S(2)}, u32[]{:S(2)}) collective-permute-start(bf16[48,7168]{1,0:T(8,128)(2,1)S(1)} %get-tuple-element.57), channel_id=1, source_target_pairs={{0,8},{1,9},{2,10},{3,11},{4,12},{5,13},{6,14},{7,15},{8,0},{9,1},... | collective-permute-start | bytes 2064392 | tf_op jit(solution)/shard_map/ppermute | solution.py:393
  35.4 81.8 %collective-permute-start.22 = (bf16[256,7168]{1,0:T(8,128)(2,1)}, bf16[256,7168]{1,0:T(8,128)(2,1)}, u32[]{:S(2)}, u32[]{:S(2)}) collective-permute-start(bf16[256,7168]{1,0:T(8,128)(2,1)} %bitcast.12), channel_id=1, source_target_pairs={{0,112},{16,96},{32,80},{48,64},{64,48},{80,32},{96,16},{112,0},{1... | collective-permute-start | bytes 11010056 | tf_op jit(solution)/shard_map/ppermute | solution.py:393
  35.5 17.0 %collective-permute-start.7 = (bf16[48,7168]{1,0:T(8,128)(2,1)S(1)}, bf16[48,7168]{1,0:T(8,128)(2,1)S(1)}, u32[]{:S(2)}, u32[]{:S(2)}) collective-permute-start(bf16[48,7168]{1,0:T(8,128)(2,1)S(1)} %get-tuple-element.64.refs_0_), channel_id=1, source_target_pairs={{0,4},{1,5},{2,6},{3,7},{4,0},{5,1},{6,2},{7,3},{8,12},{9,13},{10,... | collective-permute-start | bytes 2064392 | tf_op jit(solution)/shard_map/ppermute | solution.py:393
  35.8 17.2 %collective-permute-start.1 = (bf16[48,7168]{1,0:T(8,128)(2,1)S(1)}, bf16[48,7168]{1,0:T(8,128)(2,1)S(1)}, u32[]{:S(2)}, u32[]{:S(2)}) collective-permute-start(bf16[48,7168]{1,0:T(8,128)(2,1)S(1)} %get-tuple-element.64.refs_0_), channel_id=1, source_target_pairs={{0,1},{1,0},{2,3},{3,2},{4,5},{5,4},{6,7},{7,6},{8,9},{9,8},{10,11... | collective-permute-start | bytes 2064392 | tf_op jit(solution)/shard_map/ppermute | solution.py:393
  56.6 19.8 %collective-permute-start.13 = (bf16[48,7168]{1,0:T(8,128)(2,1)S(1)}, bf16[48,7168]{1,0:T(8,128)(2,1)S(1)}, u32[]{:S(2)}, u32[]{:S(2)}) collective-permute-start(bf16[48,7168]{1,0:T(8,128)(2,1)S(1)} %collective-permute-done.3.refs_0_.refs_8_), channel_id=1, source_target_pairs={{0,4},{1,5},{2,6},{3,7},{4,0},{5,1},{6,2},{7,3},{8,12},{9,13},{10,... | collective-permute-start | bytes 2064392 | tf_op jit(solution)/shard_map/ppermute | solution.py:393
  56.9 33.2 %collective-permute-start.12 = (bf16[48,7168]{1,0:T(8,128)(2,1)S(1)}, bf16[48,7168]{1,0:T(8,128)(2,1)S(1)}, u32[]{:S(2)}, u32[]{:S(2)}) collective-permute-start(bf16[48,7168]{1,0:T(8,128)(2,1)S(1)} %collective-permute-done.3.refs_0_.refs_8_), channel_id=1, source_target_pairs={{0,6},{1,7},{2,0},{3,1},{4,2},{5,3},{6,4},{7,5},{8,14},{9,15},{10,... | collective-permute-start | bytes 2064392 | tf_op jit(solution)/shard_map/ppermute | solution.py:393
  58.1 32.0 %collective-permute-start.11 = (bf16[48,7168]{1,0:T(8,128)(2,1)S(1)}, bf16[48,7168]{1,0:T(8,128)(2,1)S(1)}, u32[]{:S(2)}, u32[]{:S(2)}) collective-permute-start(bf16[48,7168]{1,0:T(8,128)(2,1)S(1)} %collective-permute-done.3.refs_0_.refs_8_), channel_id=1, source_target_pairs={{0,2},{1,3},{2,4},{3,5},{4,6},{5,7},{6,0},{7,1},{8,10},{9,11},{10,... | collective-permute-start | bytes 2064392 | tf_op jit(solution)/shard_map/ppermute | solution.py:393
  60.2 29.9 %collective-permute-start.14 = (bf16[48,7168]{1,0:T(8,128)(2,1)S(1)}, bf16[48,7168]{1,0:T(8,128)(2,1)S(1)}, u32[]{:S(2)}, u32[]{:S(2)}) collective-permute-start(bf16[48,7168]{1,0:T(8,128)(2,1)S(1)} %get-tuple-element.73), channel_id=1, source_target_pairs={{16,0},{48,32},{80,64},{112,96},{17,1},{49,33},{81,65},{113,97},{1... | collective-permute-start | bytes 2064392 | tf_op jit(solution)/shard_map/ppermute | solution.py:393
  98.0 24.6 %collective-permute-start.25 = (bf16[24,7168]{1,0:T(8,128)(2,1)}, bf16[24,7168]{1,0:T(8,128)(2,1)S(1)}, u32[]{:S(2)}, u32[]{:S(2)}) collective-permute-start(bf16[24,7168]{1,0:T(8,128)(2,1)} %get-tuple-element.85), channel_id=1, source_target_pairs={{0,6},{1,7},{2,0},{3,1},{4,2},{5,3},{6,4},{7,5},{8,14},{9,15},{10,... | collective-permute-start | bytes 1032200 | tf_op jit(solution)/shard_map/ppermute | solution.py:393
  98.0 24.6 %collective-permute-start.26 = (bf16[24,7168]{1,0:T(8,128)(2,1)S(1)}, bf16[24,7168]{1,0:T(8,128)(2,1)S(1)}, u32[]{:S(2)}, u32[]{:S(2)}) collective-permute-start(bf16[24,7168]{1,0:T(8,128)(2,1)S(1)} %get-tuple-element.91), channel_id=1, source_target_pairs={{0,2},{1,3},{2,4},{3,5},{4,6},{5,7},{6,0},{7,1},{8,10},{9,11},{10,... | collective-permute-start | bytes 1032200 | tf_op jit(solution)/shard_map/ppermute | solution.py:393
  101.3 21.4 %collective-permute-start.27 = (bf16[24,7168]{1,0:T(8,128)(2,1)S(1)}, bf16[24,7168]{1,0:T(8,128)(2,1)S(1)}, u32[]{:S(2)}, u32[]{:S(2)}) collective-permute-start(bf16[24,7168]{1,0:T(8,128)(2,1)S(1)} %get-tuple-element.92), channel_id=1, source_target_pairs={{0,4},{1,5},{2,6},{3,7},{4,0},{5,1},{6,2},{7,3},{8,12},{9,13},{10,... | collective-permute-start | bytes 1032200 | tf_op jit(solution)/shard_map/ppermute | solution.py:393
  101.3 23.5 %collective-permute-start.24 = (bf16[48,7168]{1,0:T(8,128)(2,1)}, bf16[48,7168]{1,0:T(8,128)(2,1)S(1)}, u32[]{:S(2)}, u32[]{:S(2)}) collective-permute-start(bf16[48,7168]{1,0:T(8,128)(2,1)} %collective-permute-done.21), channel_id=1, source_target_pairs={{32,112},{96,48},{0,16},{64,80},{33,113},{97,49},{1,17},{65,81},{3... | collective-permute-start | bytes 2064392 | tf_op jit(solution)/shard_map/ppermute | solution.py:393
  117.3 31.3 %collective-permute-start.9 = (bf16[96,7168]{1,0:T(8,128)(2,1)}, bf16[96,7168]{1,0:T(8,128)(2,1)S(1)}, u32[]{:S(2)}, u32[]{:S(2)}) collective-permute-start(bf16[96,7168]{1,0:T(8,128)(2,1)} %get-tuple-element.61), channel_id=1, source_target_pairs={{0,112},{16,0},{32,16},{48,32},{64,48},{80,64},{96,80},{112,96},{1... | collective-permute-start | bytes 4128776 | tf_op jit(solution)/shard_map/ppermute | solution.py:393
  124.1 25.6 %collective-permute-start.23 = (bf16[48,7168]{1,0:T(8,128)(2,1)S(1)}, bf16[48,7168]{1,0:T(8,128)(2,1)S(1)}, u32[]{:S(2)}, u32[]{:S(2)}) collective-permute-start(bf16[48,7168]{1,0:T(8,128)(2,1)S(1)} %collective-permute-done.10.turned), channel_id=1, source_target_pairs={{48,112},{112,48},{49,113},{113,49},{50,114},{114,50},{51,115},{11... | collective-permute-start | bytes 2064392 | tf_op jit(solution)/shard_map/ppermute | solution.py:393
  127.4 23.1 %collective-permute-start.31 = (bf16[24,7168]{1,0:T(8,128)(2,1)S(1)}, bf16[24,7168]{1,0:T(8,128)(2,1)S(1)}, u32[]{:S(2)}, u32[]{:S(2)}) collective-permute-start(bf16[24,7168]{1,0:T(8,128)(2,1)S(1)} %get-tuple-element.101), channel_id=1, source_target_pairs={{0,6},{1,7},{2,0},{3,1},{4,2},{5,3},{6,4},{7,5},{8,14},{9,15},{10,... | collective-permute-start | bytes 1032200 | tf_op jit(solution)/shard_map/ppermute | solution.py:393
  127.5 23.0 %collective-permute-start.32 = (bf16[24,7168]{1,0:T(8,128)(2,1)S(1)}, bf16[24,7168]{1,0:T(8,128)(2,1)S(1)}, u32[]{:S(2)}, u32[]{:S(2)}) collective-permute-start(bf16[24,7168]{1,0:T(8,128)(2,1)S(1)} %get-tuple-element.102), channel_id=1, source_target_pairs={{0,2},{1,3},{2,4},{3,5},{4,6},{5,7},{6,0},{7,1},{8,10},{9,11},{10,... | collective-permute-start | bytes 1032200 | tf_op jit(solution)/shard_map/ppermute | solution.py:393
  130.7 19.8 %collective-permute-start.33 = (bf16[24,7168]{1,0:T(8,128)(2,1)S(1)}, bf16[24,7168]{1,0:T(8,128)(2,1)S(1)}, u32[]{:S(2)}, u32[]{:S(2)}) collective-permute-start(bf16[24,7168]{1,0:T(8,128)(2,1)S(1)} %get-tuple-element.103), channel_id=1, source_target_pairs={{0,4},{1,5},{2,6},{3,7},{4,0},{5,1},{6,2},{7,3},{8,12},{9,13},{10,... | collective-permute-start | bytes 1032200 | tf_op jit(solution)/shard_map/ppermute | solution.py:393
  148.5 14.8 %collective-permute-start.28 = (bf16[24,7168]{1,0:T(8,128)(2,1)}, bf16[24,7168]{1,0:T(8,128)(2,1)S(1)}, u32[]{:S(2)}, u32[]{:S(2)}) collective-permute-start(bf16[24,7168]{1,0:T(8,128)(2,1)} %add_convert_fusion.1), channel_id=1, source_target_pairs={{0,112},{16,0},{32,16},{48,32},{64,48},{80,64},{96,80},{112,96},{1... | collective-permute-start | bytes 1032200 | tf_op jit(solution)/shard_map/ppermute | solution.py:393
  151.5 11.9 %collective-permute-start.34 = (bf16[24,7168]{1,0:T(8,128)(2,1)}, bf16[24,7168]{1,0:T(8,128)(2,1)}, u32[]{:S(2)}, u32[]{:S(2)}) collective-permute-start(bf16[24,7168]{1,0:T(8,128)(2,1)} %add_convert_fusion), channel_id=1, source_target_pairs={{0,120},{1,121},{2,122},{3,123},{4,124},{5,125},{6,126},{7,127},{8... | collective-permute-start | bytes 1032200 | tf_op jit(solution)/shard_map/ppermute | solution.py:393
  (32 other events, 315.6 us)

commit v5 on v4

--- a/solution.py
+++ b/solution.py
@@ -11,7 +11,7 @@
 BLOCK = 3584
 PICK_BLOCK = 1792
 RISE_BLOCK = 3584
-DIRECT = 96
+DIRECT = 80
 TURNED = 144
 LIMIT = 48 * 1024 * 1024
 F32 = jnp.float32

time: 169 us -> 183 us (1.083)
  starting transfers between devices: 36.8 us -> 48.9 us
  waiting for transfers between devices: 82.5 us -> 80.6 us
    ppermute x35, starting transfers between devices: 36.8 us -> 48.9 us  [go(): return lax.ppermute(rows, axis, perm)]
    ppermute x35, waiting for transfers between devices: 82.5 us -> 80.6 us  [go(): return lax.ppermute(rows, axis, perm)]
    unnamed x42 -> x46, local copies, waits for them, and re-layouts: 7.58 us -> 8.43 us
  transfers between devices with their start and end apart: 35 -> 35, of which waited for: 16 -> 17; matrix products, arithmetic and copies ran while one was open for 1% -> 2% of each run, Pallas kernels for 21% -> 17%
where the time goes in v5:
time: 183 us; the launch traced here: 181 us
  waiting for transfers between devices  80.6 us (44%)
  starting transfers between devices  48.9 us (27%)
  Pallas kernels  39.4 us (22%)
  local copies, waits for them, and re-layouts  8.43 us (5%)
  other arithmetic  3.01 us (2%)
    ppermute x35, waiting for transfers between devices, go(): return lax.ppermute(rows, axis, perm)  80.6 us
    ppermute x35, starting transfers between devices, go(): return lax.ppermute(rows, axis, perm)  48.9 us
    pallas_call x1, Pallas kernels, experts(): pl.pallas_call(functools.partial(experts_body, steps), grid=(2 * steps,),...  11.3 us
    unnamed x46, local copies, waits for them, and re-layouts  8.43 us
    pallas_call x1, Pallas kernels, down_grads(): pl.pallas_call(down_body, grid=(depth // BLOCK,), in_specs=[pl.BlockSpec(...  6.34 us
    pallas_call x1, Pallas kernels, rise(): pl.pallas_call(functools.partial(rise_body, steps), grid=(steps,), in_spe...  6.29 us
    pallas_call x1, Pallas kernels, fall(): pl.pallas_call(fall_body, grid=(depth // RISE_BLOCK,), in_specs=[flat, fl...  5.65 us
    pallas_call x1, Pallas kernels, pick_rows(): pl.pallas_call(pick_body, grid=(depth // PICK_BLOCK,), in_specs=[pl.Block...  4.33 us
  transfers between devices with their start and end apart: 35, of which 17 were waited for; matrix products, arithmetic and copies ran while one was open for 2% of the time, Pallas kernels for 17%

profile of v5, /device:TPU:6, one launch (start us, length us, event | category | flops | bytes accessed | tf_op | source)
XLA Modules:
  0.0 181.3 jit_solution(13695095192294254408)
XLA Ops:
  2.0 4.3 %pick_rows.1 = (bf16[48,7168]{1,0:T(8,128)(2,1)S(1)}, bf16[48,7168]{1,0:T(8,128)(2,1)S(1)}, bf16[80,7168]{1,0:T(8,128)(2,1)S(1)}, bf16[64,7168]{1,0:T(8,128)(2,1)S(1)}, bf16[48,7168]{1,0:T(8,128)(2,1)S(1)}) custom-call(s32[1]{0:T(128)} %bitcast.1.plane, s32[8,192]{1,0:T(8,128)S(1)} %bitcast.17, f32[8,192]{1,0:T(8,128)S(1)} %bitcast.16, ...), custom_call_target="tpu_custom_call" | custom-call | flops 264241152 | bytes 13762560 | tf_op jit(solution)/shard_map/pick_rows/pallas_call | solution.py:102
  7.4 4.0 %collective-permute-start.10 = (bf16[64,7168]{1,0:T(8,128)(2,1)S(1)}, bf16[64,7168]{1,0:T(8,128)(2,1)S(1)}, u32[]{:S(2)}, u32[]{:S(2)}) collective-permute-start(bf16[64,7168]{1,0:T(8,128)(2,1)S(1)} %get-tuple-element.62), channel_id=1, source_target_pairs={{0,48},{16,0},{32,16},{48,32},{64,112},{80,64},{96,80},{112,96},{1... | collective-permute-start | bytes 2752520 | tf_op jit(solution)/shard_map/ppermute | solution.py:393
  18.0 11.8 %collective-permute-done.routes = s32[8,192]{1,0:T(8,128)S(1)} collective-permute-done((s32[8,192]{1,0:T(8,128)S(1)}, s32[8,192]{1,0:T(8,128)S(1)}, u32[]{:S(2)}, u32[]{:S(2)}) %collective-permute-start) | collective-permute-done | bytes 6176 | tf_op jit(solution)/shard_map/ppermute | solution.py:393
  29.8 3.2 %collective-permute-start.3 = (bf16[48,7168]{1,0:T(8,128)(2,1)S(1)}, bf16[48,7168]{1,0:T(8,128)(2,1)S(1)}, u32[]{:S(2)}, u32[]{:S(2)}) collective-permute-start(bf16[48,7168]{1,0:T(8,128)(2,1)S(1)} %get-tuple-element.57), channel_id=1, source_target_pairs={{0,8},{1,9},{2,10},{3,11},{4,12},{5,13},{6,14},{7,15},{8,0},{9,1},... | collective-permute-start | bytes 2064392 | tf_op jit(solution)/shard_map/ppermute | solution.py:393
  33.0 2.6 %collective-permute-done.21 = bf16[48,7168]{1,0:T(8,128)(2,1)} collective-permute-done((bf16[48,7168]{1,0:T(8,128)(2,1)S(1)}, bf16[48,7168]{1,0:T(8,128)(2,1)}, u32[]{:S(2)}, u32[]{:S(2)}) %collective-permute-start.21) | collective-permute-done | bytes 688160 | tf_op jit(solution)/shard_map/ppermute | solution.py:393
  35.6 12.3 %collective-permute-done.3.refs_0_.refs_8_ = bf16[48,7168]{1,0:T(8,128)(2,1)S(1)} collective-permute-done((bf16[48,7168]{1,0:T(8,128)(2,1)S(1)}, bf16[48,7168]{1,0:T(8,128)(2,1)S(1)}, u32[]{:S(2)}, u32[]{:S(2)}) %collective-permute-start.3) | collective-permute-done | bytes 688160 | tf_op jit(solution)/shard_map/ppermute | solution.py:393
  47.9 2.5 %collective-permute-start.22 = (bf16[256,7168]{1,0:T(8,128)(2,1)}, bf16[256,7168]{1,0:T(8,128)(2,1)}, u32[]{:S(2)}, u32[]{:S(2)}) collective-permute-start(bf16[256,7168]{1,0:T(8,128)(2,1)} %bitcast.12), channel_id=1, source_target_pairs={{0,112},{16,96},{32,80},{48,64},{64,48},{80,32},{96,16},{112,0},{1... | collective-permute-start | bytes 11010056 | tf_op jit(solution)/shard_map/ppermute | solution.py:393
  51.8 15.2 %collective-permute-done.7.refs_3_ = bf16[48,7168]{1,0:T(8,128)(2,1)S(1)} collective-permute-done((bf16[48,7168]{1,0:T(8,128)(2,1)S(1)}, bf16[48,7168]{1,0:T(8,128)(2,1)S(1)}, u32[]{:S(2)}, u32[]{:S(2)}) %collective-permute-start.7) | collective-permute-done | bytes 688160 | tf_op jit(solution)/shard_map/ppermute | solution.py:393
  72.6 3.2 %collective-permute-start.11 = (bf16[48,7168]{1,0:T(8,128)(2,1)S(1)}, bf16[48,7168]{1,0:T(8,128)(2,1)S(1)}, u32[]{:S(2)}, u32[]{:S(2)}) collective-permute-start(bf16[48,7168]{1,0:T(8,128)(2,1)S(1)} %collective-permute-done.3.refs_0_.refs_8_), channel_id=1, source_target_pairs={{0,2},{1,3},{2,4},{3,5},{4,6},{5,7},{6,0},{7,1},{8,10},{9,11},{10,... | collective-permute-start | bytes 2064392 | tf_op jit(solution)/shard_map/ppermute | solution.py:393
  77.1 11.3 %experts.1 = (bf16[96,7168]{1,0:T(8,128)(2,1)}, bf16[48,7168]{1,0:T(8,128)(2,1)S(1)}, bf16[48,7168]{1,0:T(8,128)(2,1)S(1)}, bf16[256,192]{1,0:T(8,128)(2,1)S(1)}) custom-call(bf16[48,7168]{1,0:T(8,128)(2,1)S(1)} %get-tuple-element.64.refs_0_, bf16[48,7168]{1,0:T(8,128)(2,1)S(1)} %collective-permute-done.2.refs_1_, ...), custom_call_target="tpu_custom_call" | custom-call | flops 3523215360 | bytes 19267584 | tf_op jit(solution)/shard_map/experts/pallas_call | solution.py:198
  88.4 2.6 %collective-permute-done.13.refs_3_.refs_11_ = bf16[48,7168]{1,0:T(8,128)(2,1)S(1)} collective-permute-done((bf16[48,7168]{1,0:T(8,128)(2,1)S(1)}, bf16[48,7168]{1,0:T(8,128)(2,1)S(1)}, u32[]{:S(2)}, u32[]{:S(2)}) %collective-permute-start.13) | collective-permute-done | bytes 688160 | tf_op jit(solution)/shard_map/ppermute | solution.py:393
  91.0 13.9 %collective-permute-done.12.refs_2_.refs_10_ = bf16[48,7168]{1,0:T(8,128)(2,1)S(1)} collective-permute-done((bf16[48,7168]{1,0:T(8,128)(2,1)S(1)}, bf16[48,7168]{1,0:T(8,128)(2,1)S(1)}, u32[]{:S(2)}, u32[]{:S(2)}) %collective-permute-start.12) | collective-permute-done | bytes 688160 | tf_op jit(solution)/shard_map/ppermute | solution.py:393
  113.7 2.4 %collective-permute-start.26 = (bf16[24,7168]{1,0:T(8,128)(2,1)}, bf16[24,7168]{1,0:T(8,128)(2,1)}, u32[]{:S(2)}, u32[]{:S(2)}) collective-permute-start(bf16[24,7168]{1,0:T(8,128)(2,1)} %get-tuple-element.91), channel_id=1, source_target_pairs={{0,2},{1,3},{2,4},{3,5},{4,6},{5,7},{6,0},{7,1},{8,10},{9,11},{10,... | collective-permute-start | bytes 1032200 | tf_op jit(solution)/shard_map/ppermute | solution.py:393
  116.4 4.2 %collective-permute-start.24 = (bf16[48,7168]{1,0:T(8,128)(2,1)}, bf16[48,7168]{1,0:T(8,128)(2,1)S(1)}, u32[]{:S(2)}, u32[]{:S(2)}) collective-permute-start(bf16[48,7168]{1,0:T(8,128)(2,1)} %collective-permute-done.21), channel_id=1, source_target_pairs={{32,112},{96,48},{0,16},{64,80},{33,113},{97,49},{1,17},{65,81},{3... | collective-permute-start | bytes 2064392 | tf_op jit(solution)/shard_map/ppermute | solution.py:393
  120.6 6.3 %rise.1 = (bf16[256,192]{1,0:T(8,128)(2,1)S(1)}, bf16[192,256]{1,0:T(8,128)(2,1)S(1)}, bf16[192,256]{1,0:T(8,128)(2,1)S(1)}) custom-call(bf16[48,7168]{1,0:T(8,128)(2,1)S(1)} %collective-permute-done.3.refs_0_.refs_8_, bf16[48,7168]{1,0:T(8,128)(2,1)S(1)} %collective-permute-done.11.refs_1_.refs_9_, ...), custom_call_target="tpu_custom_call" | custom-call | tf_op jit(solution)/shard_map/rise/pallas_call | solution.py:256
  127.0 3.0 %collective-permute-done.22.refs_18_ = bf16[256,7168]{1,0:T(8,128)(2,1)} collective-permute-done((bf16[256,7168]{1,0:T(8,128)(2,1)}, bf16[256,7168]{1,0:T(8,128)(2,1)}, u32[]{:S(2)}, u32[]{:S(2)}) %collective-permute-start.22) | collective-permute-done | bytes 3670048 | tf_op jit(solution)/shard_map/ppermute | solution.py:393
  132.2 5.7 %fall.1 = (bf16[96,7168]{1,0:T(8,128)(2,1)S(1)}, bf16[48,7168]{1,0:T(8,128)(2,1)S(1)}, bf16[48,7168]{1,0:T(8,128)(2,1)}) custom-call(bf16[192,256]{1,0:T(8,128)(2,1)S(1)} %get-tuple-element.87.grad_gate, bf16[192,256]{1,0:T(8,128)(2,1)S(1)} %get-tuple-element.88.grad_up, bf16[7168,256]{1,0:T(8,128)(2,1)} %bitcast.21, bf16[7168,256]{1,0:T(8,128)(2,1)} %bitcast.24), custom_call_target="tpu_custom_call" | custom-call | flops 1409286144 | bytes 10092544 | tf_op jit(solution)/shard_map/fall/pallas_call | solution.py:288
  144.8 2.4 %collective-permute-start.32 = (bf16[24,7168]{1,0:T(8,128)(2,1)S(1)}, bf16[24,7168]{1,0:T(8,128)(2,1)S(1)}, u32[]{:S(2)}, u32[]{:S(2)}) collective-permute-start(bf16[24,7168]{1,0:T(8,128)(2,1)S(1)} %get-tuple-element.102), channel_id=1, source_target_pairs={{0,2},{1,3},{2,4},{3,5},{4,6},{5,7},{6,0},{7,1},{8,10},{9,11},{10,... | collective-permute-start | bytes 1032200 | tf_op jit(solution)/shard_map/ppermute | solution.py:393
  147.4 6.3 %down_grads.1 = bf16[256,7168]{1,0:T(8,128)(2,1)} custom-call(bf16[48,7168]{1,0:T(8,128)(2,1)S(1)} %get-tuple-element.64.refs_0_, bf16[48,7168]{1,0:T(8,128)(2,1)S(1)} %collective-permute-done.2.refs_1_, bf16[48,7168]{1,0:T(8,128)(2,1)S(1)} %collective-permute-done.5.refs_2_, bf16[48,7168]{1,0:T(8,128)(2,1)S(1)} %collective-permute-done.7.refs_3_, ...), custom_call_target="tpu_custom_call" | custom-call | flops 1409286144 | bytes 18350080 | tf_op jit(solution)/shard_map/down_grads/pallas_call | solution.py:336
  154.6 4.0 %collective-permute-start.28 = (bf16[24,7168]{1,0:T(8,128)(2,1)}, bf16[24,7168]{1,0:T(8,128)(2,1)}, u32[]{:S(2)}, u32[]{:S(2)}) collective-permute-start(bf16[24,7168]{1,0:T(8,128)(2,1)} %add_convert_fusion.1), channel_id=1, source_target_pairs={{0,112},{16,0},{32,16},{48,32},{64,48},{80,64},{96,80},{112,96},{1... | collective-permute-start | bytes 1032200 | tf_op jit(solution)/shard_map/ppermute | solution.py:393
  158.6 4.1 %collective-permute-done.31 = bf16[24,7168]{1,0:T(8,128)(2,1)S(1)} collective-permute-done((bf16[24,7168]{1,0:T(8,128)(2,1)S(1)}, bf16[24,7168]{1,0:T(8,128)(2,1)S(1)}, u32[]{:S(2)}, u32[]{:S(2)}) %collective-permute-start.31) | collective-permute-done | bytes 344096 | tf_op jit(solution)/shard_map/ppermute | solution.py:393
  163.6 4.9 %collective-permute-start.34 = (bf16[24,7168]{1,0:T(8,128)(2,1)}, bf16[24,7168]{1,0:T(8,128)(2,1)}, u32[]{:S(2)}, u32[]{:S(2)}) collective-permute-start(bf16[24,7168]{1,0:T(8,128)(2,1)} %add_convert_fusion), channel_id=1, source_target_pairs={{0,120},{1,121},{2,122},{3,123},{4,124},{5,125},{6,126},{7,127},{8... | collective-permute-start | bytes 1032200 | tf_op jit(solution)/shard_map/ppermute | solution.py:393
  168.5 7.1 %collective-permute-done.34.other = bf16[24,7168]{1,0:T(8,128)(2,1)} collective-permute-done((bf16[24,7168]{1,0:T(8,128)(2,1)}, bf16[24,7168]{1,0:T(8,128)(2,1)}, u32[]{:S(2)}, u32[]{:S(2)}) %collective-permute-start.34) | collective-permute-done | bytes 344096 | tf_op jit(solution)/shard_map/ppermute | solution.py:393
  177.8 3.5 %combine.1 = bf16[192,7168]{1,0:T(8,128)(2,1)} custom-call(s32[1]{0:T(128)} %bitcast.rank, s32[1]{0:T(128)} %bitcast.1.plane, s32[8,192]{1,0:T(8,128)S(1)} %collective-permute-done.routes, bf16[80,7168]{1,0:T(8,128)(2,1)S(1)} %collective-permute-done.9.first, bf16[64,7168]{1,0:T(8,128)(2,1)S(1)} %collective-permute-done.10.turned, ...), custom_call_target="tpu_custom_call" | custom-call | flops 132120576 | bytes 8257536 | tf_op jit(solution)/shard_map/combine/pallas_call | solution.py:370
  (102 shorter events, 39.4 us)
Async XLA Ops:
  7.4 40.6 %collective-permute-start.10 = (bf16[64,7168]{1,0:T(8,128)(2,1)S(1)}, bf16[64,7168]{1,0:T(8,128)(2,1)S(1)}, u32[]{:S(2)}, u32[]{:S(2)}) collective-permute-start(bf16[64,7168]{1,0:T(8,128)(2,1)S(1)} %get-tuple-element.62), channel_id=1, source_target_pairs={{0,48},{16,0},{32,16},{48,32},{64,112},{80,64},{96,80},{112,96},{1... | collective-permute-start | bytes 2752520 | tf_op jit(solution)/shard_map/ppermute | solution.py:393
  11.4 18.4 %collective-permute-start = (s32[8,192]{1,0:T(8,128)S(1)}, s32[8,192]{1,0:T(8,128)S(1)}, u32[]{:S(2)}, u32[]{:S(2)}) collective-permute-start(s32[8,192]{1,0:T(8,128)S(1)} %bitcast.18), channel_id=1, source_target_pairs={{0,112},{16,0},{32,16},{48,32},{64,48},{80,64},{96,80},{112,96},{1... | collective-permute-start | bytes 18440 | tf_op jit(solution)/shard_map/ppermute | solution.py:393
  12.8 22.8 %collective-permute-start.5 = (bf16[48,7168]{1,0:T(8,128)(2,1)S(1)}, bf16[48,7168]{1,0:T(8,128)(2,1)S(1)}, u32[]{:S(2)}, u32[]{:S(2)}) collective-permute-start(bf16[48,7168]{1,0:T(8,128)(2,1)S(1)} %get-tuple-element.64.refs_0_), channel_id=1, source_target_pairs={{0,6},{1,7},{2,0},{3,1},{4,2},{5,3},{6,4},{7,5},{8,14},{9,15},{10,... | collective-permute-start | bytes 2064392 | tf_op jit(solution)/shard_map/ppermute | solution.py:393
  13.7 22.0 %collective-permute-start.2 = (bf16[48,7168]{1,0:T(8,128)(2,1)S(1)}, bf16[48,7168]{1,0:T(8,128)(2,1)S(1)}, u32[]{:S(2)}, u32[]{:S(2)}) collective-permute-start(bf16[48,7168]{1,0:T(8,128)(2,1)S(1)} %get-tuple-element.64.refs_0_), channel_id=1, source_target_pairs={{0,2},{1,3},{2,4},{3,5},{4,6},{5,7},{6,0},{7,1},{8,10},{9,11},{10,... | collective-permute-start | bytes 2064392 | tf_op jit(solution)/shard_map/ppermute | solution.py:393
  16.1 19.5 %collective-permute-start.21 = (bf16[48,7168]{1,0:T(8,128)(2,1)S(1)}, bf16[48,7168]{1,0:T(8,128)(2,1)}, u32[]{:S(2)}, u32[]{:S(2)}) collective-permute-start(bf16[48,7168]{1,0:T(8,128)(2,1)S(1)} %get-tuple-element.73), channel_id=1, source_target_pairs={{0,32},{32,0},{64,96},{96,64},{1,33},{33,1},{65,97},{97,65},{2,34}... | collective-permute-start | bytes 2064392 | tf_op jit(solution)/shard_map/ppermute | solution.py:393
  29.8 18.1 %collective-permute-start.3 = (bf16[48,7168]{1,0:T(8,128)(2,1)S(1)}, bf16[48,7168]{1,0:T(8,128)(2,1)S(1)}, u32[]{:S(2)}, u32[]{:S(2)}) collective-permute-start(bf16[48,7168]{1,0:T(8,128)(2,1)S(1)} %get-tuple-element.57), channel_id=1, source_target_pairs={{0,8},{1,9},{2,10},{3,11},{4,12},{5,13},{6,14},{7,15},{8,0},{9,1},... | collective-permute-start | bytes 2064392 | tf_op jit(solution)/shard_map/ppermute | solution.py:393
  47.9 82.0 %collective-permute-start.22 = (bf16[256,7168]{1,0:T(8,128)(2,1)}, bf16[256,7168]{1,0:T(8,128)(2,1)}, u32[]{:S(2)}, u32[]{:S(2)}) collective-permute-start(bf16[256,7168]{1,0:T(8,128)(2,1)} %bitcast.12), channel_id=1, source_target_pairs={{0,112},{16,96},{32,80},{48,64},{64,48},{80,32},{96,16},{112,0},{1... | collective-permute-start | bytes 11010056 | tf_op jit(solution)/shard_map/ppermute | solution.py:393
  50.4 16.6 %collective-permute-start.7 = (bf16[48,7168]{1,0:T(8,128)(2,1)S(1)}, bf16[48,7168]{1,0:T(8,128)(2,1)S(1)}, u32[]{:S(2)}, u32[]{:S(2)}) collective-permute-start(bf16[48,7168]{1,0:T(8,128)(2,1)S(1)} %get-tuple-element.64.refs_0_), channel_id=1, source_target_pairs={{0,4},{1,5},{2,6},{3,7},{4,0},{5,1},{6,2},{7,3},{8,12},{9,13},{10,... | collective-permute-start | bytes 2064392 | tf_op jit(solution)/shard_map/ppermute | solution.py:393
  51.8 15.7 %collective-permute-start.1 = (bf16[48,7168]{1,0:T(8,128)(2,1)S(1)}, bf16[48,7168]{1,0:T(8,128)(2,1)S(1)}, u32[]{:S(2)}, u32[]{:S(2)}) collective-permute-start(bf16[48,7168]{1,0:T(8,128)(2,1)S(1)} %get-tuple-element.64.refs_0_), channel_id=1, source_target_pairs={{0,1},{1,0},{2,3},{3,2},{4,5},{5,4},{6,7},{7,6},{8,9},{9,8},{10,11... | collective-permute-start | bytes 2064392 | tf_op jit(solution)/shard_map/ppermute | solution.py:393
  71.2 19.8 %collective-permute-start.13 = (bf16[48,7168]{1,0:T(8,128)(2,1)S(1)}, bf16[48,7168]{1,0:T(8,128)(2,1)S(1)}, u32[]{:S(2)}, u32[]{:S(2)}) collective-permute-start(bf16[48,7168]{1,0:T(8,128)(2,1)S(1)} %collective-permute-done.3.refs_0_.refs_8_), channel_id=1, source_target_pairs={{0,4},{1,5},{2,6},{3,7},{4,0},{5,1},{6,2},{7,3},{8,12},{9,13},{10,... | collective-permute-start | bytes 2064392 | tf_op jit(solution)/shard_map/ppermute | solution.py:393
  72.5 32.3 %collective-permute-start.12 = (bf16[48,7168]{1,0:T(8,128)(2,1)S(1)}, bf16[48,7168]{1,0:T(8,128)(2,1)S(1)}, u32[]{:S(2)}, u32[]{:S(2)}) collective-permute-start(bf16[48,7168]{1,0:T(8,128)(2,1)S(1)} %collective-permute-done.3.refs_0_.refs_8_), channel_id=1, source_target_pairs={{0,6},{1,7},{2,0},{3,1},{4,2},{5,3},{6,4},{7,5},{8,14},{9,15},{10,... | collective-permute-start | bytes 2064392 | tf_op jit(solution)/shard_map/ppermute | solution.py:393
  72.6 32.3 %collective-permute-start.11 = (bf16[48,7168]{1,0:T(8,128)(2,1)S(1)}, bf16[48,7168]{1,0:T(8,128)(2,1)S(1)}, u32[]{:S(2)}, u32[]{:S(2)}) collective-permute-start(bf16[48,7168]{1,0:T(8,128)(2,1)S(1)} %collective-permute-done.3.refs_0_.refs_8_), channel_id=1, source_target_pairs={{0,2},{1,3},{2,4},{3,5},{4,6},{5,7},{6,0},{7,1},{8,10},{9,11},{10,... | collective-permute-start | bytes 2064392 | tf_op jit(solution)/shard_map/ppermute | solution.py:393
  75.8 29.1 %collective-permute-start.14 = (bf16[48,7168]{1,0:T(8,128)(2,1)S(1)}, bf16[48,7168]{1,0:T(8,128)(2,1)S(1)}, u32[]{:S(2)}, u32[]{:S(2)}) collective-permute-start(bf16[48,7168]{1,0:T(8,128)(2,1)S(1)} %get-tuple-element.73), channel_id=1, source_target_pairs={{16,0},{48,32},{80,64},{112,96},{17,1},{49,33},{81,65},{113,97},{1... | collective-permute-start | bytes 2064392 | tf_op jit(solution)/shard_map/ppermute | solution.py:393
  112.9 25.0 %collective-permute-start.25 = (bf16[24,7168]{1,0:T(8,128)(2,1)}, bf16[24,7168]{1,0:T(8,128)(2,1)S(1)}, u32[]{:S(2)}, u32[]{:S(2)}) collective-permute-start(bf16[24,7168]{1,0:T(8,128)(2,1)} %get-tuple-element.85), channel_id=1, source_target_pairs={{0,6},{1,7},{2,0},{3,1},{4,2},{5,3},{6,4},{7,5},{8,14},{9,15},{10,... | collective-permute-start | bytes 1032200 | tf_op jit(solution)/shard_map/ppermute | solution.py:393
  113.7 24.2 %collective-permute-start.26 = (bf16[24,7168]{1,0:T(8,128)(2,1)}, bf16[24,7168]{1,0:T(8,128)(2,1)}, u32[]{:S(2)}, u32[]{:S(2)}) collective-permute-start(bf16[24,7168]{1,0:T(8,128)(2,1)} %get-tuple-element.91), channel_id=1, source_target_pairs={{0,2},{1,3},{2,4},{3,5},{4,6},{5,7},{6,0},{7,1},{8,10},{9,11},{10,... | collective-permute-start | bytes 1032200 | tf_op jit(solution)/shard_map/ppermute | solution.py:393
  116.1 21.7 %collective-permute-start.27 = (bf16[24,7168]{1,0:T(8,128)(2,1)S(1)}, bf16[24,7168]{1,0:T(8,128)(2,1)}, u32[]{:S(2)}, u32[]{:S(2)}) collective-permute-start(bf16[24,7168]{1,0:T(8,128)(2,1)S(1)} %get-tuple-element.92), channel_id=1, source_target_pairs={{0,4},{1,5},{2,6},{3,7},{4,0},{5,1},{6,2},{7,3},{8,12},{9,13},{10,... | collective-permute-start | bytes 1032200 | tf_op jit(solution)/shard_map/ppermute | solution.py:393
  116.4 24.8 %collective-permute-start.24 = (bf16[48,7168]{1,0:T(8,128)(2,1)}, bf16[48,7168]{1,0:T(8,128)(2,1)S(1)}, u32[]{:S(2)}, u32[]{:S(2)}) collective-permute-start(bf16[48,7168]{1,0:T(8,128)(2,1)} %collective-permute-done.21), channel_id=1, source_target_pairs={{32,112},{96,48},{0,16},{64,80},{33,113},{97,49},{1,17},{65,81},{3... | collective-permute-start | bytes 2064392 | tf_op jit(solution)/shard_map/ppermute | solution.py:393
  130.0 24.6 %collective-permute-start.9 = (bf16[80,7168]{1,0:T(8,128)(2,1)S(1)}, bf16[80,7168]{1,0:T(8,128)(2,1)S(1)}, u32[]{:S(2)}, u32[]{:S(2)}) collective-permute-start(bf16[80,7168]{1,0:T(8,128)(2,1)S(1)} %copy-done.22), channel_id=1, source_target_pairs={{0,112},{16,0},{32,16},{48,32},{64,48},{80,64},{96,80},{112,96},{1... | collective-permute-start | bytes 3440648 | tf_op jit(solution)/shard_map/ppermute | solution.py:393
  140.5 18.1 %collective-permute-start.23 = (bf16[64,7168]{1,0:T(8,128)(2,1)S(1)}, bf16[64,7168]{1,0:T(8,128)(2,1)S(1)}, u32[]{:S(2)}, u32[]{:S(2)}) collective-permute-start(bf16[64,7168]{1,0:T(8,128)(2,1)S(1)} %collective-permute-done.10.turned), channel_id=1, source_target_pairs={{48,112},{112,48},{49,113},{113,49},{50,114},{114,50},{51,115},{11... | collective-permute-start | bytes 2752520 | tf_op jit(solution)/shard_map/ppermute | solution.py:393
  143.9 18.8 %collective-permute-start.31 = (bf16[24,7168]{1,0:T(8,128)(2,1)S(1)}, bf16[24,7168]{1,0:T(8,128)(2,1)S(1)}, u32[]{:S(2)}, u32[]{:S(2)}) collective-permute-start(bf16[24,7168]{1,0:T(8,128)(2,1)S(1)} %get-tuple-element.101), channel_id=1, source_target_pairs={{0,6},{1,7},{2,0},{3,1},{4,2},{5,3},{6,4},{7,5},{8,14},{9,15},{10,... | collective-permute-start | bytes 1032200 | tf_op jit(solution)/shard_map/ppermute | solution.py:393
  144.8 17.9 %collective-permute-start.32 = (bf16[24,7168]{1,0:T(8,128)(2,1)S(1)}, bf16[24,7168]{1,0:T(8,128)(2,1)S(1)}, u32[]{:S(2)}, u32[]{:S(2)}) collective-permute-start(bf16[24,7168]{1,0:T(8,128)(2,1)S(1)} %get-tuple-element.102), channel_id=1, source_target_pairs={{0,2},{1,3},{2,4},{3,5},{4,6},{5,7},{6,0},{7,1},{8,10},{9,11},{10,... | collective-permute-start | bytes 1032200 | tf_op jit(solution)/shard_map/ppermute | solution.py:393
  147.2 15.5 %collective-permute-start.33 = (bf16[24,7168]{1,0:T(8,128)(2,1)S(1)}, bf16[24,7168]{1,0:T(8,128)(2,1)S(1)}, u32[]{:S(2)}, u32[]{:S(2)}) collective-permute-start(bf16[24,7168]{1,0:T(8,128)(2,1)S(1)} %get-tuple-element.103), channel_id=1, source_target_pairs={{0,4},{1,5},{2,6},{3,7},{4,0},{5,1},{6,2},{7,3},{8,12},{9,13},{10,... | collective-permute-start | bytes 1032200 | tf_op jit(solution)/shard_map/ppermute | solution.py:393
  154.6 13.9 %collective-permute-start.28 = (bf16[24,7168]{1,0:T(8,128)(2,1)}, bf16[24,7168]{1,0:T(8,128)(2,1)}, u32[]{:S(2)}, u32[]{:S(2)}) collective-permute-start(bf16[24,7168]{1,0:T(8,128)(2,1)} %add_convert_fusion.1), channel_id=1, source_target_pairs={{0,112},{16,0},{32,16},{48,32},{64,48},{80,64},{96,80},{112,96},{1... | collective-permute-start | bytes 1032200 | tf_op jit(solution)/shard_map/ppermute | solution.py:393
  163.6 12.0 %collective-permute-start.34 = (bf16[24,7168]{1,0:T(8,128)(2,1)}, bf16[24,7168]{1,0:T(8,128)(2,1)}, u32[]{:S(2)}, u32[]{:S(2)}) collective-permute-start(bf16[24,7168]{1,0:T(8,128)(2,1)} %add_convert_fusion), channel_id=1, source_target_pairs={{0,120},{1,121},{2,122},{3,123},{4,124},{5,125},{6,126},{7,127},{8... | collective-permute-start | bytes 1032200 | tf_op jit(solution)/shard_map/ppermute | solution.py:393
  (34 other events, 309.1 us)
